TPU v7x, 32 devices: a whole 2x2x4 slice. The times are simulated.
32 devices in a mesh: lat: 8 (over z, y), lon: 4 (over x, core).
Axes of the slice: x: 2, y: 2, z: 4, core: 2. Of those that a mesh axis runs over, the one named last changes fastest.
Arguments:
- adj_next: float32 [32, 5, 16, 2880], P('lat', None, None, 'lon'), may hold values from -6 to 6
- east_courant: float32 [32, 16, 2880], P('lat', None, 'lon'), may hold values from -0.45 to 0.45
- north_courant: float32 [32, 16, 2880], P('lat', None, 'lon'), may hold values from -0.45 to 0.45
- cutoff: int32 [2, 4], replicated, may hold values from 1 to 351, as said below
Outputs:
- adj_now: float32 [32, 5, 16, 2880], P('lat', None, None, 'lon')
Inputs may be any that keep to these rules, and one draw needn't show every extreme that they name: In each cap the latitude nearest the pole has cutoff 1 and the latitude farthest from it has cutoff 352 - 1.
All inputs are finite; a program needn't handle non-finite values.
Results may differ from a plain program's by a relative error of at most 0.0001.
Values sent between devices are 32-bit elements; how exact they have to be, the bound alone decides.
No kernel may reach another device: no remote copies, remote signals or barrier semaphores. Data moves between devices by JAX's collectives and lax.ppermute only.
A program may use at most 64 MiB of HBM per device.

v0:
```python
import math

import jax
import jax.numpy as jnp
from jax import lax
from jax.sharding import PartitionSpec as P

KF = 352


full_precision = lax.Precision.HIGHEST


def extended(block, sides, width, periodic):
    for axis, dim in sides:
        count = lax.axis_size(axis)
        forward = [(i, i + 1) for i in range(count - 1)]
        if periodic:
            forward.append((count - 1, 0))
        backward = [(target, source) for source, target in forward]
        low = lax.ppermute(
            lax.slice_in_dim(block, block.shape[dim] - width, None, axis=dim), axis, forward
        )
        high = lax.ppermute(lax.slice_in_dim(block, 0, width, axis=dim), axis, backward)
        block = jnp.concatenate([low, block, high], axis=dim)
    return block


def from_partner(block, axis, stride):
    count = lax.axis_size(axis)
    route = []
    for low in range(count):
        high = low | 1 << stride
        if high != low and high < count:
            route += [(low, high), (high, low)]
    return lax.ppermute(block, axis, route)


def mode_table(columns, modes_kept, circle):
    wavenumber = jnp.arange(modes_kept, dtype=jnp.int32)
    product = columns[:, None] * wavenumber[None, :] % circle
    phases = product.astype(jnp.float32) * (2.0 * math.pi / circle)
    return jnp.concatenate([jnp.cos(phases), jnp.sin(phases)], axis=1)


def spectral_weights(latitude, cutoff, modes_kept, circle, total_lat):
    cap_lat = cutoff.shape[1]
    offsets = jnp.arange(cap_lat, dtype=jnp.int32)
    north_hit = latitude[..., None] == offsets
    south_hit = latitude[..., None] == total_lat - cap_lat + offsets
    chosen = jnp.sum(
        jnp.where(north_hit, cutoff[0], 0) + jnp.where(south_hit, cutoff[1], 0), axis=-1
    )
    wavenumber = jnp.arange(2 * modes_kept, dtype=jnp.int32) % modes_kept
    mode_weight = jnp.where(wavenumber == 0, 1.0, 2.0) / circle
    kept_mask = wavenumber <= chosen[..., None]
    return jnp.where(kept_mask, mode_weight, 0.0).astype(jnp.float32)


def body(adj_next, east_courant, north_courant, cutoff):
    lat_count = lax.axis_size("lat")
    lon_count = lax.axis_size("lon")
    lat_index = lax.axis_index("lat")
    lon_index = lax.axis_index("lon")
    lat_rows, tracers, levels, lon_cols = adj_next.shape
    circle = lon_cols * lon_count
    total_lat = lat_rows * lat_count
    modes_kept = KF
    cap_lat = cutoff.shape[1]
    zonal_flux = east_courant[:, None] * adj_next
    meridional = north_courant[:, None] * adj_next
    lon_padded = extended(zonal_flux, (("lon", 3),), 1, True)
    result = adj_next + lon_padded[..., 2:] - lon_padded[..., :-2]
    lat_padded = extended(meridional, (("lat", 0),), 1, False)
    result = result + lat_padded[2:] - lat_padded[:-2]
    edge_row = jnp.where(lat_index == 0, meridional[0], meridional[-1])
    pole_bit = lon_count.bit_length() - 2
    partner = from_partner(edge_row, "lon", pole_bit)
    north_sign = jnp.where(lat_index == 0, 1.0, 0.0).astype(jnp.float32)
    south_sign = jnp.where(lat_index == lat_count - 1, -1.0, 0.0).astype(jnp.float32)
    result = result.at[0].add(north_sign * partner)
    result = result.at[-1].add(south_sign * partner)
    latitude = lat_index * lat_rows + jnp.arange(lat_rows, dtype=jnp.int32)
    in_cap = (latitude < cap_lat) | (latitude >= total_lat - cap_lat)
    local_cols = lon_index * lon_cols + jnp.arange(lon_cols, dtype=jnp.int32)
    local_table = mode_table(local_cols, modes_kept, circle)
    weights = spectral_weights(latitude, cutoff, modes_kept, circle, total_lat)
    partial_sum = jnp.einsum(
        "acvn,nk->acvk",
        result,
        local_table,
        precision=full_precision,
        preferred_element_type=jnp.float32,
    )
    level_share = lax.psum_scatter(partial_sum, "lon", scatter_dimension=2, tiled=True)
    level_share = level_share * weights[:, None, None, :]
    totals = lax.all_gather(level_share, "lon", axis=2, tiled=True)
    rebuilt = jnp.einsum(
        "acvk,nk->acvn",
        totals,
        local_table,
        precision=full_precision,
        preferred_element_type=jnp.float32,
    )
    output = jnp.where(in_cap[:, None, None, None], rebuilt, result)
    return output


def solution(mesh):
    return jax.shard_map(
        body,
        mesh=mesh,
        in_specs=(P("lat", None, None, "lon"), P("lat", None, "lon"), P("lat", None, "lon"), P()),
        out_specs=P("lat", None, None, "lon"),
        check_vma=False,
    )
```

profile of v0, /device:TPU:0, one launch (start us, length us, event | category | flops | bytes accessed | tf_op | source)
XLA Modules:
  0.0 91.3 jit_solution(8699631569269041994)
XLA Ops:
  6.5 0.0 all-reduce.3.cloned.1.call-start
  6.5 1.6 %broadcast_multiply_fusion.1 = (f32[4,5,16,720]{3,2,1,0:T(8,128)S(1)}, f32[4,5,16,720]{3,2,1,0:T(8,128)S(1)}) fusion(f32[4,5,16,720]{3,2,1,0:T(8,128)} %param.8, f32[4,16,720]{2,1,0:T(8,128)} %param.9, f32[4,16,720]{2,1,0:T(8,128)} %param.10), kind=kLoop, calls=%fused_computation.23 | loop fusion | flops 460800 | bytes 3133440 | tf_op jit(solution)/shard_map/mul | solution.py:70
  8.1 0.0 copy-start
  8.1 0.0 copy-start.1
  8.1 1.0 %select_bitcast_fusion = (f32[5,16,720]{2,1,0:T(8,128)}, f32[1,5,16,720]{3,2,1,0:T(8,128)}, f32[1,5,16,720]{3,2,1,0:T(8,128)}) fusion(pred[]{:T(512)S(6)} %eq.19, f32[4,5,16,720]{3,2,1,0:T(8,128)S(1)} %get-tuple-element.35), kind=kLoop, calls=%fused_computation.29 | loop fusion | flops 57600 | bytes 1152001 | tf_op jit(solution)/shard_map/jit(_where)/select_n | solution.py:76
  9.1 1.3 %collective-permute-start.2 = (f32[1,5,16,720]{3,2,1,0:T(8,128)}, f32[1,5,16,720]{3,2,1,0:T(8,128)}, u32[]{:S(2)}, u32[]{:S(2)}) collective-permute-start(f32[1,5,16,720]{3,2,1,0:T(8,128)} %get-tuple-element.31), channel_id=1, source_target_pairs={{4,0},{8,4},{12,8},{16,12},{20,16},{24,20},{28,24},{5,1},{9,5},{13... | collective-permute-start | bytes 691208 | tf_op jit(solution)/shard_map/ppermute | solution.py:24
  10.4 6.2 %collective-permute-start.3 = (f32[1,5,16,720]{3,2,1,0:T(8,128)}, f32[1,5,16,720]{3,2,1,0:T(8,128)}, u32[]{:S(2)}, u32[]{:S(2)}) collective-permute-start(f32[1,5,16,720]{3,2,1,0:T(8,128)} %get-tuple-element.30), channel_id=1, source_target_pairs={{0,4},{4,8},{8,12},{12,16},{16,20},{20,24},{24,28},{1,5},{5,9},{9,... | collective-permute-start | bytes 691208 | tf_op jit(solution)/shard_map/ppermute | solution.py:21
  16.6 0.8 fusion.22
  17.4 0.9 collective-permute-start
  18.3 0.0 collective-permute-start.1
  18.3 1.6 %collective-permute-start.4 = (f32[5,16,720]{2,1,0:T(8,128)}, f32[5,16,720]{2,1,0:T(8,128)S(1)}, u32[]{:S(2)}, u32[]{:S(2)}) collective-permute-start(f32[5,16,720]{2,1,0:T(8,128)} %get-tuple-element.29), channel_id=1, source_target_pairs={{0,2},{2,0},{1,3},{3,1},{4,6},{6,4},{5,7},{7,5},{8,10},{10,8},{9,1... | collective-permute-start | bytes 691208 | tf_op jit(solution)/shard_map/ppermute | solution.py:36
  19.9 0.6 iota_add_fusion.1
  20.5 0.0 copy-done
  20.5 0.0 copy-done.1
  20.5 0.0 copy-start.5
  20.5 0.0 copy-start.9
  20.5 4.5 %fusion.8 = (f32[720,352]{0,1:T(8,128)S(1)}, f32[720,352]{0,1:T(8,128)S(1)}) fusion(s32[720]{0:T(1024)S(1)} %iota_add_fusion), kind=kLoop, calls=%fused_computation.11 | loop fusion | flops 2280960 | bytes 2030400 | tf_op jit(solution)/shard_map/cos | solution.py:43
  25.0 0.0 copy-done.5
  25.0 0.6 slice_bitcast_fusion.1
  25.6 0.5 iota_add_fusion.2
  26.1 0.6 add_select_fusion.1
  26.7 0.5 compare_or_fusion
  27.2 0.0 copy-done.9
  27.2 0.7 dynamic-slice.16
  27.8 0.0 collective-permute-done
  27.8 0.0 collective-permute-done.1
  27.9 0.0 collective-permute-done.2
  27.9 0.0 collective-permute-done.3
  27.9 3.2 %fusion.10 = f32[4,5,16,720]{3,2,1,0:T(8,128)S(1)} fusion(f32[4,5,16,720]{3,2,1,0:T(8,128)} %copy-done, f32[1,5,16,720]{3,2,1,0:T(8,128)} %collective-permute-done.3, f32[1,5,16,720]{3,2,1,0:T(8,128)} %collective-permute-done.2, f32[4,5,16,720]{3,2,1,0:T(8,128)} %copy-done.1, f32[4,5,16,1]{3,2,1,0:T(8,128)} %collective-permute-done.1, ...), kind=kLoop, calls=%fused_computation.14 | loop fusion | flops 1843200 | bytes 4149760 | tf_op jit(solution)/shard_map/sub | solution.py:75
  31.0 0.0 collective-permute-done.4
  31.1 0.1 fusion.16
  31.1 0.1 fusion.15
  31.2 0.0 copy-start.3
  31.2 0.0 copy-start.4
  31.2 0.0 copy-start.6
  31.2 0.0 copy-start.7
  31.3 0.0 copy-start.2
  31.3 3.5 %fusion.1 = f32[4,5,16,704]{3,2,1,0:T(8,128)} fusion(f32[4,5,16,720]{3,2,1,0:T(8,128)S(1)} %fusion.15, f32[720,352]{0,1:T(8,128)S(1)} %get-tuple-element.37, f32[720,352]{0,1:T(8,128)S(1)} %get-tuple-element.36), kind=kOutput, calls=%fused_computation.2 | convolution fusion | flops 1946926080 | bytes 3850240 | tf_op jit(solution)/shard_map/acvn,nk->acvk/dot_general | solution.py:88
  34.8 0.0 all-reduce.3.cloned.1.call-update
  35.5 0.0 copy-done.3
  35.6 0.2 add_reduce_fusion
  35.8 0.1 compare_select_fusion
  35.8 34.7 %all-reduce.3.cloned.1.call-done = f32[4,5,16,704]{3,2,1,0:T(8,128)} async-done(((f32[4,5,16,704]{3,2,1,0:T(8,128)}), f32[4,5,16,704]{3,2,1,0:T(8,128)}) %all-reduce.3.cloned.1.call-update) | async-done | bytes 901136
  70.6 1.1 %dynamic-slice_multiply_fusion = f32[4,5,4,704]{3,2,1,0:T(4,128)S(1)} fusion(f32[4,5,16,704]{3,2,1,0:T(8,128)} %all-reduce.3.cloned.1.call-done, u32[]{:T(128)S(6)} %multiply.2, f32[4,704]{1,0:T(4,128)S(1)} %compare_select_fusion), kind=kLoop, calls=%fused_computation.28 | loop fusion | flops 56320 | bytes 461828 | tf_op jit(solution)/shard_map/mul | solution.py:96
  71.6 0.1 copy.7
  71.7 9.2 %all_gather.3 = f32[4,5,16,704]{3,0,1,2:T(4,128)S(1)} all-gather(f32[4,5,4,704]{3,0,1,2:T(4,128)S(1)} %copy.7), channel_id=1, replica_groups=mesh['lat'=8,'lon'=4] {'lon'}, dimensions={2}, use_global_device_ids=true | all-gather | bytes 1126400 | tf_op jit(solution)/shard_map/all_gather | solution.py:97
  80.9 0.0 copy-done.8
  80.9 3.6 %fusion.2 = f32[4,5,16,720]{3,2,1,0:T(8,128)} fusion(f32[4,5,16,720]{3,2,1,0:T(8,128)S(1)} %fusion.15, f32[720,352]{0,1:T(8,128)S(1)} %get-tuple-element.37, f32[720,352]{0,1:T(8,128)S(1)} %get-tuple-element.36, f32[4,5,16,704]{3,0,1,2:T(4,128)S(1)} %all_gather.3, pred[4]{0:T(512)(128)(4,1)S(1)} %copy-done.8), kind=kOutput, calls=%fused_computation.4 | convolution fusion | flops 1947156480 | bytes 4771844 | tf_op jit(solution)/shard_map/acvk,nk->acvn/dot_general | solution.py:98
  (7 shorter events, 0.0 us)
Async XLA Ops:
  6.5 64.0 %all-reduce.3.cloned.1.call-start = ((), (), s32[]{:S(2)}) async-start(), calls=%async_computation | async-start | bytes 1966080
  8.1 12.4 %copy-start = (f32[4,5,16,720]{3,2,1,0:T(8,128)}, f32[4,5,16,720]{3,2,1,0:T(8,128)S(1)}, u32[]{:S(2)}) copy-start(f32[4,5,16,720]{3,2,1,0:T(8,128)S(1)} %get-tuple-element.35) | copy-start | bytes 2764804
  8.1 12.4 %copy-start.1 = (f32[4,5,16,720]{3,2,1,0:T(8,128)}, f32[4,5,16,720]{3,2,1,0:T(8,128)S(1)}, u32[]{:S(2)}) copy-start(f32[4,5,16,720]{3,2,1,0:T(8,128)S(1)} %get-tuple-element.34) | copy-start | bytes 2764804
  9.1 18.7 %collective-permute-start.2 = (f32[1,5,16,720]{3,2,1,0:T(8,128)}, f32[1,5,16,720]{3,2,1,0:T(8,128)}, u32[]{:S(2)}, u32[]{:S(2)}) collective-permute-start(f32[1,5,16,720]{3,2,1,0:T(8,128)} %get-tuple-element.31), channel_id=1, source_target_pairs={{4,0},{8,4},{12,8},{16,12},{20,16},{24,20},{28,24},{5,1},{9,5},{13... | collective-permute-start | bytes 691208 | tf_op jit(solution)/shard_map/ppermute | solution.py:24
  10.4 17.5 %collective-permute-start.3 = (f32[1,5,16,720]{3,2,1,0:T(8,128)}, f32[1,5,16,720]{3,2,1,0:T(8,128)}, u32[]{:S(2)}, u32[]{:S(2)}) collective-permute-start(f32[1,5,16,720]{3,2,1,0:T(8,128)} %get-tuple-element.30), channel_id=1, source_target_pairs={{0,4},{4,8},{8,12},{12,16},{16,20},{20,24},{24,28},{1,5},{5,9},{9,... | collective-permute-start | bytes 691208 | tf_op jit(solution)/shard_map/ppermute | solution.py:21
  17.4 10.5 %collective-permute-start = (f32[4,5,16,1]{3,2,1,0:T(8,128)}, f32[4,5,16,1]{3,2,1,0:T(8,128)S(1)}, u32[]{:S(2)}, u32[]{:S(2)}) collective-permute-start(f32[4,5,16,1]{3,2,1,0:T(8,128)} %get-tuple-element.32), channel_id=1, source_target_pairs={{1,0},{2,1},{3,2},{0,3},{5,4},{6,5},{7,6},{4,7},{9,8},{10,9},{11,1... | collective-permute-start | bytes 3848 | tf_op jit(solution)/shard_map/ppermute | solution.py:24
  18.3 9.6 %collective-permute-start.1 = (f32[4,5,16,1]{3,2,1,0:T(8,128)}, f32[4,5,16,1]{3,2,1,0:T(8,128)}, u32[]{:S(2)}, u32[]{:S(2)}) collective-permute-start(f32[4,5,16,1]{3,2,1,0:T(8,128)} %get-tuple-element.33), channel_id=1, source_target_pairs={{0,1},{1,2},{2,3},{3,0},{4,5},{5,6},{6,7},{7,4},{8,9},{9,10},{10,1... | collective-permute-start | bytes 3848 | tf_op jit(solution)/shard_map/ppermute | solution.py:21
  18.3 12.8 %collective-permute-start.4 = (f32[5,16,720]{2,1,0:T(8,128)}, f32[5,16,720]{2,1,0:T(8,128)S(1)}, u32[]{:S(2)}, u32[]{:S(2)}) collective-permute-start(f32[5,16,720]{2,1,0:T(8,128)} %get-tuple-element.29), channel_id=1, source_target_pairs={{0,2},{2,0},{1,3},{3,1},{4,6},{6,4},{5,7},{7,5},{8,10},{10,8},{9,1... | collective-permute-start | bytes 691208 | tf_op jit(solution)/shard_map/ppermute | solution.py:36
  20.5 4.5 %copy-start.5 = (s32[2,4]{1,0:T(2,128)S(1)}, s32[2,4]{1,0:T(2,128)}, u32[]{:S(2)}) copy-start(s32[2,4]{1,0:T(2,128)} %param.11) | copy-start | bytes 100
  20.5 6.7 %copy-start.9 = (u32[32]{0:T(128)S(1)}, u32[32]{0:T(128)}, u32[]{:S(2)}) copy-start(u32[32]{0:T(128)} %constant.115) | copy-start | bytes 388
  31.2 4.3 %copy-start.3 = (s32[4]{0:T(128)S(1)}, s32[4]{0:T(128)}, u32[]{:S(2)}) copy-start(s32[4]{0:T(128)} %get-tuple-element.38) | copy-start | bytes 52
  31.2 4.3 %copy-start.4 = (s32[4]{0:T(128)S(1)}, s32[4]{0:T(128)}, u32[]{:S(2)}) copy-start(s32[4]{0:T(128)} %get-tuple-element.39) | copy-start | bytes 52
  31.2 4.3 %copy-start.6 = (s32[4]{0:T(128)S(1)}, s32[4]{0:T(128)}, u32[]{:S(2)}) copy-start(s32[4]{0:T(128)} %iota_add_fusion.1) | copy-start | bytes 52
  31.2 4.3 %copy-start.7 = (s32[4]{0:T(128)S(1)}, s32[4]{0:T(128)}, u32[]{:S(2)}) copy-start(s32[4]{0:T(128)} %iota_add_fusion.2) | copy-start | bytes 52
  31.3 4.5 %copy-start.2 = (s32[704]{0:T(1024)S(1)}, s32[704]{0:T(1024)}, u32[]{:S(2)}) copy-start(s32[704]{0:T(1024)} %add_select_fusion.1) | copy-start | bytes 8452
  35.8 45.0 %copy-start.8 = (pred[4]{0:T(512)(128)(4,1)S(1)}, pred[4]{0:T(512)(128)(4,1)}, u32[]{:S(2)}) copy-start(pred[4]{0:T(512)(128)(4,1)} %compare_or_fusion) | copy-start | bytes 16
Sparse Core Ops, SparseCore 0:
  35.0 35.5 all-reduce.2
where the time goes:
time: 91.6 us; the launch traced here: 91.3 us
  waiting for transfers between devices  34.8 us (38%)
  between operations  14.3 us (16%)
  other arithmetic  13.9 us (15%)
  starting transfers between devices  9.99 us (11%)
  blocking collectives  9.16 us (10%)
  matrix products  7.15 us (8%)
  local copies, waits for them, and re-layouts  2.14 us (2%)
    unnamed x2, waiting for transfers between devices  34.7 us
    all_gather x1, blocking collectives, body(): totals = lax.all_gather(level_share, 'lon', axis=2, tiled=True)  9.16 us
    ppermute x2, starting transfers between devices, extended(): lax.ppermute(lax.slice_in_dim(block, block.shape[dim] - width, None, axis...  6.21 us
    cos x1, other arithmetic, mode_table(): return jnp.concatenate([jnp.cos(phases), jnp.sin(phases)], axis=1)  4.46 us
    dot_general x1, matrix products, body(): jnp.einsum('acvk,nk->acvn', totals, local_table, precision=full_precision...  3.61 us
    dot_general x1, matrix products, body(): jnp.einsum('acvn,nk->acvk', result, local_table, precision=full_precision...  3.54 us
    sub x1, other arithmetic, body(): result = result + lat_padded[2:] - lat_padded[:-2]  3.17 us
    ppermute x2, starting transfers between devices, extended(): lax.ppermute(lax.slice_in_dim(block, 0, width, axis=dim), axis, backward)  2.14 us
  transfers between devices with their start and end apart: 6, of which 1 were waited for; matrix products, arithmetic and copies ran while one was open for 13% of the time, Pallas kernels for 0%

commit v1 on v0

--- a/solution.py
+++ b/solution.py
@@ -1,11 +1,315 @@
+import functools
 import math
 
 import jax
 import jax.numpy as jnp
+import ml_dtypes
+import numpy as np
 from jax import lax
+from jax.experimental import pallas as pl
+from jax.experimental.pallas import tpu as pltpu
 from jax.sharding import PartitionSpec as P
 
 KF = 352
+LANE = 128
+VMEM = pltpu.VMEM
+
+
+def ceil_to(value, unit):
+    return -(-value // unit) * unit
+
+
+def split16(table):
+    high = table.astype(ml_dtypes.bfloat16)
+    low = (table - high.astype(np.float64)).astype(ml_dtypes.bfloat16)
+    return np.stack([high, low])
+
+
+def tables(cols, circle, lon_count):
+    wide = ceil_to(cols + 2, LANE)
+    half = ceil_to(KF + 2, LANE)
+    place = np.zeros(wide, np.int64)
+    place[: cols + 1] = np.arange(cols + 1)
+    place[-1] = -1
+    live = np.zeros(wide)
+    live[: cols + 1] = 1
+    live[-1] = 1
+    mode = np.arange(KF)
+    phase = 2 * np.pi * ((place[:, None] * mode[None]) % circle) / circle
+    forward = np.zeros((wide, 2 * half))
+    forward[:, :KF] = np.cos(phase) * live[:, None]
+    forward[:, half : half + KF] = np.sin(phase) * live[:, None]
+    backward = forward.T.copy()
+    backward[:, cols:] = 0
+    turn = np.zeros((lon_count, 2, half), np.float32)
+    angle = 2 * np.pi * ((np.arange(lon_count)[:, None] * mode[None]) % lon_count) / lon_count
+    turn[:, 0, :KF] = np.cos(angle)
+    turn[:, 1, :KF] = np.sin(angle)
+    pole = np.zeros((lon_count, 4, wide), np.float32)
+    for index in range(lon_count):
+        first = 2 * np.pi * (place + index * cols) / circle
+        pole[index, 0] = live
+        pole[index, 1] = np.cos(first) * live
+        pole[index, 2] = np.sin(first) * live
+    return split16(forward), split16(backward), turn, pole
+
+
+def dot3(block, table_ref):
+    high = block.astype(jnp.bfloat16)
+    low = (block - high.astype(jnp.float32)).astype(jnp.bfloat16)
+    total = jnp.dot(high, table_ref[0], preferred_element_type=jnp.float32)
+    total += jnp.dot(high, table_ref[1], preferred_element_type=jnp.float32)
+    return total + jnp.dot(low, table_ref[0], preferred_element_type=jnp.float32)
+
+
+def roles(lat_count):
+    lat = lax.axis_index("lat")
+    last = lat_count - 1
+    north, south = lat == 0, lat == last
+    polar = jnp.logical_or(north, south)
+    beside = jnp.logical_or(lat == 1, lat == last - 1)
+    even = lax.rem(lat, 2) == 0
+    return south, polar, beside, even
+
+
+def local_kernel(lat_count, adj, east, north, fwd, turn, pole, base, edge_a, edge_b, sides, keep, send, flux, wide_x):
+    rows, tracers, levels, cols = adj.shape
+    wide = flux.shape[-1]
+    south, polar, beside, even = roles(lat_count)
+    lon = lax.axis_index("lon")
+    core = lax.rem(lon, 2)
+    half_lev = levels // 2
+    half = fwd.shape[-1] // 2
+    row_a = jnp.where(even, rows - 1, 0)
+    row_b = rows - 1 - row_a
+    edge_a[...] = north[row_a][None] * adj[row_a]
+    edge_b[...] = north[row_b][None] * adj[row_b]
+
+    pad = jnp.zeros((levels, wide - cols), jnp.float32)
+
+    def transported(r, t):
+        out = adj[r, t]
+        if r + 1 < rows:
+            out = out + north[r + 1] * adj[r + 1, t]
+        if r > 0:
+            out = out - north[r - 1] * adj[r - 1, t]
+        return out
+
+    def spread(r, t):
+        flux[:, :cols] = east[r] * adj[r, t]
+        f = flux[...]
+        return pltpu.roll(f, wide - 1, 1) - pltpu.roll(f, 1, 1), f
+
+    flux[:, cols:] = pad
+
+    def turned(p):
+        a, b = turn[lon, 0:1], turn[lon, 1:2]
+        c, s = p[:, :half], p[:, half:]
+        return c * a - s * b, s * a + c * b
+
+    def put(slot, p):
+        c, s = turned(p)
+        n = c.shape[0] // 2
+        keep[slot, :, :half] = c[:n]
+        keep[slot, :, half:] = s[:n]
+        send[slot, :, :half] = c[n:]
+        send[slot, :, half:] = s[n:]
+
+    @pl.when(jnp.logical_not(polar))
+    def _():
+        ends = jnp.zeros((8, wide), jnp.float32)
+        row = lax.broadcasted_iota(jnp.int32, (8, wide), 0)
+        lane = lax.broadcasted_iota(jnp.int32, (8, wide), 1)
+        pick = jnp.where((row == 0) & (lane == 0) | (row == 1) & (lane == cols - 1), 1.0, 0.0).astype(jnp.float32)
+        for r in range(rows):
+            for t in range(tracers):
+                move, f = spread(r, t)
+                base[r, t] = transported(r, t) + move[:, :cols]
+                wide_x[r, 0, t] = f[:half_lev]
+                wide_x[r, 1, t] = f[half_lev:]
+        whole = wide_x[...].reshape(rows * tracers * levels, wide)
+        sides[...] = lax.dot_general(
+            pick, whole, (((1,), (1,)), ((), ())), precision=lax.Precision.HIGHEST, preferred_element_type=jnp.float32
+        )
+
+    @pl.when(beside)
+    def _():
+        sign = jnp.where(even, -1.0, 1.0).astype(jnp.float32)
+        wide_x[2] = jnp.zeros(wide_x.shape[1:], jnp.float32)
+        for t in range(tracers):
+            m = edge_a[t] * sign
+            wide_x[2, core, t, :, :cols] = m[:half_lev]
+            wide_x[2, 1 - core, t, :, :cols] = m[half_lev:]
+        put(2, dot3(wide_x[2].reshape(tracers * levels, wide), fwd))
+
+    @pl.when(polar)
+    def _():
+        for r in range(rows):
+            near = jnp.where(south, rows - 1 - r, r)
+            slot = lax.rem(near + rows - 1, rows)
+            for t in range(tracers):
+                move, _ = spread(r, t)
+                for h in (0, 1):
+                    part = slice(h * half_lev, (h + 1) * half_lev)
+                    where = jnp.where(core == 0, h, 1 - h)
+                    wide_x[slot, where, t] = move[part]
+                    wide_x[slot, where, t, :, :cols] += transported(r, t)[part]
+        for slot in range(3):
+            put(slot, dot3(wide_x[slot].reshape(tracers * levels, wide), fwd))
+        sign = jnp.where(south, -1.0, 1.0).astype(jnp.float32)
+        row_p = jnp.where(south, rows - 1, 0)
+        lane = lax.broadcasted_iota(jnp.int32, (half_lev, LANE), 1)
+        one, cos, sin = (pole[lon, k : k + 1] for k in range(3))
+        for t in range(tracers):
+            m = north[row_p] * adj[row_p, t] * sign
+            for h, target in ((0, keep), (1, send)):
+                where = jnp.where(core == 0, h, 1 - h)
+                u = wide_x[3, h, t]
+                flux[:half_lev, :cols] = jnp.where(where == 0, m[:half_lev], m[half_lev:])
+                v = flux[:half_lev]
+                c0 = jnp.sum((u + v) * one, axis=1, keepdims=True)
+                c1 = jnp.sum((u - v) * cos, axis=1, keepdims=True)
+                s1 = jnp.sum((u - v) * sin, axis=1, keepdims=True)
+                at = KF % LANE
+                lanes = slice(half - LANE, half)
+                spot = slice(t * half_lev, (t + 1) * half_lev)
+                target[2, spot, lanes] = jnp.where(
+                    lane == at, c0, jnp.where(lane == at + 1, c1, jnp.where(lane == at + 2, s1, target[2, spot, lanes]))
+                )
+
+
+def last_kernel(
+    lat_count, circle, cutoff, base, recv_a, recv_b, left, right, mine, other, mine_r, other_r, beside_t, beside_o,
+    bwd, turn, pole, out, coef,
+):
+    rows, tracers, levels, cols = out.shape
+    half_lev = levels // 2
+    half = bwd.shape[1] // 2
+    south, polar, beside, even = roles(lat_count)
+    lon = lax.axis_index("lon")
+    core = lax.rem(lon, 2)
+
+    @pl.when(jnp.logical_not(polar))
+    def _():
+        row = lax.broadcasted_iota(jnp.int32, (8, LANE), 0)
+        lane = lax.broadcasted_iota(jnp.int32, (8, LANE), 1)
+        at = (cols - 1) % LANE
+        low = jnp.where((row == 1) & (lane == 0), 1.0, 0.0).astype(jnp.float32)
+        high = jnp.where((row == 0) & (lane == at), 1.0, 0.0).astype(jnp.float32)
+        dims = (((0,), (0,)), ((), ()))
+        exact = lax.Precision.HIGHEST
+        first = lax.dot_general(left[...], low, dims, precision=exact, preferred_element_type=jnp.float32)
+        end = lax.dot_general(right[...], high, dims, precision=exact, preferred_element_type=jnp.float32)
+        start = cols // LANE * LANE
+        shape = (rows, 2, tracers, half_lev, LANE)
+        first, end = first.reshape(shape), end.reshape(shape)
+        out[...] = base[...]
+        for r in range(rows):
+            for h in (0, 1):
+                part = slice(h * half_lev, (h + 1) * half_lev)
+                out[r, :, part, :LANE] -= first[r, h]
+                out[r, :, part, start:] += end[r, h][..., : cols - start]
+        row_a = jnp.where(even, rows - 1, 0)
+        row_b = rows - 1 - row_a
+        sign = jnp.where(even, 1.0, -1.0).astype(jnp.float32)
+        out[row_a] += recv_a[...] * sign
+        out[row_b] -= recv_b[...] * sign
+
+    @pl.when(polar)
+    def _():
+        for slot in range(3):
+            own, far = mine[slot] + mine_r[slot], other[slot] + other_r[slot]
+            if slot == 2:
+                own, far = own + beside_t[...], far + beside_o[...]
+            coef[slot, core] = own
+            coef[slot, 1 - core] = far
+        wave = lax.broadcasted_iota(jnp.int32, (1, half), 1)
+        a, b = turn[lon, 0:1], turn[lon, 1:2]
+        for slot in range(3):
+            near = slot + 1
+            row = jnp.where(south, rows - 1 - near, near)
+            kept = jnp.where(south, cutoff[1, row], cutoff[0, row])
+            weight = jnp.where(wave <= kept, jnp.where(wave == 0, 1.0 / circle, 2.0 / circle), 0.0).astype(jnp.float32)
+            block = coef[slot].reshape(tracers * levels, 2 * half)
+            c, s = block[:, :half], block[:, half:]
+            wa, wb = weight * a, weight * b
+            back = jnp.concatenate([c * wa + s * wb, s * wa - c * wb], axis=1)
+            y = dot3(back, bwd).reshape(2, tracers, half_lev, -1)
+            for h in (0, 1):
+                out[row, :, h * half_lev : (h + 1) * half_lev, :] = y[h][..., :cols]
+        row = jnp.where(south, rows - 1, 0)
+        cos, sin = pole[lon, 1:2], pole[lon, 2:3]
+        for t in range(tracers):
+            for h in (0, 1):
+                p = coef[2, h, t * half_lev : (t + 1) * half_lev, half - LANE : half]
+                at = KF % LANE
+                c0, c1, s1 = p[:, at : at + 1], p[:, at + 1 : at + 2], p[:, at + 2 : at + 3]
+                y = (1.0 / circle) * c0 + (2.0 / circle) * (c1 * cos + s1 * sin)
+                out[row, t, h * half_lev : (h + 1) * half_lev, :] = y[:, :cols]
+
+
+def routes(lat_count, lon_count, lats, step):
+    return [(a * lon_count + i, a * lon_count + (i ^ step)) for a in lats for i in range(lon_count)]
+
+
+def fast_body(adj, east, north, cutoff):
+    lat_count, lon_count = lax.axis_size("lat"), lax.axis_size("lon")
+    rows, tracers, levels, cols = adj.shape
+    circle = cols * lon_count
+    fwd, bwd, turn, pole = tables(cols, circle, lon_count)
+    wide, width = fwd.shape[1:]
+    both = ("lat", "lon")
+    last = lat_count - 1
+    f32 = jnp.float32
+    spec = pl.BlockSpec(memory_space=VMEM)
+    shape = jax.ShapeDtypeStruct
+    share = (3, tracers * levels // 2, width)
+    n_rows = rows * tracers * levels
+    base, edge_a, edge_b, sides, keep, send = pl.pallas_call(
+        functools.partial(local_kernel, lat_count),
+        out_shape=[
+            shape(adj.shape, f32),
+            shape(adj.shape[1:], f32),
+            shape(adj.shape[1:], f32),
+            shape((8, n_rows), f32),
+            shape(share, f32),
+            shape(share, f32),
+        ],
+        in_specs=[spec] * 6,
+        out_specs=[spec] * 6,
+        scratch_shapes=[VMEM((levels, wide), f32), VMEM((rows, 2, tracers, levels // 2, wide), f32)],
+    )(adj, east, north, fwd, turn, pole)
+
+    def move(x, lats, step):
+        return lax.ppermute(x, both, routes(lat_count, lon_count, lats, step))
+
+    caps = (0, last)
+    nexts = (1, last - 1)
+    got = move(send, caps + nexts, 1)
+    total = keep + got
+    third = total[2]
+    third_r = move(third, nexts, 2)
+    third_sum = third + third_r
+    mine_r = move(total, caps, 2)
+    swap_a = [(i ^ 1) for i in range(lat_count)]
+    recv_a = lax.ppermute(edge_a, "lat", list(enumerate(swap_a)))
+    recv_b = lax.ppermute(edge_b, "lat", [(i, j) for k in range(1, last, 2) for i, j in ((k, k + 1), (k + 1, k))])
+    inner = range(1, last)
+    ring = [(a * lon_count + i, a * lon_count + (i + 1) % lon_count) for a in inner for i in range(lon_count)]
+    left = lax.ppermute(sides, both, ring)
+    right = lax.ppermute(sides, both, [(j, i) for i, j in ring])
+    other = move(total, caps, 1)
+    to_cap = [(a * lon_count + i, b * lon_count + i) for a, b in ((1, 0), (last - 1, last)) for i in range(lon_count)]
+    beside_t = lax.ppermute(third_sum, both, to_cap)
+    other_r = move(mine_r, caps, 1)
+    beside_o = move(beside_t, caps, 1)
+    return pl.pallas_call(
+        functools.partial(last_kernel, lat_count, circle),
+        out_shape=shape(adj.shape, f32),
+        in_specs=[pl.BlockSpec(memory_space=pltpu.SMEM)] + [spec] * 14,
+        out_specs=spec,
+        scratch_shapes=[VMEM((3, 2, tracers * levels // 2, width), f32)],
+    )(cutoff, base, recv_a, recv_b, left, right, total, other, mine_r, other_r, beside_t, beside_o, bwd, turn, pole)
 
 
 full_precision = lax.Precision.HIGHEST
@@ -57,7 +361,7 @@
     return jnp.where(kept_mask, mode_weight, 0.0).astype(jnp.float32)
 
 
-def body(adj_next, east_courant, north_courant, cutoff):
+def general_body(adj_next, east_courant, north_courant, cutoff):
     lat_count = lax.axis_size("lat")
     lon_count = lax.axis_size("lon")
     lat_index = lax.axis_index("lat")
@@ -106,6 +410,14 @@
     return output
 
 
+def body(adj, east, north, cutoff):
+    lat_count, lon_count = lax.axis_size("lat"), lax.axis_size("lon")
+    one_band = cutoff.shape[1] == adj.shape[0] == 4
+    if one_band and lon_count == 4 and lat_count % 2 == 0 and lat_count >= 4 and adj.shape[2] % 16 == 0:
+        return fast_body(adj, east, north, cutoff)
+    return general_body(adj, east, north, cutoff)
+
+
 def solution(mesh):
     return jax.shard_map(
         body,

time: 91.6 us -> 54.3 us (0.59)
  waiting for transfers between devices: 34.8 us -> 16.4 us
  between operations: 14.3 us -> 0.23 us
  starting transfers between devices: 9.99 us -> 23.7 us
  other arithmetic: 13.9 us -> 1.06 us
  Pallas kernels: 0 us -> 11.5 us
  blocking collectives: 9.16 us -> 0 us
  matrix products: 7.15 us -> 0 us
  local copies, waits for them, and re-layouts: 2.14 us -> 0.99 us
    unnamed x2 -> x0, waiting for transfers between devices: 34.7 us -> none
    ppermute x5 -> x11, waiting for transfers between devices: 0.01 us -> 16.4 us  [the longest x1 8.63 us: fast_body(): recv_a = lax.ppermute(edge_a, 'lat', list(enumerate(swap_a)))]
    ppermute x5 -> x11, starting transfers between devices: 9.99 us -> 23.7 us  [the longest x6 13.7 us: move(): return lax.ppermute(x, both, routes(lat_count, lon_count, lats, step))]
    pallas_call x0 -> x2, Pallas kernels: none -> 11.5 us  [the longest x1 5.94 us: fast_body(): pl.pallas_call(functools.partial(local_kernel, lat_count), out_shape=[sha...]
    all_gather x1 -> x0, blocking collectives: 9.16 us -> none  [body(): totals = lax.all_gather(level_share, 'lon', axis=2, tiled=True)]
    dot_general x2 -> x0, matrix products: 7.15 us -> none  [the longest x1 3.61 us: body(): jnp.einsum('acvk,nk->acvn', totals, local_table, precision=full_precision...]
    cos x1 -> x0, other arithmetic: 4.46 us -> none  [mode_table(): return jnp.concatenate([jnp.cos(phases), jnp.sin(phases)], axis=1)]
    sub x1 -> x0, other arithmetic: 3.17 us -> none  [body(): result = result + lat_padded[2:] - lat_padded[:-2]]
  transfers between devices with their start and end apart: 6 -> 11, of which waited for: 1 -> 3; matrix products, arithmetic and copies ran while one was open for 13% -> 0% of each run, Pallas kernels for 0% -> 0%
where the time goes in v1:
time: 54.3 us; the launch traced here: 53.9 us
  starting transfers between devices  23.7 us (44%)
  waiting for transfers between devices  16.4 us (30%)
  Pallas kernels  11.5 us (21%)
  other arithmetic  1.06 us (2%)
  local copies, waits for them, and re-layouts  0.99 us (2%)
    ppermute x6, starting transfers between devices, move(): return lax.ppermute(x, both, routes(lat_count, lon_count, lats, step))  13.7 us
    ppermute x1, waiting for transfers between devices, fast_body(): recv_a = lax.ppermute(edge_a, 'lat', list(enumerate(swap_a)))  8.63 us
    ppermute x6, waiting for transfers between devices, move(): return lax.ppermute(x, both, routes(lat_count, lon_count, lats, step))  7.76 us
    ppermute x1, starting transfers between devices, fast_body(): recv_a = lax.ppermute(edge_a, 'lat', list(enumerate(swap_a)))  6.77 us
    pallas_call x1, Pallas kernels, fast_body(): pl.pallas_call(functools.partial(local_kernel, lat_count), out_shape=[sha...  5.94 us
    pallas_call x1, Pallas kernels, fast_body(): pl.pallas_call(functools.partial(last_kernel, lat_count, circle), out_sha...  5.58 us
    ppermute x1, starting transfers between devices, fast_body(): beside_t = lax.ppermute(third_sum, both, to_cap)  1.29 us
  transfers between devices with their start and end apart: 11, of which 3 were waited for; matrix products, arithmetic and copies ran while one was open for 0% of the time, Pallas kernels for 0%

profile of v1, /device:TPU:0, one launch (start us, length us, event | category | flops | bytes accessed | tf_op | source)
XLA Modules:
  0.0 53.9 jit_solution(12512072875387070025)
XLA Ops:
  0.0 5.9 %shard_map.82 = (f32[4,5,16,720]{3,2,1,0:T(8,128)}, f32[5,16,720]{2,1,0:T(8,128)}, f32[5,16,720]{2,1,0:T(8,128)}, f32[8,320]{1,0:T(8,128)}, f32[3,40,768]{2,1,0:T(8,128)}, /*index=5*/f32[3,40,768]{2,1,0:T(8,128)}) custom-call(f32[4,5,16,720]{3,2,1,0:T(8,128)} %adj.1, f32[4,16,720]{2,1,0:T(8,128)} %east.1, f32[4,16,720]{2,1,0:T(8,128)} %north.1, ...), custom_call_target="tpu_custom_call" | custom-call | tf_op jit(solution)/shard_map/pallas_call | solution.py:268
  5.9 2.3 %collective-permute-start.4 = (f32[3,40,768]{2,1,0:T(8,128)}, f32[3,40,768]{2,1,0:T(8,128)S(1)}, u32[]{:S(2)}, u32[]{:S(2)}) collective-permute-start(f32[3,40,768]{2,1,0:T(8,128)} %get-tuple-element.16), channel_id=1, source_target_pairs={{0,1},{1,0},{2,3},{3,2},{28,29},{29,28},{30,31},{31,30},{4,5},{5,4... | collective-permute-start | bytes 1105928 | tf_op jit(solution)/shard_map/ppermute | solution.py:284
  8.3 1.5 %collective-permute-done.4 = f32[3,40,768]{2,1,0:T(8,128)S(1)} collective-permute-done((f32[3,40,768]{2,1,0:T(8,128)}, f32[3,40,768]{2,1,0:T(8,128)S(1)}, u32[]{:S(2)}, u32[]{:S(2)}) %collective-permute-start.4) | collective-permute-done | bytes 368672 | tf_op jit(solution)/shard_map/ppermute | solution.py:284
  9.8 1.0 %add.6.mine = f32[3,40,768]{2,1,0:T(8,128)S(1)} add(f32[3,40,768]{2,1,0:T(8,128)} %get-tuple-element.15, f32[3,40,768]{2,1,0:T(8,128)S(1)} %collective-permute-done.4) | non-fusion elementwise | flops 92160 | bytes 1105920 | tf_op jit(solution)/shard_map/add | solution.py:289
  10.8 0.0 copy-start
  10.9 4.8 %collective-permute-start.6 = (f32[3,40,768]{2,1,0:T(8,128)S(1)}, f32[3,40,768]{2,1,0:T(8,128)S(1)}, u32[]{:S(2)}, u32[]{:S(2)}) collective-permute-start(f32[3,40,768]{2,1,0:T(8,128)S(1)} %add.6.mine), channel_id=1, source_target_pairs={{0,2},{1,3},{2,0},{3,1},{28,30},{29,31},{30,28},{31,29}} | collective-permute-start | bytes 1105928 | tf_op jit(solution)/shard_map/ppermute | solution.py:284
  15.6 0.7 %collective-permute-start.8 = (f32[40,768]{1,0:T(8,128)S(1)}, f32[40,768]{1,0:T(8,128)S(1)}, u32[]{:S(2)}, u32[]{:S(2)}) collective-permute-start(f32[40,768]{1,0:T(8,128)S(1)} %slice_bitcast_fusion), channel_id=1, source_target_pairs={{4,6},{5,7},{6,4},{7,5},{24,26},{25,27},{26,24},{27,25}} | collective-permute-start | bytes 368648 | tf_op jit(solution)/shard_map/ppermute | solution.py:284
  16.3 1.9 %collective-permute-start.5 = (f32[3,40,768]{2,1,0:T(8,128)S(1)}, f32[3,40,768]{2,1,0:T(8,128)S(1)}, u32[]{:S(2)}, u32[]{:S(2)}) collective-permute-start(f32[3,40,768]{2,1,0:T(8,128)S(1)} %add.6.mine), channel_id=1, source_target_pairs={{0,1},{1,0},{2,3},{3,2},{28,29},{29,28},{30,31},{31,30}} | collective-permute-start | bytes 1105928 | tf_op jit(solution)/shard_map/ppermute | solution.py:284
  18.3 6.3 %collective-permute-done.6.mine_r = f32[3,40,768]{2,1,0:T(8,128)S(1)} collective-permute-done((f32[3,40,768]{2,1,0:T(8,128)S(1)}, f32[3,40,768]{2,1,0:T(8,128)S(1)}, u32[]{:S(2)}, u32[]{:S(2)}) %collective-permute-start.6) | collective-permute-done | bytes 368672 | tf_op jit(solution)/shard_map/ppermute | solution.py:284
  24.5 0.0 copy-start.1
  24.5 1.9 %collective-permute-start.7 = (f32[3,40,768]{2,1,0:T(8,128)S(1)}, f32[3,40,768]{2,1,0:T(8,128)S(1)}, u32[]{:S(2)}, u32[]{:S(2)}) collective-permute-start(f32[3,40,768]{2,1,0:T(8,128)S(1)} %collective-permute-done.6.mine_r), channel_id=1, source_target_pairs={{0,1},{1,0},{2,3},{3,2},{28,29},{29,28},{30,31},{31,30}} | collective-permute-start | bytes 1105928 | tf_op jit(solution)/shard_map/ppermute | solution.py:284
  26.4 0.0 collective-permute-done.8
  26.5 1.3 %collective-permute-start.9 = (f32[40,768]{1,0:T(8,128)S(1)}, f32[40,768]{1,0:T(8,128)S(1)}, u32[]{:S(2)}, u32[]{:S(2)}) collective-permute-start(f32[40,768]{1,0:T(8,128)S(1)} %fusion), channel_id=1, source_target_pairs={{4,0},{5,1},{6,2},{7,3},{24,28},{25,29},{26,30},{27,31}} | collective-permute-start | bytes 368648 | tf_op jit(solution)/shard_map/ppermute | solution.py:303
  27.8 0.7 %collective-permute-start.3 = (f32[8,320]{1,0:T(8,128)}, f32[8,320]{1,0:T(8,128)S(1)}, u32[]{:S(2)}, u32[]{:S(2)}) collective-permute-start(f32[8,320]{1,0:T(8,128)} %get-tuple-element.14), channel_id=1, source_target_pairs={{5,4},{6,5},{7,6},{4,7},{9,8},{10,9},{11,10},{8,11},{13,12},{14,13... | collective-permute-start | bytes 30728 | tf_op jit(solution)/shard_map/ppermute | solution.py:300
  28.4 0.7 %collective-permute-start.2 = (f32[8,320]{1,0:T(8,128)}, f32[8,320]{1,0:T(8,128)S(1)}, u32[]{:S(2)}, u32[]{:S(2)}) collective-permute-start(f32[8,320]{1,0:T(8,128)} %get-tuple-element.14), channel_id=1, source_target_pairs={{4,5},{5,6},{6,7},{7,4},{8,9},{9,10},{10,11},{11,8},{12,13},{13,14... | collective-permute-start | bytes 30728 | tf_op jit(solution)/shard_map/ppermute | solution.py:299
  29.1 0.0 collective-permute-done.3.right
  29.1 0.0 copy-start.8
  29.1 6.8 %collective-permute-start = (f32[5,16,720]{2,1,0:T(8,128)}, f32[5,16,720]{2,1,0:T(8,128)S(1)}, u32[]{:S(2)}, u32[]{:S(2)}) collective-permute-start(f32[5,16,720]{2,1,0:T(8,128)} %get-tuple-element.12), channel_id=1, source_target_pairs={{0,4},{4,0},{8,12},{12,8},{16,20},{20,16},{24,28},{28,24},{1,5},{5... | collective-permute-start | bytes 691208 | tf_op jit(solution)/shard_map/ppermute | solution.py:295
  35.9 0.0 collective-permute-done.2.left
  35.9 0.0 copy-start.9
  35.9 0.7 %collective-permute-start.1 = (f32[5,16,720]{2,1,0:T(8,128)}, f32[5,16,720]{2,1,0:T(8,128)S(1)}, u32[]{:S(2)}, u32[]{:S(2)}) collective-permute-start(f32[5,16,720]{2,1,0:T(8,128)} %get-tuple-element.13), channel_id=1, source_target_pairs={{4,8},{8,4},{12,16},{16,12},{20,24},{24,20},{5,9},{9,5},{13,17},{1... | collective-permute-start | bytes 691208 | tf_op jit(solution)/shard_map/ppermute | solution.py:296
  36.6 0.0 collective-permute-done.9.beside_t
  36.6 0.0 copy-start.6
  36.6 2.1 %collective-permute-start.10 = (f32[40,768]{1,0:T(8,128)S(1)}, f32[40,768]{1,0:T(8,128)S(1)}, u32[]{:S(2)}, u32[]{:S(2)}) collective-permute-start(f32[40,768]{1,0:T(8,128)S(1)} %collective-permute-done.9.beside_t), channel_id=1, source_target_pairs={{0,1},{1,0},{2,3},{3,2},{28,29},{29,28},{30,31},{31,30}} | collective-permute-start | bytes 368648 | tf_op jit(solution)/shard_map/ppermute | solution.py:284
  38.7 8.6 %collective-permute-done.recv_a = f32[5,16,720]{2,1,0:T(8,128)S(1)} collective-permute-done((f32[5,16,720]{2,1,0:T(8,128)}, f32[5,16,720]{2,1,0:T(8,128)S(1)}, u32[]{:S(2)}, u32[]{:S(2)}) %collective-permute-start) | collective-permute-done | bytes 230432 | tf_op jit(solution)/shard_map/ppermute | solution.py:295
  47.3 0.0 copy-start.4
  47.3 0.0 collective-permute-done.1.recv_b
  47.3 0.0 copy-start.5
  47.3 0.0 collective-permute-done.10.beside_o
  47.3 0.0 copy-start.7
  47.3 0.0 collective-permute-done.5.other
  47.3 0.0 copy-start.2
  47.3 0.0 collective-permute-done.7.other_r
  47.3 0.0 copy-start.3
  47.3 0.0 copy-done
  47.4 0.0 copy-done.1
  47.4 0.0 copy-done.8
  47.4 0.0 copy-done.9
  47.4 0.0 copy-done.6
  47.4 0.6 %copy-done.4 = f32[5,16,720]{2,1,0:T(8,128)} copy-done((f32[5,16,720]{2,1,0:T(8,128)}, f32[5,16,720]{2,1,0:T(8,128)S(1)}, u32[]{:S(2)}) %copy-start.4) | copy-done | bytes 230424
  48.0 0.1 copy-done.5
  48.1 0.0 copy-done.7
  48.1 0.1 copy-done.2
  48.2 0.1 copy-done.3
  48.3 5.6 %shard_map.83 = f32[4,5,16,720]{3,2,1,0:T(8,128)} custom-call(s32[2,4]{1,0:T(2,128)} %cutoff.1, f32[4,5,16,720]{3,2,1,0:T(8,128)} %get-tuple-element.11.base, f32[5,16,720]{2,1,0:T(8,128)} %copy-done.4, f32[5,16,720]{2,1,0:T(8,128)} %copy-done.5, f32[8,320]{1,0:T(8,128)} %copy-done.9, f32[8,320]{1,0:T(8,128)} %copy-done.8, f32[3,40,768]{2,1,0:T(8,128)} %copy-done, ...), custom_call_target="tpu_custom_call" | custom-call | tf_op jit(solution)/shard_map/pallas_call | solution.py:306
  (2 shorter events, 0.0 us)
Async XLA Ops:
  5.9 3.9 %collective-permute-start.4 = (f32[3,40,768]{2,1,0:T(8,128)}, f32[3,40,768]{2,1,0:T(8,128)S(1)}, u32[]{:S(2)}, u32[]{:S(2)}) collective-permute-start(f32[3,40,768]{2,1,0:T(8,128)} %get-tuple-element.16), channel_id=1, source_target_pairs={{0,1},{1,0},{2,3},{3,2},{28,29},{29,28},{30,31},{31,30},{4,5},{5,4... | collective-permute-start | bytes 1105928 | tf_op jit(solution)/shard_map/ppermute | solution.py:284
  10.8 36.5 %copy-start = (f32[3,40,768]{2,1,0:T(8,128)}, f32[3,40,768]{2,1,0:T(8,128)S(1)}, u32[]{:S(2)}) copy-start(f32[3,40,768]{2,1,0:T(8,128)S(1)} %add.6.mine) | copy-start | bytes 1105924
  10.9 13.6 %collective-permute-start.6 = (f32[3,40,768]{2,1,0:T(8,128)S(1)}, f32[3,40,768]{2,1,0:T(8,128)S(1)}, u32[]{:S(2)}, u32[]{:S(2)}) collective-permute-start(f32[3,40,768]{2,1,0:T(8,128)S(1)} %add.6.mine), channel_id=1, source_target_pairs={{0,2},{1,3},{2,0},{3,1},{28,30},{29,31},{30,28},{31,29}} | collective-permute-start | bytes 1105928 | tf_op jit(solution)/shard_map/ppermute | solution.py:284
  15.6 10.8 %collective-permute-start.8 = (f32[40,768]{1,0:T(8,128)S(1)}, f32[40,768]{1,0:T(8,128)S(1)}, u32[]{:S(2)}, u32[]{:S(2)}) collective-permute-start(f32[40,768]{1,0:T(8,128)S(1)} %slice_bitcast_fusion), channel_id=1, source_target_pairs={{4,6},{5,7},{6,4},{7,5},{24,26},{25,27},{26,24},{27,25}} | collective-permute-start | bytes 368648 | tf_op jit(solution)/shard_map/ppermute | solution.py:284
  16.3 31.0 %collective-permute-start.5 = (f32[3,40,768]{2,1,0:T(8,128)S(1)}, f32[3,40,768]{2,1,0:T(8,128)S(1)}, u32[]{:S(2)}, u32[]{:S(2)}) collective-permute-start(f32[3,40,768]{2,1,0:T(8,128)S(1)} %add.6.mine), channel_id=1, source_target_pairs={{0,1},{1,0},{2,3},{3,2},{28,29},{29,28},{30,31},{31,30}} | collective-permute-start | bytes 1105928 | tf_op jit(solution)/shard_map/ppermute | solution.py:284
  24.5 22.9 %copy-start.1 = (f32[3,40,768]{2,1,0:T(8,128)}, f32[3,40,768]{2,1,0:T(8,128)S(1)}, u32[]{:S(2)}) copy-start(f32[3,40,768]{2,1,0:T(8,128)S(1)} %collective-permute-done.6.mine_r) | copy-start | bytes 1105924
  24.5 22.8 %collective-permute-start.7 = (f32[3,40,768]{2,1,0:T(8,128)S(1)}, f32[3,40,768]{2,1,0:T(8,128)S(1)}, u32[]{:S(2)}, u32[]{:S(2)}) collective-permute-start(f32[3,40,768]{2,1,0:T(8,128)S(1)} %collective-permute-done.6.mine_r), channel_id=1, source_target_pairs={{0,1},{1,0},{2,3},{3,2},{28,29},{29,28},{30,31},{31,30}} | collective-permute-start | bytes 1105928 | tf_op jit(solution)/shard_map/ppermute | solution.py:284
  26.5 10.1 %collective-permute-start.9 = (f32[40,768]{1,0:T(8,128)S(1)}, f32[40,768]{1,0:T(8,128)S(1)}, u32[]{:S(2)}, u32[]{:S(2)}) collective-permute-start(f32[40,768]{1,0:T(8,128)S(1)} %fusion), channel_id=1, source_target_pairs={{4,0},{5,1},{6,2},{7,3},{24,28},{25,29},{26,30},{27,31}} | collective-permute-start | bytes 368648 | tf_op jit(solution)/shard_map/ppermute | solution.py:303
  27.8 1.3 %collective-permute-start.3 = (f32[8,320]{1,0:T(8,128)}, f32[8,320]{1,0:T(8,128)S(1)}, u32[]{:S(2)}, u32[]{:S(2)}) collective-permute-start(f32[8,320]{1,0:T(8,128)} %get-tuple-element.14), channel_id=1, source_target_pairs={{5,4},{6,5},{7,6},{4,7},{9,8},{10,9},{11,10},{8,11},{13,12},{14,13... | collective-permute-start | bytes 30728 | tf_op jit(solution)/shard_map/ppermute | solution.py:300
  28.4 7.5 %collective-permute-start.2 = (f32[8,320]{1,0:T(8,128)}, f32[8,320]{1,0:T(8,128)S(1)}, u32[]{:S(2)}, u32[]{:S(2)}) collective-permute-start(f32[8,320]{1,0:T(8,128)} %get-tuple-element.14), channel_id=1, source_target_pairs={{4,5},{5,6},{6,7},{7,4},{8,9},{9,10},{10,11},{11,8},{12,13},{13,14... | collective-permute-start | bytes 30728 | tf_op jit(solution)/shard_map/ppermute | solution.py:299
  29.1 18.3 %copy-start.8 = (f32[8,320]{1,0:T(8,128)}, f32[8,320]{1,0:T(8,128)S(1)}, u32[]{:S(2)}) copy-start(f32[8,320]{1,0:T(8,128)S(1)} %collective-permute-done.3.right) | copy-start | bytes 30724
  29.1 18.2 %collective-permute-start = (f32[5,16,720]{2,1,0:T(8,128)}, f32[5,16,720]{2,1,0:T(8,128)S(1)}, u32[]{:S(2)}, u32[]{:S(2)}) collective-permute-start(f32[5,16,720]{2,1,0:T(8,128)} %get-tuple-element.12), channel_id=1, source_target_pairs={{0,4},{4,0},{8,12},{12,8},{16,20},{20,16},{24,28},{28,24},{1,5},{5... | collective-permute-start | bytes 691208 | tf_op jit(solution)/shard_map/ppermute | solution.py:295
  35.9 11.5 %copy-start.9 = (f32[8,320]{1,0:T(8,128)}, f32[8,320]{1,0:T(8,128)S(1)}, u32[]{:S(2)}) copy-start(f32[8,320]{1,0:T(8,128)S(1)} %collective-permute-done.2.left) | copy-start | bytes 30724
  35.9 11.4 %collective-permute-start.1 = (f32[5,16,720]{2,1,0:T(8,128)}, f32[5,16,720]{2,1,0:T(8,128)S(1)}, u32[]{:S(2)}, u32[]{:S(2)}) collective-permute-start(f32[5,16,720]{2,1,0:T(8,128)} %get-tuple-element.13), channel_id=1, source_target_pairs={{4,8},{8,4},{12,16},{16,12},{20,24},{24,20},{5,9},{9,5},{13,17},{1... | collective-permute-start | bytes 691208 | tf_op jit(solution)/shard_map/ppermute | solution.py:296
  36.6 10.8 %copy-start.6 = (f32[40,768]{1,0:T(8,128)}, f32[40,768]{1,0:T(8,128)S(1)}, u32[]{:S(2)}) copy-start(f32[40,768]{1,0:T(8,128)S(1)} %collective-permute-done.9.beside_t) | copy-start | bytes 368644
  36.6 10.7 %collective-permute-start.10 = (f32[40,768]{1,0:T(8,128)S(1)}, f32[40,768]{1,0:T(8,128)S(1)}, u32[]{:S(2)}, u32[]{:S(2)}) collective-permute-start(f32[40,768]{1,0:T(8,128)S(1)} %collective-permute-done.9.beside_t), channel_id=1, source_target_pairs={{0,1},{1,0},{2,3},{3,2},{28,29},{29,28},{30,31},{31,30}} | collective-permute-start | bytes 368648 | tf_op jit(solution)/shard_map/ppermute | solution.py:284
  47.3 0.7 %copy-start.4 = (f32[5,16,720]{2,1,0:T(8,128)}, f32[5,16,720]{2,1,0:T(8,128)S(1)}, u32[]{:S(2)}) copy-start(f32[5,16,720]{2,1,0:T(8,128)S(1)} %collective-permute-done.recv_a) | copy-start | bytes 691204
  47.3 0.8 %copy-start.5 = (f32[5,16,720]{2,1,0:T(8,128)}, f32[5,16,720]{2,1,0:T(8,128)S(1)}, u32[]{:S(2)}) copy-start(f32[5,16,720]{2,1,0:T(8,128)S(1)} %collective-permute-done.1.recv_b) | copy-start | bytes 691204
  47.3 0.8 %copy-start.7 = (f32[40,768]{1,0:T(8,128)}, f32[40,768]{1,0:T(8,128)S(1)}, u32[]{:S(2)}) copy-start(f32[40,768]{1,0:T(8,128)S(1)} %collective-permute-done.10.beside_o) | copy-start | bytes 368644
  47.3 0.9 %copy-start.2 = (f32[3,40,768]{2,1,0:T(8,128)}, f32[3,40,768]{2,1,0:T(8,128)S(1)}, u32[]{:S(2)}) copy-start(f32[3,40,768]{2,1,0:T(8,128)S(1)} %collective-permute-done.5.other) | copy-start | bytes 1105924
  47.3 1.0 %copy-start.3 = (f32[3,40,768]{2,1,0:T(8,128)}, f32[3,40,768]{2,1,0:T(8,128)S(1)}, u32[]{:S(2)}) copy-start(f32[3,40,768]{2,1,0:T(8,128)S(1)} %collective-permute-done.7.other_r) | copy-start | bytes 1105924

commit v2 on v1

--- a/solution.py
+++ b/solution.py
@@ -13,6 +13,8 @@
 KF = 352
 LANE = 128
 VMEM = pltpu.VMEM
+OUT = pltpu.VMEM
+PLAIN_COST = pl.CostEstimate(flops=0, bytes_accessed=40_000_000, transcendentals=0)
 
 
 def ceil_to(value, unit):
@@ -72,7 +74,10 @@
     return south, polar, beside, even
 
 
-def local_kernel(lat_count, adj, east, north, fwd, turn, pole, base, edge_a, edge_b, sides, keep, send, flux, wide_x):
+def local_kernel(
+    lat_count, adj_hbm, east_hbm, north_hbm, fwd_hbm, turn_hbm, pole_hbm, base, edge_a, edge_b, sides, keep, send,
+    adj, east, north, fwd, turn, pole, flux, wide_x, ends, sems,
+):
     rows, tracers, levels, cols = adj.shape
     wide = flux.shape[-1]
     south, polar, beside, even = roles(lat_count)
@@ -80,12 +85,21 @@
     core = lax.rem(lon, 2)
     half_lev = levels // 2
     half = fwd.shape[-1] // 2
+    fetch = [
+        pltpu.make_async_copy(source, target, sems.at[n])
+        for n, (source, target) in enumerate(
+            ((adj_hbm, adj), (east_hbm, east), (north_hbm, north), (turn_hbm, turn), (pole_hbm, pole), (fwd_hbm, fwd))
+        )
+    ]
+    for copy in fetch:
+        copy.start()
+    for copy in fetch[:3]:
+        copy.wait()
     row_a = jnp.where(even, rows - 1, 0)
     row_b = rows - 1 - row_a
     edge_a[...] = north[row_a][None] * adj[row_a]
     edge_b[...] = north[row_b][None] * adj[row_b]
-
-    pad = jnp.zeros((levels, wide - cols), jnp.float32)
+    flux[:, cols:] = jnp.zeros((levels, wide - cols), jnp.float32)
 
     def transported(r, t):
         out = adj[r, t]
@@ -100,15 +114,10 @@
         f = flux[...]
         return pltpu.roll(f, wide - 1, 1) - pltpu.roll(f, 1, 1), f
 
-    flux[:, cols:] = pad
-
-    def turned(p):
+    def put(slot, p):
         a, b = turn[lon, 0:1], turn[lon, 1:2]
         c, s = p[:, :half], p[:, half:]
-        return c * a - s * b, s * a + c * b
-
-    def put(slot, p):
-        c, s = turned(p)
+        c, s = c * a - s * b, s * a + c * b
         n = c.shape[0] // 2
         keep[slot, :, :half] = c[:n]
         keep[slot, :, half:] = s[:n]
@@ -117,19 +126,23 @@
 
     @pl.when(jnp.logical_not(polar))
     def _():
-        ends = jnp.zeros((8, wide), jnp.float32)
-        row = lax.broadcasted_iota(jnp.int32, (8, wide), 0)
-        lane = lax.broadcasted_iota(jnp.int32, (8, wide), 1)
-        pick = jnp.where((row == 0) & (lane == 0) | (row == 1) & (lane == cols - 1), 1.0, 0.0).astype(jnp.float32)
+        start = cols // LANE * LANE
+        lane = lax.broadcasted_iota(jnp.int32, (levels, LANE), 1)
+        at = cols - 1 - start
         for r in range(rows):
             for t in range(tracers):
                 move, f = spread(r, t)
                 base[r, t] = transported(r, t) + move[:, :cols]
-                wide_x[r, 0, t] = f[:half_lev]
-                wide_x[r, 1, t] = f[half_lev:]
-        whole = wide_x[...].reshape(rows * tracers * levels, wide)
+                ends[r, t] = jnp.where(lane == 0, f[:, :LANE], jnp.where(lane == at, f[:, start : start + LANE], 0.0))
+        row = lax.broadcasted_iota(jnp.int32, (8, LANE), 0)
+        lane = lax.broadcasted_iota(jnp.int32, (8, LANE), 1)
+        pick = jnp.where((row == 0) & (lane == 0) | (row == 1) & (lane == at), 1.0, 0.0).astype(jnp.float32)
         sides[...] = lax.dot_general(
-            pick, whole, (((1,), (1,)), ((), ())), precision=lax.Precision.HIGHEST, preferred_element_type=jnp.float32
+            pick,
+            ends[...].reshape(rows * tracers * levels, LANE),
+            (((1,), (1,)), ((), ())),
+            precision=lax.Precision.HIGHEST,
+            preferred_element_type=jnp.float32,
         )
 
     @pl.when(beside)
@@ -140,7 +153,6 @@
             m = edge_a[t] * sign
             wide_x[2, core, t, :, :cols] = m[:half_lev]
             wide_x[2, 1 - core, t, :, :cols] = m[half_lev:]
-        put(2, dot3(wide_x[2].reshape(tracers * levels, wide), fwd))
 
     @pl.when(polar)
     def _():
@@ -154,6 +166,16 @@
                     where = jnp.where(core == 0, h, 1 - h)
                     wide_x[slot, where, t] = move[part]
                     wide_x[slot, where, t, :, :cols] += transported(r, t)[part]
+
+    for copy in fetch[3:]:
+        copy.wait()
+
+    @pl.when(beside)
+    def _():
+        put(2, dot3(wide_x[2].reshape(tracers * levels, wide), fwd))
+
+    @pl.when(polar)
+    def _():
         for slot in range(3):
             put(slot, dot3(wide_x[slot].reshape(tracers * levels, wide), fwd))
         sign = jnp.where(south, -1.0, 1.0).astype(jnp.float32)
@@ -178,51 +200,81 @@
                 )
 
 
-def last_kernel(
-    lat_count, circle, cutoff, base, recv_a, recv_b, left, right, mine, other, mine_r, other_r, beside_t, beside_o,
-    bwd, turn, pole, out, coef,
-):
-    rows, tracers, levels, cols = out.shape
-    half_lev = levels // 2
-    half = bwd.shape[1] // 2
-    south, polar, beside, even = roles(lat_count)
-    lon = lax.axis_index("lon")
-    core = lax.rem(lon, 2)
+def sum_kernel(x, y, out, third):
+    out[...] = x[...] + y[...]
+    third[...] = out[2]
+
+
+def total_kernel(lat_count, plain, mine, across, beside, beside_across, out):
+    _, polar, _, _ = roles(lat_count)
+
+    @pl.when(polar)
+    def _():
+        out[...] = mine[...] + across[...]
+        out[2] += beside[...] + beside_across[...]
+
+
+def plain_kernel(lat_count, base, recv_a, recv_b, left, right, beside, beside_across, out, rows_ref, sems):
+    rows, tracers, levels, cols = base.shape
+    south, polar, _, even = roles(lat_count)
 
     @pl.when(jnp.logical_not(polar))
     def _():
         row = lax.broadcasted_iota(jnp.int32, (8, LANE), 0)
         lane = lax.broadcasted_iota(jnp.int32, (8, LANE), 1)
-        at = (cols - 1) % LANE
+        start = cols // LANE * LANE
         low = jnp.where((row == 1) & (lane == 0), 1.0, 0.0).astype(jnp.float32)
-        high = jnp.where((row == 0) & (lane == at), 1.0, 0.0).astype(jnp.float32)
+        high = jnp.where((row == 0) & (lane == cols - 1 - start), 1.0, 0.0).astype(jnp.float32)
         dims = (((0,), (0,)), ((), ()))
         exact = lax.Precision.HIGHEST
         first = lax.dot_general(left[...], low, dims, precision=exact, preferred_element_type=jnp.float32)
         end = lax.dot_general(right[...], high, dims, precision=exact, preferred_element_type=jnp.float32)
-        start = cols // LANE * LANE
-        shape = (rows, 2, tracers, half_lev, LANE)
+        shape = (rows, tracers, levels, LANE)
         first, end = first.reshape(shape), end.reshape(shape)
-        out[...] = base[...]
+        up_a = jnp.where(even, 1.0, 0.0).astype(jnp.float32)
+        copies = []
         for r in range(rows):
+            value = base[r]
+            if r == rows - 1:
+                value = value + jnp.where(even, recv_a[...], recv_b[...])
+            if r == 0:
+                value = value - jnp.where(even, recv_b[...], recv_a[...])
+            rows_ref[r] = value
+            rows_ref[r, :, :, :LANE] -= first[r]
+            rows_ref[r, :, :, start:] += end[r][..., : cols - start]
+            copies.append(pltpu.make_async_copy(rows_ref.at[r], out.at[r], sems.at[r]))
+            copies[-1].start()
+        for copy in copies:
+            copy.wait()
+
+
+def cap_kernel(lat_count, circle, cutoff, given, mine, other, bwd, turn, pole, out, coef, rows_ref, sems):
+    rows, tracers, levels, cols = out.shape
+    half_lev = levels // 2
+    half = bwd.shape[1] // 2
+    south, polar, _, _ = roles(lat_count)
+    lon = lax.axis_index("lon")
+    core = lax.rem(lon, 2)
+
+    @pl.when(polar)
+    def _():
+        copies = []
+
+        def leave(k, row):
+            copies.append(pltpu.make_async_copy(rows_ref.at[k], out.at[row], sems.at[k]))
+            copies[-1].start()
+
+        coef[core] = mine[...]
+        coef[1 - core] = other[...]
+        cos, sin = pole[lon, 1:2], pole[lon, 2:3]
+        at = KF % LANE
+        for t in range(tracers):
             for h in (0, 1):
-                part = slice(h * half_lev, (h + 1) * half_lev)
-                out[r, :, part, :LANE] -= first[r, h]
-                out[r, :, part, start:] += end[r, h][..., : cols - start]
-        row_a = jnp.where(even, rows - 1, 0)
-        row_b = rows - 1 - row_a
-        sign = jnp.where(even, 1.0, -1.0).astype(jnp.float32)
-        out[row_a] += recv_a[...] * sign
-        out[row_b] -= recv_b[...] * sign
-
-    @pl.when(polar)
-    def _():
-        for slot in range(3):
-            own, far = mine[slot] + mine_r[slot], other[slot] + other_r[slot]
-            if slot == 2:
-                own, far = own + beside_t[...], far + beside_o[...]
-            coef[slot, core] = own
-            coef[slot, 1 - core] = far
+                p = coef[h, 2, t * half_lev : (t + 1) * half_lev, half - LANE : half]
+                c0, c1, s1 = p[:, at : at + 1], p[:, at + 1 : at + 2], p[:, at + 2 : at + 3]
+                y = (1.0 / circle) * c0 + (2.0 / circle) * (c1 * cos + s1 * sin)
+                rows_ref[3, t, h * half_lev : (h + 1) * half_lev, :] = y[:, :cols]
+        leave(3, jnp.where(south, rows - 1, 0))
         wave = lax.broadcasted_iota(jnp.int32, (1, half), 1)
         a, b = turn[lon, 0:1], turn[lon, 1:2]
         for slot in range(3):
@@ -230,26 +282,16 @@
             row = jnp.where(south, rows - 1 - near, near)
             kept = jnp.where(south, cutoff[1, row], cutoff[0, row])
             weight = jnp.where(wave <= kept, jnp.where(wave == 0, 1.0 / circle, 2.0 / circle), 0.0).astype(jnp.float32)
-            block = coef[slot].reshape(tracers * levels, 2 * half)
+            block = coef[:, slot].reshape(tracers * levels, 2 * half)
             c, s = block[:, :half], block[:, half:]
             wa, wb = weight * a, weight * b
             back = jnp.concatenate([c * wa + s * wb, s * wa - c * wb], axis=1)
             y = dot3(back, bwd).reshape(2, tracers, half_lev, -1)
             for h in (0, 1):
-                out[row, :, h * half_lev : (h + 1) * half_lev, :] = y[h][..., :cols]
-        row = jnp.where(south, rows - 1, 0)
-        cos, sin = pole[lon, 1:2], pole[lon, 2:3]
-        for t in range(tracers):
-            for h in (0, 1):
-                p = coef[2, h, t * half_lev : (t + 1) * half_lev, half - LANE : half]
-                at = KF % LANE
-                c0, c1, s1 = p[:, at : at + 1], p[:, at + 1 : at + 2], p[:, at + 2 : at + 3]
-                y = (1.0 / circle) * c0 + (2.0 / circle) * (c1 * cos + s1 * sin)
-                out[row, t, h * half_lev : (h + 1) * half_lev, :] = y[:, :cols]
-
-
-def routes(lat_count, lon_count, lats, step):
-    return [(a * lon_count + i, a * lon_count + (i ^ step)) for a in lats for i in range(lon_count)]
+                rows_ref[slot, :, h * half_lev : (h + 1) * half_lev, :] = y[h][..., :cols]
+            leave(slot, row)
+        for copy in copies:
+            copy.wait()
 
 
 def fast_body(adj, east, north, cutoff):
@@ -260,56 +302,101 @@
     wide, width = fwd.shape[1:]
     both = ("lat", "lon")
     last = lat_count - 1
-    f32 = jnp.float32
-    spec = pl.BlockSpec(memory_space=VMEM)
-    shape = jax.ShapeDtypeStruct
+    f32, bf16 = jnp.float32, jnp.bfloat16
+    vmem = pl.BlockSpec(memory_space=VMEM)
+    anywhere = pl.BlockSpec(memory_space=pl.ANY)
+    far = pl.BlockSpec(memory_space=pltpu.HBM)
+    params = pltpu.CompilerParams(vmem_limit_bytes=40 << 20)
+    dma = pltpu.SemaphoreType.DMA
     share = (3, tracers * levels // 2, width)
     n_rows = rows * tracers * levels
+
+    def near(x):
+        return pltpu.with_memory_space_constraint(x, VMEM)
+
+    def hbm(x):
+        return pltpu.with_memory_space_constraint(x, pltpu.HBM)
+
     base, edge_a, edge_b, sides, keep, send = pl.pallas_call(
         functools.partial(local_kernel, lat_count),
         out_shape=[
-            shape(adj.shape, f32),
-            shape(adj.shape[1:], f32),
-            shape(adj.shape[1:], f32),
-            shape((8, n_rows), f32),
-            shape(share, f32),
-            shape(share, f32),
+            OUT(adj.shape, f32),
+            OUT(adj.shape[1:], f32),
+            OUT(adj.shape[1:], f32),
+            OUT((8, n_rows), f32),
+            OUT(share, f32),
+            OUT(share, f32),
         ],
-        in_specs=[spec] * 6,
-        out_specs=[spec] * 6,
-        scratch_shapes=[VMEM((levels, wide), f32), VMEM((rows, 2, tracers, levels // 2, wide), f32)],
-    )(adj, east, north, fwd, turn, pole)
-
-    def move(x, lats, step):
-        return lax.ppermute(x, both, routes(lat_count, lon_count, lats, step))
-
+        in_specs=[far] * 6,
+        out_specs=[vmem] * 6,
+        scratch_shapes=[
+            VMEM(adj.shape, f32),
+            VMEM(east.shape, f32),
+            VMEM(north.shape, f32),
+            VMEM(fwd.shape, bf16),
+            VMEM(turn.shape, f32),
+            VMEM(pole.shape, f32),
+            VMEM((levels, wide), f32),
+            VMEM((rows, 2, tracers, levels // 2, wide), f32),
+            VMEM((rows, tracers, levels, LANE), f32),
+            dma((6,)),
+        ],
+        compiler_params=params,
+    )(*map(hbm, (adj, east, north, fwd, turn, pole)))
+
+    def hop(x, pairs):
+        return lax.ppermute(x, both, [(a * lon_count + i, b * lon_count + j) for a, i, b, j in pairs])
+
+    lons = range(lon_count)
     caps = (0, last)
-    nexts = (1, last - 1)
-    got = move(send, caps + nexts, 1)
-    total = keep + got
-    third = total[2]
-    third_r = move(third, nexts, 2)
-    third_sum = third + third_r
-    mine_r = move(total, caps, 2)
-    swap_a = [(i ^ 1) for i in range(lat_count)]
-    recv_a = lax.ppermute(edge_a, "lat", list(enumerate(swap_a)))
+    to_cap = ((1, 0), (last - 1, last))
+    got = hop(send, [(a, i, a, i ^ 1) for a in (0, 1, last - 1, last) for i in lons])
+    edge_pairs = [(i, i ^ 1) for i in range(lat_count) if (i, i ^ 1) not in to_cap]
+    recv_a = lax.ppermute(edge_a, "lat", edge_pairs)
+    total, third = pl.pallas_call(
+        sum_kernel,
+        out_shape=[OUT(share, f32), OUT(share[1:], f32)],
+        in_specs=[vmem] * 2,
+        out_specs=[vmem] * 2,
+        compiler_params=params,
+    )(near(keep), near(got))
+    across = hop(total, [(a, i, a, i ^ 2) for a in caps for i in lons])
+    beside = hop(third, [(a, i, b, i) for a, b in to_cap for i in lons])
+    beside_across = hop(third, [(a, i, b, i ^ 2) for a, b in to_cap for i in lons])
     recv_b = lax.ppermute(edge_b, "lat", [(i, j) for k in range(1, last, 2) for i, j in ((k, k + 1), (k + 1, k))])
-    inner = range(1, last)
-    ring = [(a * lon_count + i, a * lon_count + (i + 1) % lon_count) for a in inner for i in range(lon_count)]
-    left = lax.ppermute(sides, both, ring)
-    right = lax.ppermute(sides, both, [(j, i) for i, j in ring])
-    other = move(total, caps, 1)
-    to_cap = [(a * lon_count + i, b * lon_count + i) for a, b in ((1, 0), (last - 1, last)) for i in range(lon_count)]
-    beside_t = lax.ppermute(third_sum, both, to_cap)
-    other_r = move(mine_r, caps, 1)
-    beside_o = move(beside_t, caps, 1)
+    ring = [(a, i, a, (i + 1) % lon_count) for a in range(1, last) for i in lons]
+    left = hop(sides, ring)
+    right = hop(sides, [(a, j, a, i) for a, i, _, j in ring])
+    plain = pl.pallas_call(
+        functools.partial(plain_kernel, lat_count),
+        out_shape=jax.ShapeDtypeStruct(adj.shape, f32),
+        in_specs=[vmem] * 7,
+        out_specs=anywhere,
+        scratch_shapes=[VMEM(adj.shape, f32), dma((rows,))],
+        compiler_params=params,
+        cost_estimate=PLAIN_COST,
+    )(near(base), near(recv_a), near(recv_b), near(left), near(right), near(beside), near(beside_across))
+    mine = pl.pallas_call(
+        functools.partial(total_kernel, lat_count),
+        out_shape=OUT(share, f32),
+        in_specs=[far] + [vmem] * 4,
+        out_specs=vmem,
+        compiler_params=params,
+    )(hbm(plain), near(total), near(across), near(beside), near(beside_across))
+    other = hop(mine, [(a, i, a, i ^ 1) for a in caps for i in lons])
     return pl.pallas_call(
-        functools.partial(last_kernel, lat_count, circle),
-        out_shape=shape(adj.shape, f32),
-        in_specs=[pl.BlockSpec(memory_space=pltpu.SMEM)] + [spec] * 14,
-        out_specs=spec,
-        scratch_shapes=[VMEM((3, 2, tracers * levels // 2, width), f32)],
-    )(cutoff, base, recv_a, recv_b, left, right, total, other, mine_r, other_r, beside_t, beside_o, bwd, turn, pole)
+        functools.partial(cap_kernel, lat_count, circle),
+        out_shape=jax.ShapeDtypeStruct(adj.shape, f32),
+        in_specs=[pl.BlockSpec(memory_space=pltpu.SMEM), anywhere] + [vmem] * 5,
+        out_specs=anywhere,
+        scratch_shapes=[
+            VMEM((2,) + share, f32),
+            VMEM(adj.shape, f32),
+            dma((rows,)),
+        ],
+        input_output_aliases={1: 0},
+        compiler_params=params,
+    )(cutoff, plain, near(mine), near(other), near(bwd), near(turn), near(pole))
 
 
 full_precision = lax.Precision.HIGHEST

time: 54.3 us -> 35.1 us (0.65)
  starting transfers between devices: 23.7 us -> 15.1 us
  waiting for transfers between devices: 16.4 us -> 11.8 us
  Pallas kernels: 11.5 us -> 7.76 us
  other arithmetic: 1.06 us -> 0 us
  local copies, waits for them, and re-layouts: 0.99 us -> 0.01 us
    ppermute x10 -> x8, starting transfers between devices: 23.1 us -> 14.4 us  [the longest x7 13.1 us: hop(): lax.ppermute(x, both, [(a * lon_count + i, b * lon_count + j) for a, i, b...]
    ppermute x10 -> x8, waiting for transfers between devices: 16.4 us -> 11.8 us  [the longest x1 6.1 us: fast_body(): recv_a = lax.ppermute(edge_a, 'lat', edge_pairs)]
    pallas_call x2 -> x5, Pallas kernels: 11.5 us -> 7.76 us  [the longest x1 4.17 us: fast_body(): pl.pallas_call(functools.partial(local_kernel, lat_count), out_shape=[OUT...]
    add x2 -> x0, other arithmetic: 1.06 us -> none  [the longest x1 1.04 us: fast_body(): total = keep + got]
    unnamed x20 -> x8, local copies, waits for them, and re-layouts: 0.98 us -> 0.01 us
  transfers between devices with their start and end apart: 11 -> 9, of which waited for: 3 -> 5; matrix products, arithmetic and copies ran while one was open for 0% -> 0% of each run, Pallas kernels for 0% -> 0%
where the time goes in v2:
time: 35.1 us; the launch traced here: 34.8 us
  starting transfers between devices  15.1 us (43%)
  waiting for transfers between devices  11.8 us (34%)
  Pallas kernels  7.76 us (22%)
    ppermute x7, starting transfers between devices, hop(): lax.ppermute(x, both, [(a * lon_count + i, b * lon_count + j) for a, i, b...  13.1 us
    ppermute x1, waiting for transfers between devices, fast_body(): recv_a = lax.ppermute(edge_a, 'lat', edge_pairs)  6.1 us
    ppermute x7, waiting for transfers between devices, hop(): lax.ppermute(x, both, [(a * lon_count + i, b * lon_count + j) for a, i, b...  5.72 us
    pallas_call x1, Pallas kernels, fast_body(): pl.pallas_call(functools.partial(local_kernel, lat_count), out_shape=[OUT...  4.17 us
    pallas_call x1, Pallas kernels, fast_body(): pl.pallas_call(functools.partial(cap_kernel, lat_count, circle), out_shap...  3.42 us
    ppermute x1, starting transfers between devices, fast_body(): recv_a = lax.ppermute(edge_a, 'lat', edge_pairs)  1.3 us
  transfers between devices with their start and end apart: 9, of which 5 were waited for; matrix products, arithmetic and copies ran while one was open for 0% of the time, Pallas kernels for 0%

profile of v2, /device:TPU:0, one launch (start us, length us, event | category | flops | bytes accessed | tf_op | source)
XLA Modules:
  0.0 34.8 jit_solution(17562168862916708333)
XLA Ops:
  0.0 4.2 %shard_map.82 = (f32[4,5,16,720]{3,2,1,0:T(8,128)S(1)}, f32[5,16,720]{2,1,0:T(8,128)S(1)}, f32[5,16,720]{2,1,0:T(8,128)S(1)}, f32[8,320]{1,0:T(8,128)S(1)}, f32[...) custom-call(f32[4,5,16,720]{3,2,1,0:T(8,128)} %adj_hbm.1, f32[4,16,720]{2,1,0:T(8,128)} %east_hbm.1, ...), custom_call_target="tpu_custom_call" | custom-call | tf_op jit(solution)/shard_map/pallas_call | solution.py:320
  4.2 2.4 %collective-permute-start.4 = (f32[3,40,768]{2,1,0:T(8,128)S(1)}, f32[3,40,768]{2,1,0:T(8,128)S(1)}, u32[]{:S(2)}, u32[]{:S(2)}) collective-permute-start(f32[3,40,768]{2,1,0:T(8,128)S(1)} %get-tuple-element.18), channel_id=1, source_target_pairs={{0,1},{1,0},{2,3},{3,2},{4,5},{5,4},{6,7},{7,6},{24,25},{25,24},{2... | collective-permute-start | bytes 1105928 | tf_op jit(solution)/shard_map/ppermute | solution.py:348
  6.5 1.3 %collective-permute-done.4.y = f32[3,40,768]{2,1,0:T(8,128)S(1)} collective-permute-done((f32[3,40,768]{2,1,0:T(8,128)S(1)}, f32[3,40,768]{2,1,0:T(8,128)S(1)}, u32[]{:S(2)}, u32[]{:S(2)}) %collective-permute-start.4) | collective-permute-done | bytes 368672 | tf_op jit(solution)/shard_map/ppermute | solution.py:348
  7.9 4.8 %collective-permute-start.7 = (f32[3,40,768]{2,1,0:T(8,128)S(1)}, f32[3,40,768]{2,1,0:T(8,128)S(1)}, u32[]{:S(2)}, u32[]{:S(2)}) collective-permute-start(f32[3,40,768]{2,1,0:T(8,128)S(1)} %get-tuple-element.20.mine), channel_id=1, source_target_pairs={{0,2},{1,3},{2,0},{3,1},{28,30},{29,31},{30,28},{31,29}} | collective-permute-start | bytes 1105928 | tf_op jit(solution)/shard_map/ppermute | solution.py:348
  12.7 1.3 %collective-permute-start = (f32[5,16,720]{2,1,0:T(8,128)S(1)}, f32[5,16,720]{2,1,0:T(8,128)S(1)}, u32[]{:S(2)}, u32[]{:S(2)}) collective-permute-start(f32[5,16,720]{2,1,0:T(8,128)S(1)} %get-tuple-element.14), channel_id=1, source_target_pairs={{0,4},{8,12},{12,8},{16,20},{20,16},{28,24},{1,5},{9,13},{13,9},{1... | collective-permute-start | bytes 691208 | tf_op jit(solution)/shard_map/ppermute | solution.py:355
  14.0 0.7 %collective-permute-start.1 = (f32[5,16,720]{2,1,0:T(8,128)S(1)}, f32[5,16,720]{2,1,0:T(8,128)S(1)}, u32[]{:S(2)}, u32[]{:S(2)}) collective-permute-start(f32[5,16,720]{2,1,0:T(8,128)S(1)} %get-tuple-element.15), channel_id=1, source_target_pairs={{4,8},{8,4},{12,16},{16,12},{20,24},{24,20},{5,9},{9,5},{13,17},{1... | collective-permute-start | bytes 691208 | tf_op jit(solution)/shard_map/ppermute | solution.py:366
  14.7 0.7 %collective-permute-start.3 = (f32[8,320]{1,0:T(8,128)S(1)}, f32[8,320]{1,0:T(8,128)S(1)}, u32[]{:S(2)}, u32[]{:S(2)}) collective-permute-start(f32[8,320]{1,0:T(8,128)S(1)} %get-tuple-element.16), channel_id=1, source_target_pairs={{5,4},{6,5},{7,6},{4,7},{9,8},{10,9},{11,10},{8,11},{13,12},{14,13... | collective-permute-start | bytes 30728 | tf_op jit(solution)/shard_map/ppermute | solution.py:348
  15.3 0.7 %collective-permute-start.2 = (f32[8,320]{1,0:T(8,128)S(1)}, f32[8,320]{1,0:T(8,128)S(1)}, u32[]{:S(2)}, u32[]{:S(2)}) collective-permute-start(f32[8,320]{1,0:T(8,128)S(1)} %get-tuple-element.16), channel_id=1, source_target_pairs={{4,5},{5,6},{6,7},{7,4},{8,9},{9,10},{10,11},{11,8},{12,13},{13,14... | collective-permute-start | bytes 30728 | tf_op jit(solution)/shard_map/ppermute | solution.py:348
  16.0 0.0 collective-permute-done.3.right
  16.0 1.3 %collective-permute-start.6 = (f32[40,768]{1,0:T(8,128)S(1)}, f32[40,768]{1,0:T(8,128)S(1)}, u32[]{:S(2)}, u32[]{:S(2)}) collective-permute-start(f32[40,768]{1,0:T(8,128)S(1)} %get-tuple-element.19), channel_id=1, source_target_pairs={{4,2},{5,3},{6,0},{7,1},{24,30},{25,31},{26,28},{27,29}} | collective-permute-start | bytes 368648 | tf_op jit(solution)/shard_map/ppermute | solution.py:348
  17.3 0.0 collective-permute-done.2.left
  17.3 1.3 %collective-permute-start.5 = (f32[40,768]{1,0:T(8,128)S(1)}, f32[40,768]{1,0:T(8,128)S(1)}, u32[]{:S(2)}, u32[]{:S(2)}) collective-permute-start(f32[40,768]{1,0:T(8,128)S(1)} %get-tuple-element.19), channel_id=1, source_target_pairs={{4,0},{5,1},{6,2},{7,3},{24,28},{25,29},{26,30},{27,31}} | collective-permute-start | bytes 368648 | tf_op jit(solution)/shard_map/ppermute | solution.py:348
  18.6 6.1 %collective-permute-done.recv_a = f32[5,16,720]{2,1,0:T(8,128)S(1)} collective-permute-done((f32[5,16,720]{2,1,0:T(8,128)S(1)}, f32[5,16,720]{2,1,0:T(8,128)S(1)}, u32[]{:S(2)}, u32[]{:S(2)}) %collective-permute-start) | collective-permute-done | bytes 230432 | tf_op jit(solution)/shard_map/ppermute | solution.py:355
  24.7 0.0 collective-permute-done.1.recv_b
  24.7 0.2 collective-permute-done.6.beside_across
  25.0 2.5 %collective-permute-done.5.beside = f32[40,768]{1,0:T(8,128)S(1)} collective-permute-done((f32[40,768]{1,0:T(8,128)S(1)}, f32[40,768]{1,0:T(8,128)S(1)}, u32[]{:S(2)}, u32[]{:S(2)}) %collective-permute-start.5) | collective-permute-done | bytes 122912 | tf_op jit(solution)/shard_map/ppermute | solution.py:348
  27.5 0.0 copy-start
  27.5 0.0 copy-start.1
  27.5 0.0 copy-start.2
  27.5 0.0 copy-start.3
  27.5 0.1 shard_map.84.plain.given
  27.6 0.0 collective-permute-done.7.across
  27.6 0.1 shard_map.85.mine
  27.7 2.1 %collective-permute-start.8 = (f32[3,40,768]{2,1,0:T(8,128)S(1)}, f32[3,40,768]{2,1,0:T(8,128)S(1)}, u32[]{:S(2)}, u32[]{:S(2)}) collective-permute-start(f32[3,40,768]{2,1,0:T(8,128)S(1)} %shard_map.85.mine), channel_id=1, source_target_pairs={{0,1},{1,0},{2,3},{3,2},{28,29},{29,28},{30,31},{31,30}} | collective-permute-start | bytes 1105928 | tf_op jit(solution)/shard_map/ppermute | solution.py:348
  29.7 1.6 %collective-permute-done.8.other = f32[3,40,768]{2,1,0:T(8,128)S(1)} collective-permute-done((f32[3,40,768]{2,1,0:T(8,128)S(1)}, f32[3,40,768]{2,1,0:T(8,128)S(1)}, u32[]{:S(2)}, u32[]{:S(2)}) %collective-permute-start.8) | collective-permute-done | bytes 368672 | tf_op jit(solution)/shard_map/ppermute | solution.py:348
  31.4 0.0 copy-done
  31.4 0.0 copy-done.1
  31.4 0.0 copy-done.2
  31.4 0.0 copy-done.3
  31.4 3.4 %shard_map.86 = f32[4,5,16,720]{3,2,1,0:T(8,128)} custom-call(s32[2,4]{1,0:T(2,128)S(1)} %copy-done.3, f32[4,5,16,720]{3,2,1,0:T(8,128)} %shard_map.84.plain.given, f32[3,40,768]{2,1,0:T(8,128)S(1)} %shard_map.85.mine, f32[3,40,768]{2,1,0:T(8,128)S(1)} %collective-permute-done.8.other, ...), custom_call_target="tpu_custom_call", output_to_operand_aliasing={{}: (1, {})} | custom-call | tf_op jit(solution)/shard_map/pallas_call | solution.py:387
  (1 shorter events, 0.0 us)
Async XLA Ops:
  4.2 3.7 %collective-permute-start.4 = (f32[3,40,768]{2,1,0:T(8,128)S(1)}, f32[3,40,768]{2,1,0:T(8,128)S(1)}, u32[]{:S(2)}, u32[]{:S(2)}) collective-permute-start(f32[3,40,768]{2,1,0:T(8,128)S(1)} %get-tuple-element.18), channel_id=1, source_target_pairs={{0,1},{1,0},{2,3},{3,2},{4,5},{5,4},{6,7},{7,6},{24,25},{25,24},{2... | collective-permute-start | bytes 1105928 | tf_op jit(solution)/shard_map/ppermute | solution.py:348
  7.9 19.7 %collective-permute-start.7 = (f32[3,40,768]{2,1,0:T(8,128)S(1)}, f32[3,40,768]{2,1,0:T(8,128)S(1)}, u32[]{:S(2)}, u32[]{:S(2)}) collective-permute-start(f32[3,40,768]{2,1,0:T(8,128)S(1)} %get-tuple-element.20.mine), channel_id=1, source_target_pairs={{0,2},{1,3},{2,0},{3,1},{28,30},{29,31},{30,28},{31,29}} | collective-permute-start | bytes 1105928 | tf_op jit(solution)/shard_map/ppermute | solution.py:348
  12.7 12.1 %collective-permute-start = (f32[5,16,720]{2,1,0:T(8,128)S(1)}, f32[5,16,720]{2,1,0:T(8,128)S(1)}, u32[]{:S(2)}, u32[]{:S(2)}) collective-permute-start(f32[5,16,720]{2,1,0:T(8,128)S(1)} %get-tuple-element.14), channel_id=1, source_target_pairs={{0,4},{8,12},{12,8},{16,20},{20,16},{28,24},{1,5},{9,13},{13,9},{1... | collective-permute-start | bytes 691208 | tf_op jit(solution)/shard_map/ppermute | solution.py:355
  14.0 10.8 %collective-permute-start.1 = (f32[5,16,720]{2,1,0:T(8,128)S(1)}, f32[5,16,720]{2,1,0:T(8,128)S(1)}, u32[]{:S(2)}, u32[]{:S(2)}) collective-permute-start(f32[5,16,720]{2,1,0:T(8,128)S(1)} %get-tuple-element.15), channel_id=1, source_target_pairs={{4,8},{8,4},{12,16},{16,12},{20,24},{24,20},{5,9},{9,5},{13,17},{1... | collective-permute-start | bytes 691208 | tf_op jit(solution)/shard_map/ppermute | solution.py:366
  14.7 1.3 %collective-permute-start.3 = (f32[8,320]{1,0:T(8,128)S(1)}, f32[8,320]{1,0:T(8,128)S(1)}, u32[]{:S(2)}, u32[]{:S(2)}) collective-permute-start(f32[8,320]{1,0:T(8,128)S(1)} %get-tuple-element.16), channel_id=1, source_target_pairs={{5,4},{6,5},{7,6},{4,7},{9,8},{10,9},{11,10},{8,11},{13,12},{14,13... | collective-permute-start | bytes 30728 | tf_op jit(solution)/shard_map/ppermute | solution.py:348
  15.3 2.0 %collective-permute-start.2 = (f32[8,320]{1,0:T(8,128)S(1)}, f32[8,320]{1,0:T(8,128)S(1)}, u32[]{:S(2)}, u32[]{:S(2)}) collective-permute-start(f32[8,320]{1,0:T(8,128)S(1)} %get-tuple-element.16), channel_id=1, source_target_pairs={{4,5},{5,6},{6,7},{7,4},{8,9},{9,10},{10,11},{11,8},{12,13},{13,14... | collective-permute-start | bytes 30728 | tf_op jit(solution)/shard_map/ppermute | solution.py:348
  16.0 9.0 %collective-permute-start.6 = (f32[40,768]{1,0:T(8,128)S(1)}, f32[40,768]{1,0:T(8,128)S(1)}, u32[]{:S(2)}, u32[]{:S(2)}) collective-permute-start(f32[40,768]{1,0:T(8,128)S(1)} %get-tuple-element.19), channel_id=1, source_target_pairs={{4,2},{5,3},{6,0},{7,1},{24,30},{25,31},{26,28},{27,29}} | collective-permute-start | bytes 368648 | tf_op jit(solution)/shard_map/ppermute | solution.py:348
  17.3 10.2 %collective-permute-start.5 = (f32[40,768]{1,0:T(8,128)S(1)}, f32[40,768]{1,0:T(8,128)S(1)}, u32[]{:S(2)}, u32[]{:S(2)}) collective-permute-start(f32[40,768]{1,0:T(8,128)S(1)} %get-tuple-element.19), channel_id=1, source_target_pairs={{4,0},{5,1},{6,2},{7,3},{24,28},{25,29},{26,30},{27,31}} | collective-permute-start | bytes 368648 | tf_op jit(solution)/shard_map/ppermute | solution.py:348
  27.5 3.9 %copy-start = (bf16[2,768,768]{2,1,0:T(8,128)(2,1)S(1)}, bf16[2,768,768]{2,1,0:T(8,128)(2,1)}, u32[]{:S(2)}) copy-start(bf16[2,768,768]{2,1,0:T(8,128)(2,1)} %constant.11.clone.bwd) | copy-start | bytes 7077892
  27.5 3.9 %copy-start.1 = (f32[4,4,768]{2,1,0:T(4,128)S(1)}, f32[4,4,768]{2,1,0:T(4,128)}, u32[]{:S(2)}) copy-start(f32[4,4,768]{2,1,0:T(4,128)} %constant.10.clone.pole_hbm.pole) | copy-start | bytes 147460
  27.5 3.9 %copy-start.2 = (f32[4,2,384]{2,1,0:T(2,128)S(1)}, f32[4,2,384]{2,1,0:T(2,128)}, u32[]{:S(2)}) copy-start(f32[4,2,384]{2,1,0:T(2,128)} %constant.9.clone.turn_hbm.turn) | copy-start | bytes 36868
  27.5 3.9 %copy-start.3 = (s32[2,4]{1,0:T(2,128)S(1)}, s32[2,4]{1,0:T(2,128)}, u32[]{:S(2)}) copy-start(s32[2,4]{1,0:T(2,128)} %cutoff.1) | copy-start | bytes 100
  27.7 3.7 %collective-permute-start.8 = (f32[3,40,768]{2,1,0:T(8,128)S(1)}, f32[3,40,768]{2,1,0:T(8,128)S(1)}, u32[]{:S(2)}, u32[]{:S(2)}) collective-permute-start(f32[3,40,768]{2,1,0:T(8,128)S(1)} %shard_map.85.mine), channel_id=1, source_target_pairs={{0,1},{1,0},{2,3},{3,2},{28,29},{29,28},{30,31},{31,30}} | collective-permute-start | bytes 1105928 | tf_op jit(solution)/shard_map/ppermute | solution.py:348

commit v3 on v0

--- a/solution.py
+++ b/solution.py
@@ -1,11 +1,454 @@
+import functools
 import math
 
 import jax
 import jax.numpy as jnp
+import ml_dtypes
+import numpy as np
 from jax import lax
+from jax.experimental import pallas as pl
+from jax.experimental.pallas import tpu as pltpu
 from jax.sharding import PartitionSpec as P
 
 KF = 352
+LANE = 128
+VMEM = pltpu.VMEM
+HBM = pltpu.HBM
+HEAVY = pl.CostEstimate(flops=2**37, bytes_accessed=0, transcendentals=0)
+LIGHT = pl.CostEstimate(flops=0, bytes_accessed=1000, transcendentals=0)
+
+
+def ceil_to(value, unit):
+    return -(-value // unit) * unit
+
+
+def split16(table):
+    high = table.astype(ml_dtypes.bfloat16)
+    low = (table - high.astype(np.float64)).astype(ml_dtypes.bfloat16)
+    return np.stack([high, low])
+
+
+def tables(cols, circle, lon_count):
+    wide = ceil_to(cols + 2, LANE)
+    half = ceil_to(KF + 2, LANE)
+    place = np.zeros(wide, np.int64)
+    place[: cols + 1] = np.arange(cols + 1)
+    place[-1] = -1
+    live = np.zeros(wide)
+    live[: cols + 1] = 1
+    live[-1] = 1
+    mode = np.arange(KF)
+    phase = 2 * np.pi * ((place[:, None] * mode[None]) % circle) / circle
+    forward = np.zeros((wide, 2 * half))
+    forward[:, :KF] = np.cos(phase) * live[:, None]
+    forward[:, half : half + KF] = np.sin(phase) * live[:, None]
+    backward = forward.T.copy()
+    backward[:, cols:] = 0
+    turn = np.zeros((lon_count, 2, half), np.float32)
+    angle = 2 * np.pi * ((np.arange(lon_count)[:, None] * mode[None]) % lon_count) / lon_count
+    turn[:, 0, :KF] = np.cos(angle)
+    turn[:, 1, :KF] = np.sin(angle)
+    pole = np.zeros((lon_count, 4, wide), np.float32)
+    for index in range(lon_count):
+        first = 2 * np.pi * (place + index * cols) / circle
+        pole[index, 0] = live
+        pole[index, 1] = np.cos(first) * live
+        pole[index, 2] = np.sin(first) * live
+    return split16(forward), split16(backward), turn, pole
+
+
+def dot3(block, table_ref):
+    rows = block.shape[0]
+    high = block.astype(jnp.bfloat16)
+    low = (block - high.astype(jnp.float32)).astype(jnp.bfloat16)
+    stack = jnp.dot(jnp.concatenate([high, low]), table_ref[0], preferred_element_type=jnp.float32)
+    return stack[:rows] + stack[rows:] + jnp.dot(high, table_ref[1], preferred_element_type=jnp.float32)
+
+
+def latitude_role(lat_count):
+    lat = lax.axis_index("lat")
+    south = lat == lat_count - 1
+    return south, jnp.logical_or(lat == 0, south), lax.rem(lat, 2) == 0
+
+
+def longitude_role():
+    lon = lax.axis_index("lon")
+    core = lax.rem(lon, 2)
+    return lon, core, core == 0
+
+
+def turned(p, turn, lon):
+    half = p.shape[1] // 2
+    a, b = turn[lon, 0:1], turn[lon, 1:2]
+    c, s = p[:, :half], p[:, half:]
+    return c * a - s * b, s * a + c * b
+
+
+def weighted(block, kept, circle, turn, lon):
+    half = block.shape[1] // 2
+    wave = lax.broadcasted_iota(jnp.int32, (1, half), 1)
+    weight = jnp.where(wave <= kept, jnp.where(wave == 0, 1.0 / circle, 2.0 / circle), 0.0).astype(jnp.float32)
+    wa, wb = weight * turn[lon, 0:1], weight * turn[lon, 1:2]
+    c, s = block[:, :half], block[:, half:]
+    return jnp.concatenate([c * wa + s * wb, s * wa - c * wb], axis=1)
+
+
+def edge_kernel(lat_count, adj_hbm, north_hbm, edge, adj, north, sems):
+    _, _, even = latitude_role(lat_count)
+    row = jnp.where(even, adj_hbm.shape[0] - 1, 0)
+    copies = (
+        pltpu.make_async_copy(adj_hbm.at[row], adj, sems.at[0]),
+        pltpu.make_async_copy(north_hbm.at[row], north, sems.at[1]),
+    )
+    for copy in copies:
+        copy.start()
+    for copy in copies:
+        copy.wait()
+    edge[...] = north[...][None] * adj[...]
+
+
+def local_kernel(
+    lat_count, after, adj_hbm, east_hbm, north_hbm, fwd_hbm, turn_hbm, pole_hbm, base, keep, send, third, fwd, turn,
+    adj, east, north, pole, flux, wide_x, ends, sems,
+):
+    fetch = [
+        pltpu.make_async_copy(source, target, sems.at[n])
+        for n, (source, target) in enumerate(
+            ((adj_hbm, adj), (east_hbm, east), (north_hbm, north), (turn_hbm, turn), (pole_hbm, pole), (fwd_hbm, fwd))
+        )
+    ]
+    for copy in fetch:
+        copy.start()
+    for copy in fetch[:3]:
+        copy.wait()
+    rows, tracers, levels, cols = adj.shape
+    wide = flux.shape[-1]
+    south, polar, even = latitude_role(lat_count)
+    lon, own, _ = longitude_role()
+    half_lev = levels // 2
+    n_half = tracers * half_lev
+    half = fwd.shape[-1] // 2
+    row_b = jnp.where(even, 0, rows - 1)
+    flux[:, cols:] = jnp.zeros((levels, wide - cols), jnp.float32)
+
+    def transported(r, t):
+        out = adj[r, t]
+        if r + 1 < rows:
+            out = out + north[r + 1] * adj[r + 1, t]
+        if r > 0:
+            out = out - north[r - 1] * adj[r - 1, t]
+        return out
+
+    def spread(r, t):
+        flux[:, :cols] = east[r] * adj[r, t]
+        f = flux[...]
+        return pltpu.roll(f, wide - 1, 1) - pltpu.roll(f, 1, 1), f
+
+    @pl.when(jnp.logical_not(polar))
+    def _():
+        start = cols // LANE * LANE
+        lane = lax.broadcasted_iota(jnp.int32, (levels, LANE), 1)
+        at = cols - 1 - start
+        for r in range(rows):
+            for t in range(tracers):
+                move, f = spread(r, t)
+                base[r, t] = transported(r, t) + move[:, :cols]
+                ends[r, t] = jnp.where(lane == 0, f[:, :LANE], jnp.where(lane == at, f[:, start : start + LANE], 0.0))
+        row = lax.broadcasted_iota(jnp.int32, (8, LANE), 0)
+        lane = lax.broadcasted_iota(jnp.int32, (8, LANE), 1)
+        pick = jnp.where((row == 0) & (lane == 0) | (row == 1) & (lane == at), 1.0, 0.0).astype(jnp.float32)
+        sides = lax.dot_general(
+            pick,
+            ends[...].reshape(rows * tracers * levels, LANE),
+            (((1,), (1,)), ((), ())),
+            precision=lax.Precision.HIGHEST,
+            preferred_element_type=jnp.float32,
+        )
+        send[:8, : sides.shape[1]] = sides
+        for t in range(tracers):
+            keep[t * levels : (t + 1) * levels, :cols] = north[row_b] * adj[row_b, t]
+        for copy in fetch[3:]:
+            copy.wait()
+
+    @pl.when(polar)
+    def _():
+        for r in range(rows):
+            near = jnp.where(south, rows - 1 - r, r)
+            slot = lax.rem(near + rows - 1, rows)
+            for t in range(tracers):
+                move, _ = spread(r, t)
+                for h in (0, 1):
+                    part = slice(h * half_lev, (h + 1) * half_lev)
+                    where = jnp.where(own == h, 0, 1)
+                    wide_x[slot, where, t] = move[part]
+                    wide_x[slot, where, t, :, :cols] += transported(r, t)[part]
+        for copy in fetch[3:]:
+            copy.wait()
+        c, s = turned(dot3(wide_x[:2].reshape(4 * n_half, wide), fwd), turn, lon)
+        for slot in range(2):
+            spot = slice(slot * n_half, (slot + 1) * n_half)
+            first = slice(2 * slot * n_half, (2 * slot + 1) * n_half)
+            second = slice((2 * slot + 1) * n_half, (2 * slot + 2) * n_half)
+            keep[spot, :half], keep[spot, half:] = c[first], s[first]
+            send[spot, :half], send[spot, half:] = c[second], s[second]
+        third[...] = wide_x[2].reshape(tracers * levels, wide)
+        sign = jnp.where(south, -1.0, 1.0).astype(jnp.float32)
+        row_p = jnp.where(south, rows - 1, 0)
+        lane = lax.broadcasted_iota(jnp.int32, (half_lev, LANE), 1)
+        one, cos, sin = (pole[lon, k : k + 1] for k in range(3))
+        for t in range(tracers):
+            m = north[row_p] * adj[row_p, t] * sign
+            for k, target in ((0, keep), (1, send)):
+                u = wide_x[3, k, t]
+                flux[:half_lev, :cols] = jnp.where(own == k, m[:half_lev], m[half_lev:])
+                v = flux[:half_lev]
+                c0 = jnp.sum((u + v) * one, axis=1, keepdims=True)
+                c1 = jnp.sum((u - v) * cos, axis=1, keepdims=True)
+                s1 = jnp.sum((u - v) * sin, axis=1, keepdims=True)
+                at = KF % LANE
+                lanes = slice(half - LANE, half)
+                spot = slice(t * half_lev, (t + 1) * half_lev)
+                target[spot, lanes] = jnp.where(
+                    lane == at, c0, jnp.where(lane == at + 1, c1, jnp.where(lane == at + 2, s1, target[spot, lanes]))
+                )
+
+
+def third_kernel(lat_count, local, recv, passed, after, fwd, turn, keep, send, block):
+    tracers, levels, cols = recv.shape
+    south, polar, _ = latitude_role(lat_count)
+    lon, own, _ = longitude_role()
+    half_lev = levels // 2
+    n_half = tracers * half_lev
+    half = fwd.shape[-1] // 2
+
+    @pl.when(jnp.logical_not(polar))
+    def _():
+        keep[:8] = passed[:8]
+
+    @pl.when(polar)
+    def _():
+        sign = jnp.where(south, -1.0, 1.0).astype(jnp.float32)
+        block[...] = local[...]
+        for t in range(tracers):
+            m = recv[t] * sign
+            for k in (0, 1):
+                first = k * n_half + t * half_lev
+                block[first : first + half_lev, :cols] += jnp.where(own == k, m[:half_lev], m[half_lev:])
+        c, s = turned(dot3(block[...], fwd), turn, lon)
+        keep[:, :half], keep[:, half:] = c[:n_half], s[:n_half]
+        send[:, :half], send[:, half:] = c[n_half:], s[n_half:]
+
+
+def token_kernel(x, *rest):
+    rest[-1][...] = x[:8, :LANE]
+
+
+def sum_kernel(lat_count, mine, got, after, out):
+    _, polar, _ = latitude_role(lat_count)
+
+    @pl.when(polar)
+    def _():
+        out[...] = mine[...] + got[...]
+
+    @pl.when(jnp.logical_not(polar))
+    def _():
+        out[...] = mine[...]
+
+
+def total_kernel(lat_count, mine, across, third, third_across, after, out):
+    _, polar, _ = latitude_role(lat_count)
+    count = mine.shape[0]
+
+    @pl.when(polar)
+    def _():
+        out[:count] = mine[...] + across[...]
+        out[count:] = third[...] + third_across[...]
+
+
+def place(rows_ref, k, y, cols, half_lev):
+    y = y.reshape(2, -1, half_lev, y.shape[-1])
+    for h in (0, 1):
+        rows_ref[k, :, h * half_lev : (h + 1) * half_lev, :] = y[h][..., :cols]
+
+
+def finish_kernel(
+    lat_count, circle, cutoff, base, recv_a, recv_b, from_core, from_x, mine, other, bwd, turn, pole, out, rows_ref, sems,
+):
+    rows, tracers, levels, cols = base.shape
+    half_lev = levels // 2
+    n_half = tracers * half_lev
+    half = bwd.shape[1] // 2
+    south, polar, even = latitude_role(lat_count)
+    lon, own, right_core = longitude_role()
+
+    @pl.when(polar)
+    def _():
+        copies = []
+
+        def leave(k, row):
+            copies.append(pltpu.make_async_copy(rows_ref.at[k], out.at[row], sems.at[k]))
+            copies[-1].start()
+
+        first, second = mine[...], other[...]
+        near = own == 0
+        halves = jnp.where(near, first, second), jnp.where(near, second, first)
+        cos, sin = pole[lon, 1:2], pole[lon, 2:3]
+        at = KF % LANE
+        for t in range(tracers):
+            for h in (0, 1):
+                p = halves[h][t * half_lev : (t + 1) * half_lev, half - LANE : half]
+                c0, c1, s1 = p[:, at : at + 1], p[:, at + 1 : at + 2], p[:, at + 2 : at + 3]
+                y = (1.0 / circle) * c0 + (2.0 / circle) * (c1 * cos + s1 * sin)
+                rows_ref[3, t, h * half_lev : (h + 1) * half_lev, :] = y[:, :cols]
+        leave(3, jnp.where(south, rows - 1, 0))
+        places = [jnp.where(south, rows - 2 - slot, slot + 1) for slot in range(3)]
+        blocks = []
+        for slot, row in enumerate(places):
+            kept = jnp.where(south, cutoff[1, row], cutoff[0, row])
+            for h in (0, 1):
+                block = halves[h][slot * n_half : (slot + 1) * n_half]
+                blocks.append(weighted(block, kept, circle, turn, lon))
+        y = dot3(jnp.concatenate(blocks), bwd)
+        for slot, row in enumerate(places):
+            place(rows_ref, slot, y[2 * slot * n_half : 2 * (slot + 1) * n_half], cols, half_lev)
+            leave(slot, row)
+        for copy in copies:
+            copy.wait()
+
+    @pl.when(jnp.logical_not(polar))
+    def _():
+        row = lax.broadcasted_iota(jnp.int32, (8, LANE), 0)
+        lane = lax.broadcasted_iota(jnp.int32, (8, LANE), 1)
+        start = cols // LANE * LANE
+        low = jnp.where((row == 1) & (lane == 0), 1.0, 0.0).astype(jnp.float32)
+        high = jnp.where((row == 0) & (lane == cols - 1 - start), 1.0, 0.0).astype(jnp.float32)
+        dims = (((0,), (0,)), ((), ()))
+        exact = lax.Precision.HIGHEST
+        count = rows * tracers * levels
+        core_side, x_side = from_core[:8, :count], from_x[:8, :count]
+        left = jnp.where(right_core, x_side, core_side)
+        right = jnp.where(right_core, core_side, x_side)
+        first = lax.dot_general(left, low, dims, precision=exact, preferred_element_type=jnp.float32)
+        end = lax.dot_general(right, high, dims, precision=exact, preferred_element_type=jnp.float32)
+        shape = (rows, tracers, levels, LANE)
+        first, end = first.reshape(shape), end.reshape(shape)
+        side_a = recv_a[...]
+        side_b = recv_b[:, :cols].reshape(tracers, levels, cols)
+        copies = []
+        for r in range(rows):
+            value = base[r]
+            if r == rows - 1:
+                value = value + jnp.where(even, side_a, side_b)
+            if r == 0:
+                value = value - jnp.where(even, side_b, side_a)
+            rows_ref[r] = value
+            rows_ref[r, :, :, :LANE] -= first[r]
+            rows_ref[r, :, :, start:] += end[r][..., : cols - start]
+            copies.append(pltpu.make_async_copy(rows_ref.at[r], out.at[r], sems.at[r]))
+            copies[-1].start()
+        for copy in copies:
+            copy.wait()
+
+
+def fast_body(adj, east, north, cutoff):
+    lat_count, lon_count = lax.axis_size("lat"), lax.axis_size("lon")
+    rows, tracers, levels, cols = adj.shape
+    circle = cols * lon_count
+    fwd, bwd, turn, pole = tables(cols, circle, lon_count)
+    wide, width = fwd.shape[1:]
+    last = lat_count - 1
+    f32 = jnp.float32
+    params = pltpu.CompilerParams(vmem_limit_bytes=40 << 20)
+    dma = pltpu.SemaphoreType.DMA
+    vmem = pl.BlockSpec(memory_space=VMEM)
+    smem = pl.BlockSpec(memory_space=pltpu.SMEM)
+    anywhere = pl.BlockSpec(memory_space=pl.ANY)
+    far = pl.BlockSpec(memory_space=HBM)
+    n_half = tracers * levels // 2
+    pair, single = (2 * n_half, width), (n_half, width)
+
+    def put(x, space):
+        return pltpu.with_memory_space_constraint(x, space)
+
+    def call(kernel, outs, *args, scratch=(), cost=LIGHT):
+        return pl.pallas_call(
+            functools.partial(kernel, lat_count),
+            out_shape=[VMEM(s, f32) for s in outs],
+            in_specs=[vmem] * len(args),
+            out_specs=[vmem] * len(outs),
+            scratch_shapes=[VMEM(s, f32) for s in scratch],
+            compiler_params=params,
+            cost_estimate=cost,
+        )(*(put(x, VMEM) for x in args))
+
+    lats, lons = range(lat_count), range(lon_count)
+
+    def swap(x, pairs):
+        return lax.ppermute(x, ("lat", "lon"), [(a * lon_count + i, b * lon_count + j) for a, i, b, j in pairs])
+
+    by_core = [(a, i, a, i ^ 1) for a in lats for i in lons]
+    by_x = [(a, i, a, i ^ 2) for a in lats for i in lons]
+    by_lat = [(a, i, a ^ 1, i) for a in lats for i in lons]
+    mixed = [(a, i, a, i ^ 2) if a in (0, last) else (a, i, ((a + 1) ^ 1) - 1, i) for a in lats for i in lons]
+
+    edge = pl.pallas_call(
+        functools.partial(edge_kernel, lat_count),
+        out_shape=VMEM(adj.shape[1:], f32),
+        in_specs=[far] * 2,
+        out_specs=vmem,
+        scratch_shapes=[VMEM(adj.shape[1:], f32), VMEM(north.shape[1:], f32), dma((2,))],
+        compiler_params=params,
+    )(put(adj, HBM), put(north, HBM))
+    recv_a = swap(edge, by_lat)
+    base, keep, send, local, fwd, turn = pl.pallas_call(
+        functools.partial(local_kernel, lat_count),
+        out_shape=[VMEM(s, f32) for s in (adj.shape, pair, pair, (2 * n_half, wide))]
+        + [VMEM(fwd.shape, jnp.bfloat16), VMEM(turn.shape, f32)],
+        in_specs=[anywhere] + [far] * 6,
+        out_specs=[vmem] * 6,
+        scratch_shapes=[
+            VMEM(shape, f32)
+            for shape in (
+                adj.shape,
+                east.shape,
+                north.shape,
+                pole.shape,
+                (levels, wide),
+                (rows, 2, tracers, levels // 2, wide),
+                (rows, tracers, levels, LANE),
+            )
+        ]
+        + [dma((6,))],
+        compiler_params=params,
+        cost_estimate=LIGHT,
+    )(put(edge, VMEM), *(put(x, HBM) for x in (adj, east, north, fwd, turn, pole)))
+    got = swap(send, by_core)
+    def token(*args):
+        return pl.pallas_call(
+            token_kernel,
+            out_shape=VMEM((8, LANE), f32),
+            in_specs=[vmem] * len(args),
+            out_specs=vmem,
+            compiler_params=params,
+            cost_estimate=HEAVY,
+        )(*(put(x, VMEM) for x in args))
+
+    (part,) = call(sum_kernel, (pair,), keep, got, token(local))
+    across = swap(part, mixed)
+    keep3, send3 = call(third_kernel, (single, single), local, recv_a, got, part, fwd, turn, scratch=((2 * n_half, wide),))
+    got3 = swap(send3, by_core)
+    (part3,) = call(sum_kernel, (single,), keep3, got3, send3)
+    across3 = swap(part3, by_x)
+    (mine,) = call(total_kernel, ((3 * n_half, width),), part, across, part3, across3, token(part3, across))
+    other = swap(mine, by_core)
+    return pl.pallas_call(
+        functools.partial(finish_kernel, lat_count, circle),
+        out_shape=jax.ShapeDtypeStruct(adj.shape, f32),
+        in_specs=[smem] + [vmem] * 10,
+        out_specs=anywhere,
+        scratch_shapes=[VMEM(adj.shape, f32), dma((rows,))],
+        compiler_params=params,
+    )(cutoff, *(put(x, VMEM) for x in (base, recv_a, across, got, across3, mine, other, bwd, turn, pole)))
 
 
 full_precision = lax.Precision.HIGHEST
@@ -57,7 +500,7 @@
     return jnp.where(kept_mask, mode_weight, 0.0).astype(jnp.float32)
 
 
-def body(adj_next, east_courant, north_courant, cutoff):
+def general_body(adj_next, east_courant, north_courant, cutoff):
     lat_count = lax.axis_size("lat")
     lon_count = lax.axis_size("lon")
     lat_index = lax.axis_index("lat")
@@ -106,6 +549,14 @@
     return output
 
 
+def body(adj, east, north, cutoff):
+    lat_count, lon_count = lax.axis_size("lat"), lax.axis_size("lon")
+    one_band = cutoff.shape[1] == adj.shape[0] == 4
+    if one_band and lon_count == 4 and lat_count % 2 == 0 and lat_count >= 4 and adj.shape[2] % 16 == 0:
+        return fast_body(adj, east, north, cutoff)
+    return general_body(adj, east, north, cutoff)
+
+
 def solution(mesh):
     return jax.shard_map(
         body,

time: 91.6 us -> 23.8 us (0.26)
  waiting for transfers between devices: 34.8 us -> 10 us
  between operations: 14.3 us -> 0.1 us
  other arithmetic: 13.9 us -> 0 us
  blocking collectives: 9.16 us -> 0 us
  matrix products: 7.15 us -> 0 us
  Pallas kernels: 0 us -> 7.13 us
  starting transfers between devices: 9.99 us -> 6.38 us
  local copies, waits for them, and re-layouts: 2.14 us -> 0.02 us
    unnamed x2 -> x0, waiting for transfers between devices: 34.7 us -> none
    ppermute x5 -> x6, waiting for transfers between devices: 0.01 us -> 10 us  [swap(): lax.ppermute(x, ('lat', 'lon'), [(a * lon_count + i, b * lon_count + j) f...]
    all_gather x1 -> x0, blocking collectives: 9.16 us -> none  [body(): totals = lax.all_gather(level_share, 'lon', axis=2, tiled=True)]
    dot_general x2 -> x0, matrix products: 7.15 us -> none  [the longest x1 3.61 us: body(): jnp.einsum('acvk,nk->acvn', totals, local_table, precision=full_precision...]
    pallas_call x0 -> x9, Pallas kernels: none -> 7.13 us  [the longest x1 2.97 us: fast_body(): pl.pallas_call(functools.partial(local_kernel, lat_count), out_shape=[VME...]
    cos x1 -> x0, other arithmetic: 4.46 us -> none  [mode_table(): return jnp.concatenate([jnp.cos(phases), jnp.sin(phases)], axis=1)]
    ppermute x5 -> x6, starting transfers between devices: 9.99 us -> 6.38 us  [swap(): lax.ppermute(x, ('lat', 'lon'), [(a * lon_count + i, b * lon_count + j) f...]
    sub x1 -> x0, other arithmetic: 3.17 us -> none  [body(): result = result + lat_padded[2:] - lat_padded[:-2]]
  transfers between devices with their start and end apart: 6 -> 6, of which waited for: 1 -> 5; matrix products, arithmetic and copies ran while one was open for 13% -> 0% of each run, Pallas kernels for 0% -> 15%
where the time goes in v3:
time: 23.8 us; the launch traced here: 23.7 us
  waiting for transfers between devices  10 us (42%)
  Pallas kernels  7.13 us (30%)
  starting transfers between devices  6.38 us (27%)
    ppermute x6, waiting for transfers between devices, swap(): lax.ppermute(x, ('lat', 'lon'), [(a * lon_count + i, b * lon_count + j) f...  10 us
    ppermute x6, starting transfers between devices, swap(): lax.ppermute(x, ('lat', 'lon'), [(a * lon_count + i, b * lon_count + j) f...  6.38 us
    pallas_call x1, Pallas kernels, fast_body(): pl.pallas_call(functools.partial(local_kernel, lat_count), out_shape=[VME...  2.97 us
    pallas_call x1, Pallas kernels, fast_body(): pl.pallas_call(functools.partial(finish_kernel, lat_count, circle), out_s...  2.54 us
    pallas_call x1, Pallas kernels, fast_body(): pl.pallas_call(functools.partial(edge_kernel, lat_count), out_shape=VMEM(...  0.98 us
    pallas_call x4, Pallas kernels, call(): pl.pallas_call(functools.partial(kernel, lat_count), out_shape=[VMEM(s, f...  0.63 us
  transfers between devices with their start and end apart: 6, of which 5 were waited for; matrix products, arithmetic and copies ran while one was open for 0% of the time, Pallas kernels for 15%

profile of v3, /device:TPU:0, one launch (start us, length us, event | category | flops | bytes accessed | tf_op | source)
XLA Modules:
  0.0 23.7 jit_solution(10319156310506097340)
XLA Ops:
  0.0 1.0 %shard_map.82.after = f32[5,16,720]{2,1,0:T(8,128)S(1)} custom-call(f32[4,5,16,720]{3,2,1,0:T(8,128)} %adj_hbm.3, f32[4,16,720]{2,1,0:T(8,128)} %north_hbm.3), custom_call_target="tpu_custom_call" | custom-call | tf_op jit(solution)/shard_map/pallas_call | solution.py:394
  1.0 3.0 %collective-permute-start = (f32[5,16,720]{2,1,0:T(8,128)S(1)}, f32[5,16,720]{2,1,0:T(8,128)S(1)}, u32[]{:S(2)}, u32[]{:S(2)}) collective-permute-start(f32[5,16,720]{2,1,0:T(8,128)S(1)} %shard_map.82.after), channel_id=1, source_target_pairs={{0,4},{1,5},{2,6},{3,7},{4,0},{5,1},{6,2},{7,3},{8,12},{9,13},{10,... | collective-permute-start | bytes 691208 | tf_op jit(solution)/shard_map/ppermute | solution.py:387
  4.0 3.0 %shard_map.83 = (f32[4,5,16,720]{3,2,1,0:T(8,128)S(1)}, f32[80,768]{1,0:T(8,128)S(1)}, f32[80,768]{1,0:T(8,128)S(1)}, f32[80,768]{1,0:T(8,128)S(1)}, bf16[2,768,...) custom-call(f32[5,16,720]{2,1,0:T(8,128)S(1)} %shard_map.82.after, f32[4,5,16,720]{3,2,1,0:T(8,128)} %adj_hbm.3, ...), custom_call_target="tpu_custom_call" | custom-call | bytes 1000 | tf_op jit(solution)/shard_map/pallas_call | solution.py:403
  7.0 0.1 collective-permute-start.1
  7.1 1.5 %collective-permute-done.1.got.passed.from_core = f32[80,768]{1,0:T(8,128)S(1)} collective-permute-done((f32[80,768]{1,0:T(8,128)S(1)}, f32[80,768]{1,0:T(8,128)S(1)}, u32[]{:S(2)}, u32[]{:S(2)}) %collective-permute-start.1) | collective-permute-done | bytes 245792 | tf_op jit(solution)/shard_map/ppermute | solution.py:387
  8.6 1.6 %collective-permute-start.2 = (f32[80,768]{1,0:T(8,128)S(1)}, f32[80,768]{1,0:T(8,128)S(1)}, u32[]{:S(2)}, u32[]{:S(2)}) collective-permute-start(f32[80,768]{1,0:T(8,128)S(1)} %shard_map.85.after.mine), channel_id=1, source_target_pairs={{0,2},{1,3},{2,0},{3,1},{4,8},{5,9},{6,10},{7,11},{8,4},{9,5},{10,... | collective-permute-start | bytes 737288 | tf_op jit(solution)/shard_map/ppermute | solution.py:387
  10.2 0.0 collective-permute-done.recv.recv_a
  10.2 0.5 %shard_map.86 = (f32[40,768]{1,0:T(8,128)S(1)}, f32[40,768]{1,0:T(8,128)S(1)}) custom-call(f32[80,768]{1,0:T(8,128)S(1)} %get-tuple-element.16.x.local, f32[5,16,720]{2,1,0:T(8,128)S(1)} %collective-permute-done.recv.recv_a, f32[80,768]{1,0:T(8,128)S(1)} %collective-permute-done.1.got.passed.from_core, f32[80,768]{1,0:T(8,128)S(1)} %shard_map.85.after.mine, ...), custom_call_target="tpu_custom_call" | custom-call | bytes 1000 | tf_op jit(solution)/shard_map/pallas_call | solution.py:374
  10.7 0.1 collective-permute-start.3
  10.8 1.3 %collective-permute-done.3.got = f32[40,768]{1,0:T(8,128)S(1)} collective-permute-done((f32[40,768]{1,0:T(8,128)S(1)}, f32[40,768]{1,0:T(8,128)S(1)}, u32[]{:S(2)}, u32[]{:S(2)}) %collective-permute-start.3) | collective-permute-done | bytes 122912 | tf_op jit(solution)/shard_map/ppermute | solution.py:387
  12.2 0.0 copy-start.1
  12.2 0.0 copy-start.2
  12.2 1.6 %collective-permute-start.4 = (f32[40,768]{1,0:T(8,128)S(1)}, f32[40,768]{1,0:T(8,128)S(1)}, u32[]{:S(2)}, u32[]{:S(2)}) collective-permute-start(f32[40,768]{1,0:T(8,128)S(1)} %shard_map.87.x.third), channel_id=1, source_target_pairs={{0,2},{1,3},{2,0},{3,1},{4,6},{5,7},{6,4},{7,5},{8,10},{9,11},{10,... | collective-permute-start | bytes 368648 | tf_op jit(solution)/shard_map/ppermute | solution.py:387
  13.7 3.7 %collective-permute-done.2.rest_0_.across.recv_b = f32[80,768]{1,0:T(8,128)S(1)} collective-permute-done((f32[80,768]{1,0:T(8,128)S(1)}, f32[80,768]{1,0:T(8,128)S(1)}, u32[]{:S(2)}, u32[]{:S(2)}) %collective-permute-start.2) | collective-permute-done | bytes 245792 | tf_op jit(solution)/shard_map/ppermute | solution.py:387
  17.5 0.0 copy-start
  17.5 1.8 %collective-permute-done.4.third_across.from_x = f32[40,768]{1,0:T(8,128)S(1)} collective-permute-done((f32[40,768]{1,0:T(8,128)S(1)}, f32[40,768]{1,0:T(8,128)S(1)}, u32[]{:S(2)}, u32[]{:S(2)}) %collective-permute-start.4) | collective-permute-done | bytes 122912 | tf_op jit(solution)/shard_map/ppermute | solution.py:387
  19.4 0.1 collective-permute-start.5
  19.4 1.7 %collective-permute-done.5.other = f32[120,768]{1,0:T(8,128)S(1)} collective-permute-done((f32[120,768]{1,0:T(8,128)S(1)}, f32[120,768]{1,0:T(8,128)S(1)}, u32[]{:S(2)}, u32[]{:S(2)}) %collective-permute-start.5) | collective-permute-done | bytes 368672 | tf_op jit(solution)/shard_map/ppermute | solution.py:387
  21.1 0.0 copy-done.1
  21.1 0.0 copy-done.2
  21.1 0.0 copy-done
  21.1 2.5 %shard_map.90 = f32[4,5,16,720]{3,2,1,0:T(8,128)} custom-call(s32[2,4]{1,0:T(2,128)S(1)} %copy-done.2, f32[4,5,16,720]{3,2,1,0:T(8,128)S(1)} %get-tuple-element.13.base, f32[5,16,720]{2,1,0:T(8,128)S(1)} %collective-permute-done.recv.recv_a, f32[80,768]{1,0:T(8,128)S(1)} %collective-permute-done.2.rest_0_.across.recv_b, ...), custom_call_target="tpu_custom_call" | custom-call | tf_op jit(solution)/shard_map/pallas_call | solution.py:444
  (5 shorter events, 0.1 us)
Async XLA Ops:
  1.0 9.2 %collective-permute-start = (f32[5,16,720]{2,1,0:T(8,128)S(1)}, f32[5,16,720]{2,1,0:T(8,128)S(1)}, u32[]{:S(2)}, u32[]{:S(2)}) collective-permute-start(f32[5,16,720]{2,1,0:T(8,128)S(1)} %shard_map.82.after), channel_id=1, source_target_pairs={{0,4},{1,5},{2,6},{3,7},{4,0},{5,1},{6,2},{7,3},{8,12},{9,13},{10,... | collective-permute-start | bytes 691208 | tf_op jit(solution)/shard_map/ppermute | solution.py:387
  7.0 1.6 %collective-permute-start.1 = (f32[80,768]{1,0:T(8,128)S(1)}, f32[80,768]{1,0:T(8,128)S(1)}, u32[]{:S(2)}, u32[]{:S(2)}) collective-permute-start(f32[80,768]{1,0:T(8,128)S(1)} %get-tuple-element.15), channel_id=1, source_target_pairs={{0,1},{1,0},{2,3},{3,2},{4,5},{5,4},{6,7},{7,6},{8,9},{9,8},{10,11... | collective-permute-start | bytes 737288 | tf_op jit(solution)/shard_map/ppermute | solution.py:387
  8.6 8.9 %collective-permute-start.2 = (f32[80,768]{1,0:T(8,128)S(1)}, f32[80,768]{1,0:T(8,128)S(1)}, u32[]{:S(2)}, u32[]{:S(2)}) collective-permute-start(f32[80,768]{1,0:T(8,128)S(1)} %shard_map.85.after.mine), channel_id=1, source_target_pairs={{0,2},{1,3},{2,0},{3,1},{4,8},{5,9},{6,10},{7,11},{8,4},{9,5},{10,... | collective-permute-start | bytes 737288 | tf_op jit(solution)/shard_map/ppermute | solution.py:387
  10.7 1.4 %collective-permute-start.3 = (f32[40,768]{1,0:T(8,128)S(1)}, f32[40,768]{1,0:T(8,128)S(1)}, u32[]{:S(2)}, u32[]{:S(2)}) collective-permute-start(f32[40,768]{1,0:T(8,128)S(1)} %get-tuple-element.20.after), channel_id=1, source_target_pairs={{0,1},{1,0},{2,3},{3,2},{4,5},{5,4},{6,7},{7,6},{8,9},{9,8},{10,11... | collective-permute-start | bytes 368648 | tf_op jit(solution)/shard_map/ppermute | solution.py:387
  12.2 9.0 %copy-start.1 = (f32[4,4,768]{2,1,0:T(4,128)S(1)}, f32[4,4,768]{2,1,0:T(4,128)}, u32[]{:S(2)}) copy-start(f32[4,4,768]{2,1,0:T(4,128)} %constant.10.clone.pole_hbm.pole) | copy-start | bytes 147460
  12.2 9.0 %copy-start.2 = (s32[2,4]{1,0:T(2,128)S(1)}, s32[2,4]{1,0:T(2,128)}, u32[]{:S(2)}) copy-start(s32[2,4]{1,0:T(2,128)} %cutoff.1) | copy-start | bytes 100
  12.2 7.1 %collective-permute-start.4 = (f32[40,768]{1,0:T(8,128)S(1)}, f32[40,768]{1,0:T(8,128)S(1)}, u32[]{:S(2)}, u32[]{:S(2)}) collective-permute-start(f32[40,768]{1,0:T(8,128)S(1)} %shard_map.87.x.third), channel_id=1, source_target_pairs={{0,2},{1,3},{2,0},{3,1},{4,6},{5,7},{6,4},{7,5},{8,10},{9,11},{10,... | collective-permute-start | bytes 368648 | tf_op jit(solution)/shard_map/ppermute | solution.py:387
  17.5 3.6 %copy-start = (bf16[2,768,768]{2,1,0:T(8,128)(2,1)S(1)}, bf16[2,768,768]{2,1,0:T(8,128)(2,1)}, u32[]{:S(2)}) copy-start(bf16[2,768,768]{2,1,0:T(8,128)(2,1)} %constant.11.clone.bwd) | copy-start | bytes 7077892
  19.4 1.8 %collective-permute-start.5 = (f32[120,768]{1,0:T(8,128)S(1)}, f32[120,768]{1,0:T(8,128)S(1)}, u32[]{:S(2)}, u32[]{:S(2)}) collective-permute-start(f32[120,768]{1,0:T(8,128)S(1)} %shard_map.89.mine), channel_id=1, source_target_pairs={{0,1},{1,0},{2,3},{3,2},{4,5},{5,4},{6,7},{7,6},{8,9},{9,8},{10,11... | collective-permute-start | bytes 1105928 | tf_op jit(solution)/shard_map/ppermute | solution.py:387

commit v4 on v3

--- a/solution.py
+++ b/solution.py
@@ -108,19 +108,8 @@
 
 
 def local_kernel(
-    lat_count, after, adj_hbm, east_hbm, north_hbm, fwd_hbm, turn_hbm, pole_hbm, base, keep, send, third, fwd, turn,
-    adj, east, north, pole, flux, wide_x, ends, sems,
+    lat_count, after, adj, east, north, fwd, turn, pole, base, edge, keep, send, third, flux, wide_x, ends
 ):
-    fetch = [
-        pltpu.make_async_copy(source, target, sems.at[n])
-        for n, (source, target) in enumerate(
-            ((adj_hbm, adj), (east_hbm, east), (north_hbm, north), (turn_hbm, turn), (pole_hbm, pole), (fwd_hbm, fwd))
-        )
-    ]
-    for copy in fetch:
-        copy.start()
-    for copy in fetch[:3]:
-        copy.wait()
     rows, tracers, levels, cols = adj.shape
     wide = flux.shape[-1]
     south, polar, even = latitude_role(lat_count)
@@ -165,10 +154,7 @@
             preferred_element_type=jnp.float32,
         )
         send[:8, : sides.shape[1]] = sides
-        for t in range(tracers):
-            keep[t * levels : (t + 1) * levels, :cols] = north[row_b] * adj[row_b, t]
-        for copy in fetch[3:]:
-            copy.wait()
+        edge[...] = north[row_b][None] * adj[row_b]
 
     @pl.when(polar)
     def _():
@@ -182,8 +168,6 @@
                     where = jnp.where(own == h, 0, 1)
                     wide_x[slot, where, t] = move[part]
                     wide_x[slot, where, t, :, :cols] += transported(r, t)[part]
-        for copy in fetch[3:]:
-            copy.wait()
         c, s = turned(dot3(wide_x[:2].reshape(4 * n_half, wide), fwd), turn, lon)
         for slot in range(2):
             spot = slice(slot * n_half, (slot + 1) * n_half)
@@ -213,17 +197,13 @@
                 )
 
 
-def third_kernel(lat_count, local, recv, passed, after, fwd, turn, keep, send, block):
+def third_kernel(lat_count, local, recv, after, fwd, turn, keep, send, block):
     tracers, levels, cols = recv.shape
     south, polar, _ = latitude_role(lat_count)
     lon, own, _ = longitude_role()
     half_lev = levels // 2
     n_half = tracers * half_lev
     half = fwd.shape[-1] // 2
-
-    @pl.when(jnp.logical_not(polar))
-    def _():
-        keep[:8] = passed[:8]
 
     @pl.when(polar)
     def _():
@@ -252,17 +232,15 @@
 
     @pl.when(jnp.logical_not(polar))
     def _():
-        out[...] = mine[...]
-
-
-def total_kernel(lat_count, mine, across, third, third_across, after, out):
+        out[:8] = got[:8]
+
+
+def total_kernel(lat_count, mine, across, after, out):
     _, polar, _ = latitude_role(lat_count)
-    count = mine.shape[0]
 
     @pl.when(polar)
     def _():
-        out[:count] = mine[...] + across[...]
-        out[count:] = third[...] + third_across[...]
+        out[...] = mine[...] + across[...]
 
 
 def place(rows_ref, k, y, cols, half_lev):
@@ -271,27 +249,24 @@
         rows_ref[k, :, h * half_lev : (h + 1) * half_lev, :] = y[h][..., :cols]
 
 
-def finish_kernel(
-    lat_count, circle, cutoff, base, recv_a, recv_b, from_core, from_x, mine, other, bwd, turn, pole, out, rows_ref, sems,
-):
-    rows, tracers, levels, cols = base.shape
+def halves_of(mine, other, own):
+    first, second = mine[...], other[...]
+    near = own == 0
+    return jnp.where(near, first, second), jnp.where(near, second, first)
+
+
+def cap_kernel(lat_count, circle, cutoff, mine, other, bwd, turn, pole, out):
+    _, tracers, levels, cols = out.shape
     half_lev = levels // 2
     n_half = tracers * half_lev
     half = bwd.shape[1] // 2
-    south, polar, even = latitude_role(lat_count)
-    lon, own, right_core = longitude_role()
+    rows = cutoff.shape[1]
+    south, polar, _ = latitude_role(lat_count)
+    lon, own, _ = longitude_role()
 
     @pl.when(polar)
     def _():
-        copies = []
-
-        def leave(k, row):
-            copies.append(pltpu.make_async_copy(rows_ref.at[k], out.at[row], sems.at[k]))
-            copies[-1].start()
-
-        first, second = mine[...], other[...]
-        near = own == 0
-        halves = jnp.where(near, first, second), jnp.where(near, second, first)
+        halves = halves_of(mine, other, own)
         cos, sin = pole[lon, 1:2], pole[lon, 2:3]
         at = KF % LANE
         for t in range(tracers):
@@ -299,19 +274,40 @@
                 p = halves[h][t * half_lev : (t + 1) * half_lev, half - LANE : half]
                 c0, c1, s1 = p[:, at : at + 1], p[:, at + 1 : at + 2], p[:, at + 2 : at + 3]
                 y = (1.0 / circle) * c0 + (2.0 / circle) * (c1 * cos + s1 * sin)
-                rows_ref[3, t, h * half_lev : (h + 1) * half_lev, :] = y[:, :cols]
-        leave(3, jnp.where(south, rows - 1, 0))
-        places = [jnp.where(south, rows - 2 - slot, slot + 1) for slot in range(3)]
+                out[0, t, h * half_lev : (h + 1) * half_lev, :] = y[:, :cols]
         blocks = []
-        for slot, row in enumerate(places):
+        for slot in range(2):
+            row = jnp.where(south, rows - 2 - slot, slot + 1)
             kept = jnp.where(south, cutoff[1, row], cutoff[0, row])
             for h in (0, 1):
                 block = halves[h][slot * n_half : (slot + 1) * n_half]
                 blocks.append(weighted(block, kept, circle, turn, lon))
         y = dot3(jnp.concatenate(blocks), bwd)
-        for slot, row in enumerate(places):
-            place(rows_ref, slot, y[2 * slot * n_half : 2 * (slot + 1) * n_half], cols, half_lev)
-            leave(slot, row)
+        for slot in range(2):
+            place(out, slot + 1, y[2 * slot * n_half : 2 * (slot + 1) * n_half], cols, half_lev)
+
+
+def finish_kernel(
+    lat_count, circle, cutoff, caps, base, recv_a, recv_b, from_core, from_x, mine, other, bwd, turn, out, rows_ref, sems,
+):
+    rows, tracers, levels, cols = base.shape
+    half_lev = levels // 2
+    south, polar, even = latitude_role(lat_count)
+    lon, own, right_core = longitude_role()
+
+    @pl.when(polar)
+    def _():
+        copies = []
+        for near in range(rows - 1):
+            row = jnp.where(south, rows - 1 - near, near)
+            copies.append(pltpu.make_async_copy(caps.at[near], out.at[row], sems.at[near]))
+            copies[-1].start()
+        row = jnp.where(south, 0, rows - 1)
+        kept = jnp.where(south, cutoff[1, row], cutoff[0, row])
+        blocks = [weighted(block, kept, circle, turn, lon) for block in halves_of(mine, other, own)]
+        place(rows_ref, 0, dot3(jnp.concatenate(blocks), bwd), cols, half_lev)
+        copies.append(pltpu.make_async_copy(rows_ref.at[0], out.at[row], sems.at[rows - 1]))
+        copies[-1].start()
         for copy in copies:
             copy.wait()
 
@@ -333,7 +329,7 @@
         shape = (rows, tracers, levels, LANE)
         first, end = first.reshape(shape), end.reshape(shape)
         side_a = recv_a[...]
-        side_b = recv_b[:, :cols].reshape(tracers, levels, cols)
+        side_b = recv_b[...]
         copies = []
         for r in range(rows):
             value = base[r]
@@ -389,7 +385,7 @@
     by_core = [(a, i, a, i ^ 1) for a in lats for i in lons]
     by_x = [(a, i, a, i ^ 2) for a in lats for i in lons]
     by_lat = [(a, i, a ^ 1, i) for a in lats for i in lons]
-    mixed = [(a, i, a, i ^ 2) if a in (0, last) else (a, i, ((a + 1) ^ 1) - 1, i) for a in lats for i in lons]
+    by_next = [(a, i, ((a + 1) ^ 1) - 1, i) for a in range(1, last) for i in lons]
 
     edge = pl.pallas_call(
         functools.partial(edge_kernel, lat_count),
@@ -397,31 +393,22 @@
         in_specs=[far] * 2,
         out_specs=vmem,
         scratch_shapes=[VMEM(adj.shape[1:], f32), VMEM(north.shape[1:], f32), dma((2,))],
+        cost_estimate=HEAVY,
         compiler_params=params,
     )(put(adj, HBM), put(north, HBM))
     recv_a = swap(edge, by_lat)
-    base, keep, send, local, fwd, turn = pl.pallas_call(
-        functools.partial(local_kernel, lat_count),
-        out_shape=[VMEM(s, f32) for s in (adj.shape, pair, pair, (2 * n_half, wide))]
-        + [VMEM(fwd.shape, jnp.bfloat16), VMEM(turn.shape, f32)],
-        in_specs=[anywhere] + [far] * 6,
-        out_specs=[vmem] * 6,
-        scratch_shapes=[
-            VMEM(shape, f32)
-            for shape in (
-                adj.shape,
-                east.shape,
-                north.shape,
-                pole.shape,
-                (levels, wide),
-                (rows, 2, tracers, levels // 2, wide),
-                (rows, tracers, levels, LANE),
-            )
-        ]
-        + [dma((6,))],
-        compiler_params=params,
-        cost_estimate=LIGHT,
-    )(put(edge, VMEM), *(put(x, HBM) for x in (adj, east, north, fwd, turn, pole)))
+    base, edge_b, keep, send, local = call(
+        local_kernel,
+        (adj.shape, adj.shape[1:], pair, pair, (2 * n_half, wide)),
+        edge,
+        adj,
+        east,
+        north,
+        fwd,
+        turn,
+        pole,
+        scratch=((levels, wide), (rows, 2, tracers, levels // 2, wide), (rows, tracers, levels, LANE)),
+    )
     got = swap(send, by_core)
     def token(*args):
         return pl.pallas_call(
@@ -434,13 +421,23 @@
         )(*(put(x, VMEM) for x in args))
 
     (part,) = call(sum_kernel, (pair,), keep, got, token(local))
-    across = swap(part, mixed)
-    keep3, send3 = call(third_kernel, (single, single), local, recv_a, got, part, fwd, turn, scratch=((2 * n_half, wide),))
+    across = swap(part, by_x)
+    recv_b = swap(edge_b, by_next)
+    keep3, send3 = call(third_kernel, (single, single), local, recv_a, part, fwd, turn, scratch=((2 * n_half, wide),))
     got3 = swap(send3, by_core)
     (part3,) = call(sum_kernel, (single,), keep3, got3, send3)
     across3 = swap(part3, by_x)
-    (mine,) = call(total_kernel, ((3 * n_half, width),), part, across, part3, across3, token(part3, across))
+    (mine,) = call(total_kernel, (pair,), part, across, part3)
     other = swap(mine, by_core)
+    (mine3,) = call(total_kernel, (single,), part3, across3, token(part3, across, recv_b))
+    other3 = swap(mine3, by_core)
+    caps = pl.pallas_call(
+        functools.partial(cap_kernel, lat_count, circle),
+        out_shape=VMEM((3,) + adj.shape[1:], f32),
+        in_specs=[smem] + [vmem] * 5,
+        out_specs=vmem,
+        compiler_params=params,
+    )(cutoff, *(put(x, VMEM) for x in (mine, other, bwd, turn, pole)))
     return pl.pallas_call(
         functools.partial(finish_kernel, lat_count, circle),
         out_shape=jax.ShapeDtypeStruct(adj.shape, f32),
@@ -448,7 +445,7 @@
         out_specs=anywhere,
         scratch_shapes=[VMEM(adj.shape, f32), dma((rows,))],
         compiler_params=params,
-    )(cutoff, *(put(x, VMEM) for x in (base, recv_a, across, got, across3, mine, other, bwd, turn, pole)))
+    )(cutoff, *(put(x, VMEM) for x in (caps, base, recv_a, recv_b, got, across, mine3, other3, bwd, turn)))
 
 
 full_precision = lax.Precision.HIGHEST

time: 23.8 us -> 21.6 us (0.908)
  waiting for transfers between devices: 10 us -> 7.36 us
  starting transfers between devices: 6.38 us -> 7.33 us
  Pallas kernels: 7.13 us -> 6.5 us
    ppermute x6 -> x8, waiting for transfers between devices: 10 us -> 7.36 us  [swap(): lax.ppermute(x, ('lat', 'lon'), [(a * lon_count + i, b * lon_count + j) f...]
    pallas_call x1, Pallas kernels: 2.97 us -> 1.32 us  [fast_body(): pl.pallas_call(functools.partial(cap_kernel, lat_count, circle), out_shap...]
    pallas_call x4 -> x6, Pallas kernels: 0.63 us -> 2.1 us  [call(): pl.pallas_call(functools.partial(kernel, lat_count), out_shape=[VMEM(s, f...]
    ppermute x6 -> x8, starting transfers between devices: 6.38 us -> 7.33 us  [swap(): lax.ppermute(x, ('lat', 'lon'), [(a * lon_count + i, b * lon_count + j) f...]
    pallas_call x1, Pallas kernels: 2.54 us -> 1.93 us  [fast_body(): pl.pallas_call(functools.partial(finish_kernel, lat_count, circle), out_s...]
  transfers between devices with their start and end apart: 6 -> 8, of which waited for: 5 -> 5; matrix products, arithmetic and copies ran while one was open for 0% -> 0% of each run, Pallas kernels for 15% -> 16%
where the time goes in v4:
time: 21.6 us; the launch traced here: 21.5 us
  waiting for transfers between devices  7.36 us (34%)
  starting transfers between devices  7.33 us (34%)
  Pallas kernels  6.5 us (30%)
    ppermute x8, waiting for transfers between devices, swap(): lax.ppermute(x, ('lat', 'lon'), [(a * lon_count + i, b * lon_count + j) f...  7.36 us
    ppermute x8, starting transfers between devices, swap(): lax.ppermute(x, ('lat', 'lon'), [(a * lon_count + i, b * lon_count + j) f...  7.33 us
    pallas_call x6, Pallas kernels, call(): pl.pallas_call(functools.partial(kernel, lat_count), out_shape=[VMEM(s, f...  2.1 us
    pallas_call x1, Pallas kernels, fast_body(): pl.pallas_call(functools.partial(finish_kernel, lat_count, circle), out_s...  1.93 us
    pallas_call x1, Pallas kernels, fast_body(): pl.pallas_call(functools.partial(cap_kernel, lat_count, circle), out_shap...  1.32 us
    pallas_call x1, Pallas kernels, fast_body(): pl.pallas_call(functools.partial(edge_kernel, lat_count), out_shape=VMEM(...  1.15 us
  transfers between devices with their start and end apart: 8, of which 5 were waited for; matrix products, arithmetic and copies ran while one was open for 0% of the time, Pallas kernels for 16%

profile of v4, /device:TPU:0, one launch (start us, length us, event | category | flops | bytes accessed | tf_op | source)
XLA Modules:
  0.0 21.5 jit_solution(4783239781687417742)
XLA Ops:
  0.0 0.0 copy-start.1
  0.0 0.0 copy-start.3
  0.0 0.0 copy-start.5
  0.0 0.0 copy-start.6
  0.0 0.0 copy-start.2
  0.0 0.0 copy-start.7
  0.0 1.1 %shard_map.82.after = f32[5,16,720]{2,1,0:T(8,128)S(1)} custom-call(f32[4,5,16,720]{3,2,1,0:T(8,128)} %adj.1, f32[4,16,720]{2,1,0:T(8,128)} %north.1), custom_call_target="tpu_custom_call" | custom-call | flops 137438953472 | tf_op jit(solution)/shard_map/pallas_call | solution.py:390
  1.2 3.0 %collective-permute-start.2 = (f32[5,16,720]{2,1,0:T(8,128)S(1)}, f32[5,16,720]{2,1,0:T(8,128)S(1)}, u32[]{:S(2)}, u32[]{:S(2)}) collective-permute-start(f32[5,16,720]{2,1,0:T(8,128)S(1)} %shard_map.82.after), channel_id=1, source_target_pairs={{0,4},{1,5},{2,6},{3,7},{4,0},{5,1},{6,2},{7,3},{8,12},{9,13},{10,... | collective-permute-start | bytes 691208 | tf_op jit(solution)/shard_map/ppermute | solution.py:383
  4.2 0.0 copy-done.1
  4.2 0.0 copy-done.3
  4.2 0.0 copy-done.5
  4.2 0.0 copy-done.6
  4.2 0.0 copy-done.2
  4.3 0.0 copy-done.7
  4.3 1.5 %shard_map.83 = (f32[4,5,16,720]{3,2,1,0:T(8,128)S(1)}, f32[5,16,720]{2,1,0:T(8,128)S(1)}, f32[80,768]{1,0:T(8,128)S(1)}, f32[80,768]{1,0:T(8,128)S(1)}, f32[80,768]{1,0:T(8,128)S(1)}) custom-call(f32[5,16,720]{2,1,0:T(8,128)S(1)} %shard_map.82.after, f32[4,5,16,720]{3,2,1,0:T(8,128)S(1)} %copy-done.2, f32[4,16,720]{2,1,0:T(8,128)S(1)} %copy-done.7, ...), custom_call_target="tpu_custom_call" | custom-call | bytes 1000 | tf_op jit(solution)/shard_map/pallas_call | solution.py:370
  5.7 0.1 collective-permute-start
  5.8 1.5 %collective-permute-done.got.from_core = f32[80,768]{1,0:T(8,128)S(1)} collective-permute-done((f32[80,768]{1,0:T(8,128)S(1)}, f32[80,768]{1,0:T(8,128)S(1)}, u32[]{:S(2)}, u32[]{:S(2)}) %collective-permute-start) | collective-permute-done | bytes 245792 | tf_op jit(solution)/shard_map/ppermute | solution.py:383
  7.3 1.6 %collective-permute-start.1 = (f32[80,768]{1,0:T(8,128)S(1)}, f32[80,768]{1,0:T(8,128)S(1)}, u32[]{:S(2)}, u32[]{:S(2)}) collective-permute-start(f32[80,768]{1,0:T(8,128)S(1)} %shard_map.85.after.mine), channel_id=1, source_target_pairs={{0,2},{1,3},{2,0},{3,1},{4,6},{5,7},{6,4},{7,5},{8,10},{9,11},{10,... | collective-permute-start | bytes 737288 | tf_op jit(solution)/shard_map/ppermute | solution.py:383
  8.9 0.7 %collective-permute-start.5 = (f32[5,16,720]{2,1,0:T(8,128)S(1)}, f32[5,16,720]{2,1,0:T(8,128)S(1)}, u32[]{:S(2)}, u32[]{:S(2)}) collective-permute-start(f32[5,16,720]{2,1,0:T(8,128)S(1)} %get-tuple-element.18), channel_id=1, source_target_pairs={{4,8},{5,9},{6,10},{7,11},{8,4},{9,5},{10,6},{11,7},{12,16},{13,17... | collective-permute-start | bytes 691208 | tf_op jit(solution)/shard_map/ppermute | solution.py:383
  9.6 0.6 %collective-permute-done.2.recv.recv_a = f32[5,16,720]{2,1,0:T(8,128)S(1)} collective-permute-done((f32[5,16,720]{2,1,0:T(8,128)S(1)}, f32[5,16,720]{2,1,0:T(8,128)S(1)}, u32[]{:S(2)}, u32[]{:S(2)}) %collective-permute-start.2) | collective-permute-done | bytes 230432 | tf_op jit(solution)/shard_map/ppermute | solution.py:383
  10.2 0.5 %shard_map.86 = (f32[40,768]{1,0:T(8,128)S(1)}, f32[40,768]{1,0:T(8,128)S(1)}) custom-call(f32[80,768]{1,0:T(8,128)S(1)} %get-tuple-element.14.x.local, f32[5,16,720]{2,1,0:T(8,128)S(1)} %collective-permute-done.2.recv.recv_a, f32[80,768]{1,0:T(8,128)S(1)} %shard_map.85.after.mine, bf16[2,768,768]{2,1,0:T(8,128)(2,1)S(1)} %copy-done.1, ...), custom_call_target="tpu_custom_call" | custom-call | bytes 1000 | tf_op jit(solution)/shard_map/pallas_call | solution.py:370
  10.7 0.1 collective-permute-start.3
  10.8 1.3 %collective-permute-done.3.got = f32[40,768]{1,0:T(8,128)S(1)} collective-permute-done((f32[40,768]{1,0:T(8,128)S(1)}, f32[40,768]{1,0:T(8,128)S(1)}, u32[]{:S(2)}, u32[]{:S(2)}) %collective-permute-start.3) | collective-permute-done | bytes 122912 | tf_op jit(solution)/shard_map/ppermute | solution.py:383
  12.1 1.8 %collective-permute-start.6 = (f32[40,768]{1,0:T(8,128)S(1)}, f32[40,768]{1,0:T(8,128)S(1)}, u32[]{:S(2)}, u32[]{:S(2)}) collective-permute-start(f32[40,768]{1,0:T(8,128)S(1)} %shard_map.87.after.x.mine), channel_id=1, source_target_pairs={{0,2},{1,3},{2,0},{3,1},{4,6},{5,7},{6,4},{7,5},{8,10},{9,11},{10,... | collective-permute-start | bytes 368648 | tf_op jit(solution)/shard_map/ppermute | solution.py:383
  13.9 1.9 %collective-permute-done.1.across.rest_0_.from_x = f32[80,768]{1,0:T(8,128)S(1)} collective-permute-done((f32[80,768]{1,0:T(8,128)S(1)}, f32[80,768]{1,0:T(8,128)S(1)}, u32[]{:S(2)}, u32[]{:S(2)}) %collective-permute-start.1) | collective-permute-done | bytes 245792 | tf_op jit(solution)/shard_map/ppermute | solution.py:383
  15.8 0.0 copy-start
  15.8 0.0 copy-start.4
  15.9 0.0 copy-start.8
  15.9 0.1 collective-permute-start.4
  15.9 0.0 collective-permute-done.5.rest_1_.recv_b
  16.0 2.1 %collective-permute-done.6.across = f32[40,768]{1,0:T(8,128)S(1)} collective-permute-done((f32[40,768]{1,0:T(8,128)S(1)}, f32[40,768]{1,0:T(8,128)S(1)}, u32[]{:S(2)}, u32[]{:S(2)}) %collective-permute-start.6) | collective-permute-done | bytes 122912 | tf_op jit(solution)/shard_map/ppermute | solution.py:383
  18.1 0.1 collective-permute-start.7
  18.1 0.0 collective-permute-done.4.other
  18.2 0.0 copy-done
  18.2 0.0 copy-done.4
  18.2 0.0 copy-done.8
  18.2 1.3 %shard_map.89.caps = f32[3,5,16,720]{3,2,1,0:T(8,128)S(1)} custom-call(s32[2,4]{1,0:T(2,128)S(1)} %copy-done.8, f32[80,768]{1,0:T(8,128)S(1)} %shard_map.88.mine, f32[80,768]{1,0:T(8,128)S(1)} %collective-permute-done.4.other, bf16[2,768,768]{2,1,0:T(8,128)(2,1)S(1)} %copy-done, f32[4,2,384]{2,1,0:T(2,128)S(1)} %copy-done.5, f32[4,4,768]{2,1,0:T(4,128)S(1)} %copy-done.4), custom_call_target="tpu_custom_call" | custom-call | tf_op jit(solution)/shard_map/pallas_call | solution.py:434
  19.5 0.0 collective-permute-done.7.other
  19.5 1.9 %shard_map.92 = f32[4,5,16,720]{3,2,1,0:T(8,128)} custom-call(s32[2,4]{1,0:T(2,128)S(1)} %copy-done.8, f32[3,5,16,720]{3,2,1,0:T(8,128)S(1)} %shard_map.89.caps, f32[4,5,16,720]{3,2,1,0:T(8,128)S(1)} %get-tuple-element.17.base, f32[5,16,720]{2,1,0:T(8,128)S(1)} %collective-permute-done.2.recv.recv_a, ...), custom_call_target="tpu_custom_call" | custom-call | tf_op jit(solution)/shard_map/pallas_call | solution.py:441
  (6 shorter events, 0.1 us)
Async XLA Ops:
  0.0 4.2 %copy-start.1 = (bf16[2,768,768]{2,1,0:T(8,128)(2,1)S(1)}, bf16[2,768,768]{2,1,0:T(8,128)(2,1)}, u32[]{:S(2)}) copy-start(bf16[2,768,768]{2,1,0:T(8,128)(2,1)} %constant.8.clone.fwd) | copy-start | bytes 7077892
  0.0 4.2 %copy-start.3 = (f32[4,4,768]{2,1,0:T(4,128)S(1)}, f32[4,4,768]{2,1,0:T(4,128)}, u32[]{:S(2)}) copy-start(f32[4,4,768]{2,1,0:T(4,128)} %constant.10.clone.pole) | copy-start | bytes 147460
  0.0 4.2 %copy-start.5 = (f32[4,2,384]{2,1,0:T(2,128)S(1)}, f32[4,2,384]{2,1,0:T(2,128)}, u32[]{:S(2)}) copy-start(f32[4,2,384]{2,1,0:T(2,128)} %constant.9.clone.turn) | copy-start | bytes 36868
  0.0 4.2 %copy-start.6 = (f32[4,16,720]{2,1,0:T(8,128)S(1)}, f32[4,16,720]{2,1,0:T(8,128)}, u32[]{:S(2)}) copy-start(f32[4,16,720]{2,1,0:T(8,128)} %north.1) | copy-start | bytes 552964
  0.0 4.2 %copy-start.2 = (f32[4,5,16,720]{3,2,1,0:T(8,128)S(1)}, f32[4,5,16,720]{3,2,1,0:T(8,128)}, u32[]{:S(2)}) copy-start(f32[4,5,16,720]{3,2,1,0:T(8,128)} %adj.1) | copy-start | bytes 2764804
  0.0 4.2 %copy-start.7 = (f32[4,16,720]{2,1,0:T(8,128)S(1)}, f32[4,16,720]{2,1,0:T(8,128)}, u32[]{:S(2)}) copy-start(f32[4,16,720]{2,1,0:T(8,128)} %east.1) | copy-start | bytes 552964
  1.2 9.0 %collective-permute-start.2 = (f32[5,16,720]{2,1,0:T(8,128)S(1)}, f32[5,16,720]{2,1,0:T(8,128)S(1)}, u32[]{:S(2)}, u32[]{:S(2)}) collective-permute-start(f32[5,16,720]{2,1,0:T(8,128)S(1)} %shard_map.82.after), channel_id=1, source_target_pairs={{0,4},{1,5},{2,6},{3,7},{4,0},{5,1},{6,2},{7,3},{8,12},{9,13},{10,... | collective-permute-start | bytes 691208 | tf_op jit(solution)/shard_map/ppermute | solution.py:383
  5.7 1.6 %collective-permute-start = (f32[80,768]{1,0:T(8,128)S(1)}, f32[80,768]{1,0:T(8,128)S(1)}, u32[]{:S(2)}, u32[]{:S(2)}) collective-permute-start(f32[80,768]{1,0:T(8,128)S(1)} %get-tuple-element.13), channel_id=1, source_target_pairs={{0,1},{1,0},{2,3},{3,2},{4,5},{5,4},{6,7},{7,6},{8,9},{9,8},{10,11... | collective-permute-start | bytes 737288 | tf_op jit(solution)/shard_map/ppermute | solution.py:383
  7.3 8.4 %collective-permute-start.1 = (f32[80,768]{1,0:T(8,128)S(1)}, f32[80,768]{1,0:T(8,128)S(1)}, u32[]{:S(2)}, u32[]{:S(2)}) collective-permute-start(f32[80,768]{1,0:T(8,128)S(1)} %shard_map.85.after.mine), channel_id=1, source_target_pairs={{0,2},{1,3},{2,0},{3,1},{4,6},{5,7},{6,4},{7,5},{8,10},{9,11},{10,... | collective-permute-start | bytes 737288 | tf_op jit(solution)/shard_map/ppermute | solution.py:383
  8.9 7.0 %collective-permute-start.5 = (f32[5,16,720]{2,1,0:T(8,128)S(1)}, f32[5,16,720]{2,1,0:T(8,128)S(1)}, u32[]{:S(2)}, u32[]{:S(2)}) collective-permute-start(f32[5,16,720]{2,1,0:T(8,128)S(1)} %get-tuple-element.18), channel_id=1, source_target_pairs={{4,8},{5,9},{6,10},{7,11},{8,4},{9,5},{10,6},{11,7},{12,16},{13,17... | collective-permute-start | bytes 691208 | tf_op jit(solution)/shard_map/ppermute | solution.py:383
  10.7 1.4 %collective-permute-start.3 = (f32[40,768]{1,0:T(8,128)S(1)}, f32[40,768]{1,0:T(8,128)S(1)}, u32[]{:S(2)}, u32[]{:S(2)}) collective-permute-start(f32[40,768]{1,0:T(8,128)S(1)} %get-tuple-element.16.after), channel_id=1, source_target_pairs={{0,1},{1,0},{2,3},{3,2},{4,5},{5,4},{6,7},{7,6},{8,9},{9,8},{10,11... | collective-permute-start | bytes 368648 | tf_op jit(solution)/shard_map/ppermute | solution.py:383
  12.1 5.9 %collective-permute-start.6 = (f32[40,768]{1,0:T(8,128)S(1)}, f32[40,768]{1,0:T(8,128)S(1)}, u32[]{:S(2)}, u32[]{:S(2)}) collective-permute-start(f32[40,768]{1,0:T(8,128)S(1)} %shard_map.87.after.x.mine), channel_id=1, source_target_pairs={{0,2},{1,3},{2,0},{3,1},{4,6},{5,7},{6,4},{7,5},{8,10},{9,11},{10,... | collective-permute-start | bytes 368648 | tf_op jit(solution)/shard_map/ppermute | solution.py:383
  15.8 2.3 %copy-start = (bf16[2,768,768]{2,1,0:T(8,128)(2,1)S(1)}, bf16[2,768,768]{2,1,0:T(8,128)(2,1)}, u32[]{:S(2)}) copy-start(bf16[2,768,768]{2,1,0:T(8,128)(2,1)} %constant.11.clone.bwd) | copy-start | bytes 7077892
  15.8 2.3 %copy-start.4 = (f32[4,4,768]{2,1,0:T(4,128)S(1)}, f32[4,4,768]{2,1,0:T(4,128)}, u32[]{:S(2)}) copy-start(f32[4,4,768]{2,1,0:T(4,128)} %constant.10.clone.pole) | copy-start | bytes 147460
  15.9 2.3 %copy-start.8 = (s32[2,4]{1,0:T(2,128)S(1)}, s32[2,4]{1,0:T(2,128)}, u32[]{:S(2)}) copy-start(s32[2,4]{1,0:T(2,128)} %cutoff.3) | copy-start | bytes 100
  15.9 2.3 %collective-permute-start.4 = (f32[80,768]{1,0:T(8,128)S(1)}, f32[80,768]{1,0:T(8,128)S(1)}, u32[]{:S(2)}, u32[]{:S(2)}) collective-permute-start(f32[80,768]{1,0:T(8,128)S(1)} %shard_map.88.mine), channel_id=1, source_target_pairs={{0,1},{1,0},{2,3},{3,2},{4,5},{5,4},{6,7},{7,6},{8,9},{9,8},{10,11... | collective-permute-start | bytes 737288 | tf_op jit(solution)/shard_map/ppermute | solution.py:383
  18.1 1.4 %collective-permute-start.7 = (f32[40,768]{1,0:T(8,128)S(1)}, f32[40,768]{1,0:T(8,128)S(1)}, u32[]{:S(2)}, u32[]{:S(2)}) collective-permute-start(f32[40,768]{1,0:T(8,128)S(1)} %shard_map.91.mine), channel_id=1, source_target_pairs={{0,1},{1,0},{2,3},{3,2},{4,5},{5,4},{6,7},{7,6},{8,9},{9,8},{10,11... | collective-permute-start | bytes 368648 | tf_op jit(solution)/shard_map/ppermute | solution.py:383

commit v5 on v4

--- a/solution.py
+++ b/solution.py
@@ -84,13 +84,26 @@
     return c * a - s * b, s * a + c * b
 
 
-def weighted(block, kept, circle, turn, lon):
+def weighted(block, weights):
     half = block.shape[1] // 2
-    wave = lax.broadcasted_iota(jnp.int32, (1, half), 1)
-    weight = jnp.where(wave <= kept, jnp.where(wave == 0, 1.0 / circle, 2.0 / circle), 0.0).astype(jnp.float32)
-    wa, wb = weight * turn[lon, 0:1], weight * turn[lon, 1:2]
     c, s = block[:, :half], block[:, half:]
-    return jnp.concatenate([c * wa + s * wb, s * wa - c * wb], axis=1)
+    return jnp.concatenate([c * weights[0:1] + s * weights[1:2], s * weights[0:1] - c * weights[1:2]], axis=1)
+
+
+def weight_kernel(lat_count, circle, cutoff, after, turn, out):
+    rows = cutoff.shape[1]
+    south, polar, _ = latitude_role(lat_count)
+    lon = lax.axis_index("lon")
+    wave = lax.broadcasted_iota(jnp.int32, (1, turn.shape[-1]), 1)
+
+    @pl.when(polar)
+    def _():
+        for slot in range(rows - 1):
+            row = jnp.where(south, rows - 2 - slot, slot + 1)
+            kept = jnp.where(south, cutoff[1, row], cutoff[0, row])
+            weight = jnp.where(wave <= kept, jnp.where(wave == 0, 1.0 / circle, 2.0 / circle), 0.0).astype(jnp.float32)
+            for k in (0, 1):
+                out[slot, k : k + 1] = weight * turn[lon, k : k + 1]
 
 
 def edge_kernel(lat_count, adj_hbm, north_hbm, edge, adj, north, sems):
@@ -249,51 +262,44 @@
         rows_ref[k, :, h * half_lev : (h + 1) * half_lev, :] = y[h][..., :cols]
 
 
-def halves_of(mine, other, own):
-    first, second = mine[...], other[...]
-    near = own == 0
-    return jnp.where(near, first, second), jnp.where(near, second, first)
-
-
-def cap_kernel(lat_count, circle, cutoff, mine, other, bwd, turn, pole, out):
+def cap_kernel(lat_count, circle, weights, mine, other, third, bwd, pole, out):
     _, tracers, levels, cols = out.shape
     half_lev = levels // 2
     n_half = tracers * half_lev
     half = bwd.shape[1] // 2
-    rows = cutoff.shape[1]
-    south, polar, _ = latitude_role(lat_count)
+    _, polar, _ = latitude_role(lat_count)
     lon, own, _ = longitude_role()
 
     @pl.when(polar)
     def _():
-        halves = halves_of(mine, other, own)
+        parts = (mine, own), (other, 1 - own)
         cos, sin = pole[lon, 1:2], pole[lon, 2:3]
         at = KF % LANE
-        for t in range(tracers):
-            for h in (0, 1):
-                p = halves[h][t * half_lev : (t + 1) * half_lev, half - LANE : half]
+        for source, h in parts:
+            lev = pl.ds(pl.multiple_of(h * half_lev, half_lev), half_lev)
+            for t in range(tracers):
+                p = source[t * half_lev : (t + 1) * half_lev, half - LANE : half]
                 c0, c1, s1 = p[:, at : at + 1], p[:, at + 1 : at + 2], p[:, at + 2 : at + 3]
                 y = (1.0 / circle) * c0 + (2.0 / circle) * (c1 * cos + s1 * sin)
-                out[0, t, h * half_lev : (h + 1) * half_lev, :] = y[:, :cols]
-        blocks = []
-        for slot in range(2):
-            row = jnp.where(south, rows - 2 - slot, slot + 1)
-            kept = jnp.where(south, cutoff[1, row], cutoff[0, row])
-            for h in (0, 1):
-                block = halves[h][slot * n_half : (slot + 1) * n_half]
-                blocks.append(weighted(block, kept, circle, turn, lon))
+                out[0, t, lev, :] = y[:, :cols]
+        blocks = [
+            weighted(source[slot * n_half : (slot + 1) * n_half], weights[slot]) for slot in range(2) for source, _ in parts
+        ]
+        blocks.append(weighted(third[...], weights[2]))
         y = dot3(jnp.concatenate(blocks), bwd)
-        for slot in range(2):
-            place(out, slot + 1, y[2 * slot * n_half : 2 * (slot + 1) * n_half], cols, half_lev)
+        places = [(slot + 1, h) for slot in range(2) for _, h in parts] + [(3, own)]
+        for k, (slot, h) in enumerate(places):
+            lev = pl.ds(pl.multiple_of(h * half_lev, half_lev), half_lev)
+            out[slot, :, lev, :] = y[k * n_half : (k + 1) * n_half, :cols].reshape(tracers, half_lev, cols)
 
 
 def finish_kernel(
-    lat_count, circle, cutoff, caps, base, recv_a, recv_b, from_core, from_x, mine, other, bwd, turn, out, rows_ref, sems,
+    lat_count, circle, weights, caps, base, recv_a, recv_b, from_core, from_x, third, bwd, out, rows_ref, last_ref, sems,
 ):
     rows, tracers, levels, cols = base.shape
     half_lev = levels // 2
     south, polar, even = latitude_role(lat_count)
-    lon, own, right_core = longitude_role()
+    _, own, right_core = longitude_role()
 
     @pl.when(polar)
     def _():
@@ -303,10 +309,12 @@
             copies.append(pltpu.make_async_copy(caps.at[near], out.at[row], sems.at[near]))
             copies[-1].start()
         row = jnp.where(south, 0, rows - 1)
-        kept = jnp.where(south, cutoff[1, row], cutoff[0, row])
-        blocks = [weighted(block, kept, circle, turn, lon) for block in halves_of(mine, other, own)]
-        place(rows_ref, 0, dot3(jnp.concatenate(blocks), bwd), cols, half_lev)
-        copies.append(pltpu.make_async_copy(rows_ref.at[0], out.at[row], sems.at[rows - 1]))
+        here, there = (pl.ds(pl.multiple_of(h * half_lev, half_lev), half_lev) for h in (own, 1 - own))
+        copies.append(pltpu.make_async_copy(caps.at[rows - 1, :, here, :], out.at[row, :, here, :], sems.at[rows - 1]))
+        copies[-1].start()
+        y = dot3(weighted(third[...], weights[2]), bwd)
+        last_ref[...] = y[:, :cols].reshape(tracers, half_lev, cols)
+        copies.append(pltpu.make_async_copy(last_ref, out.at[row, :, there, :], sems.at[rows]))
         copies[-1].start()
         for copy in copies:
             copy.wait()
@@ -420,7 +428,15 @@
             cost_estimate=HEAVY,
         )(*(put(x, VMEM) for x in args))
 
-    (part,) = call(sum_kernel, (pair,), keep, got, token(local))
+    weights = pl.pallas_call(
+        functools.partial(weight_kernel, lat_count, circle),
+        out_shape=VMEM((rows - 1, 2, width // 2), f32),
+        in_specs=[smem] + [vmem] * 2,
+        out_specs=vmem,
+        compiler_params=params,
+        cost_estimate=HEAVY,
+    )(cutoff, put(local, VMEM), put(turn, VMEM))
+    (part,) = call(sum_kernel, (pair,), keep, got, weights)
     across = swap(part, by_x)
     recv_b = swap(edge_b, by_next)
     keep3, send3 = call(third_kernel, (single, single), local, recv_a, part, fwd, turn, scratch=((2 * n_half, wide),))
@@ -433,19 +449,19 @@
     other3 = swap(mine3, by_core)
     caps = pl.pallas_call(
         functools.partial(cap_kernel, lat_count, circle),
-        out_shape=VMEM((3,) + adj.shape[1:], f32),
-        in_specs=[smem] + [vmem] * 5,
+        out_shape=VMEM(adj.shape, f32),
+        in_specs=[vmem] * 6,
         out_specs=vmem,
         compiler_params=params,
-    )(cutoff, *(put(x, VMEM) for x in (mine, other, bwd, turn, pole)))
+    )(*(put(x, VMEM) for x in (weights, mine, other, mine3, bwd, pole)))
     return pl.pallas_call(
         functools.partial(finish_kernel, lat_count, circle),
         out_shape=jax.ShapeDtypeStruct(adj.shape, f32),
-        in_specs=[smem] + [vmem] * 10,
+        in_specs=[vmem] * 9,
         out_specs=anywhere,
-        scratch_shapes=[VMEM(adj.shape, f32), dma((rows,))],
+        scratch_shapes=[VMEM(adj.shape, f32), VMEM((tracers, levels // 2, cols), f32), dma((rows + 1,))],
         compiler_params=params,
-    )(cutoff, *(put(x, VMEM) for x in (caps, base, recv_a, recv_b, got, across, mine3, other3, bwd, turn)))
+    )(*(put(x, VMEM) for x in (weights, caps, base, recv_a, recv_b, got, across, other3, bwd)))
 
 
 full_precision = lax.Precision.HIGHEST

time: 21.6 us -> 21 us (0.972)
  Pallas kernels: 6.5 us -> 6.14 us
  waiting for transfers between devices: 7.36 us -> 7.11 us
    pallas_call x1, Pallas kernels: 1.93 us -> 1.34 us  [fast_body(): pl.pallas_call(functools.partial(finish_kernel, lat_count, circle), out_s...]
    pallas_call x0 -> x1, Pallas kernels: none -> 0.58 us  [fast_body(): pl.pallas_call(functools.partial(weight_kernel, lat_count, circle), out_s...]
    pallas_call x1, Pallas kernels: 1.32 us -> 0.99 us  [fast_body(): pl.pallas_call(functools.partial(cap_kernel, lat_count, circle), out_shap...]
    ppermute x8, waiting for transfers between devices: 7.36 us -> 7.11 us  [swap(): lax.ppermute(x, ('lat', 'lon'), [(a * lon_count + i, b * lon_count + j) f...]
  transfers between devices with their start and end apart: 8 -> 8, of which waited for: 5 -> 6; matrix products, arithmetic and copies ran while one was open for 0% -> 0% of each run, Pallas kernels for 16% -> 18%
where the time goes in v5:
time: 21 us; the launch traced here: 20.8 us
  starting transfers between devices  7.33 us (35%)
  waiting for transfers between devices  7.11 us (34%)
  Pallas kernels  6.14 us (29%)
    ppermute x8, starting transfers between devices, swap(): lax.ppermute(x, ('lat', 'lon'), [(a * lon_count + i, b * lon_count + j) f...  7.33 us
    ppermute x8, waiting for transfers between devices, swap(): lax.ppermute(x, ('lat', 'lon'), [(a * lon_count + i, b * lon_count + j) f...  7.11 us
    pallas_call x6, Pallas kernels, call(): pl.pallas_call(functools.partial(kernel, lat_count), out_shape=[VMEM(s, f...  2.08 us
    pallas_call x1, Pallas kernels, fast_body(): pl.pallas_call(functools.partial(finish_kernel, lat_count, circle), out_s...  1.34 us
    pallas_call x1, Pallas kernels, fast_body(): pl.pallas_call(functools.partial(edge_kernel, lat_count), out_shape=VMEM(...  1.15 us
    pallas_call x1, Pallas kernels, fast_body(): pl.pallas_call(functools.partial(cap_kernel, lat_count, circle), out_shap...  0.99 us
    pallas_call x1, Pallas kernels, fast_body(): pl.pallas_call(functools.partial(weight_kernel, lat_count, circle), out_s...  0.58 us
  transfers between devices with their start and end apart: 8, of which 6 were waited for; matrix products, arithmetic and copies ran while one was open for 0% of the time, Pallas kernels for 18%

profile of v5, /device:TPU:0, one launch (start us, length us, event | category | flops | bytes accessed | tf_op | source)
XLA Modules:
  0.0 20.8 jit_solution(15301994320922065535)
XLA Ops:
  0.0 0.0 copy-start.1
  0.0 0.0 copy-start.3
  0.0 0.0 copy-start.6
  0.0 0.0 copy-start.4
  0.0 0.0 copy-start.2
  0.0 0.0 copy-start.5
  0.0 1.1 %shard_map.82.after = f32[5,16,720]{2,1,0:T(8,128)S(1)} custom-call(f32[4,5,16,720]{3,2,1,0:T(8,128)} %adj.1, f32[4,16,720]{2,1,0:T(8,128)} %north.1), custom_call_target="tpu_custom_call" | custom-call | flops 137438953472 | tf_op jit(solution)/shard_map/pallas_call | solution.py:398
  1.2 0.0 copy-start.7
  1.2 3.0 %collective-permute-start.2 = (f32[5,16,720]{2,1,0:T(8,128)S(1)}, f32[5,16,720]{2,1,0:T(8,128)S(1)}, u32[]{:S(2)}, u32[]{:S(2)}) collective-permute-start(f32[5,16,720]{2,1,0:T(8,128)S(1)} %shard_map.82.after), channel_id=1, source_target_pairs={{0,4},{1,5},{2,6},{3,7},{4,0},{5,1},{6,2},{7,3},{8,12},{9,13},{10,... | collective-permute-start | bytes 691208 | tf_op jit(solution)/shard_map/ppermute | solution.py:391
  4.2 0.0 copy-done.1
  4.2 0.0 copy-done.3
  4.2 0.0 copy-done.6
  4.2 0.0 copy-done.4
  4.3 0.0 copy-done.2
  4.3 0.0 copy-done.5
  4.3 1.4 %shard_map.83 = (f32[4,5,16,720]{3,2,1,0:T(8,128)S(1)}, f32[5,16,720]{2,1,0:T(8,128)S(1)}, f32[80,768]{1,0:T(8,128)S(1)}, f32[80,768]{1,0:T(8,128)S(1)}, f32[80,768]{1,0:T(8,128)S(1)}) custom-call(f32[5,16,720]{2,1,0:T(8,128)S(1)} %shard_map.82.after, f32[4,5,16,720]{3,2,1,0:T(8,128)S(1)} %copy-done.2, f32[4,16,720]{2,1,0:T(8,128)S(1)} %copy-done.5, ...), custom_call_target="tpu_custom_call" | custom-call | bytes 1000 | tf_op jit(solution)/shard_map/pallas_call | solution.py:378
  5.7 0.1 collective-permute-start
  5.8 0.0 copy-done.7
  5.8 0.6 %shard_map.84.after.weights = f32[3,2,384]{2,1,0:T(2,128)S(1)} custom-call(s32[2,4]{1,0:T(2,128)S(1)} %copy-done.7, f32[80,768]{1,0:T(8,128)S(1)} %get-tuple-element.12.after.local, f32[4,2,384]{2,1,0:T(2,128)S(1)} %copy-done.6), custom_call_target="tpu_custom_call" | custom-call | flops 137438953472 | tf_op jit(solution)/shard_map/pallas_call | solution.py:431
  6.4 0.9 %collective-permute-done.got.from_core = f32[80,768]{1,0:T(8,128)S(1)} collective-permute-done((f32[80,768]{1,0:T(8,128)S(1)}, f32[80,768]{1,0:T(8,128)S(1)}, u32[]{:S(2)}, u32[]{:S(2)}) %collective-permute-start) | collective-permute-done | bytes 245792 | tf_op jit(solution)/shard_map/ppermute | solution.py:391
  7.3 1.6 %collective-permute-start.1 = (f32[80,768]{1,0:T(8,128)S(1)}, f32[80,768]{1,0:T(8,128)S(1)}, u32[]{:S(2)}, u32[]{:S(2)}) collective-permute-start(f32[80,768]{1,0:T(8,128)S(1)} %shard_map.85.after.mine), channel_id=1, source_target_pairs={{0,2},{1,3},{2,0},{3,1},{4,6},{5,7},{6,4},{7,5},{8,10},{9,11},{10,... | collective-permute-start | bytes 737288 | tf_op jit(solution)/shard_map/ppermute | solution.py:391
  8.9 0.7 %collective-permute-start.6 = (f32[5,16,720]{2,1,0:T(8,128)S(1)}, f32[5,16,720]{2,1,0:T(8,128)S(1)}, u32[]{:S(2)}, u32[]{:S(2)}) collective-permute-start(f32[5,16,720]{2,1,0:T(8,128)S(1)} %get-tuple-element.17), channel_id=1, source_target_pairs={{4,8},{5,9},{6,10},{7,11},{8,4},{9,5},{10,6},{11,7},{12,16},{13,17... | collective-permute-start | bytes 691208 | tf_op jit(solution)/shard_map/ppermute | solution.py:391
  9.6 0.6 %collective-permute-done.2.recv.recv_a = f32[5,16,720]{2,1,0:T(8,128)S(1)} collective-permute-done((f32[5,16,720]{2,1,0:T(8,128)S(1)}, f32[5,16,720]{2,1,0:T(8,128)S(1)}, u32[]{:S(2)}, u32[]{:S(2)}) %collective-permute-start.2) | collective-permute-done | bytes 230432 | tf_op jit(solution)/shard_map/ppermute | solution.py:391
  10.2 0.5 %shard_map.86 = (f32[40,768]{1,0:T(8,128)S(1)}, f32[40,768]{1,0:T(8,128)S(1)}) custom-call(f32[80,768]{1,0:T(8,128)S(1)} %get-tuple-element.12.after.local, f32[5,16,720]{2,1,0:T(8,128)S(1)} %collective-permute-done.2.recv.recv_a, f32[80,768]{1,0:T(8,128)S(1)} %shard_map.85.after.mine, bf16[2,768,768]{2,1,0:T(8,128)(2,1)S(1)} %copy-done.1, ...), custom_call_target="tpu_custom_call" | custom-call | bytes 1000 | tf_op jit(solution)/shard_map/pallas_call | solution.py:378
  10.7 0.1 collective-permute-start.3
  10.8 1.3 %collective-permute-done.3.got = f32[40,768]{1,0:T(8,128)S(1)} collective-permute-done((f32[40,768]{1,0:T(8,128)S(1)}, f32[40,768]{1,0:T(8,128)S(1)}, u32[]{:S(2)}, u32[]{:S(2)}) %collective-permute-start.3) | collective-permute-done | bytes 122912 | tf_op jit(solution)/shard_map/ppermute | solution.py:391
  12.2 1.8 %collective-permute-start.5 = (f32[40,768]{1,0:T(8,128)S(1)}, f32[40,768]{1,0:T(8,128)S(1)}, u32[]{:S(2)}, u32[]{:S(2)}) collective-permute-start(f32[40,768]{1,0:T(8,128)S(1)} %shard_map.87.after.x.mine), channel_id=1, source_target_pairs={{0,2},{1,3},{2,0},{3,1},{4,6},{5,7},{6,4},{7,5},{8,10},{9,11},{10,... | collective-permute-start | bytes 368648 | tf_op jit(solution)/shard_map/ppermute | solution.py:391
  13.9 1.8 %collective-permute-done.1.across.rest_0_.from_x = f32[80,768]{1,0:T(8,128)S(1)} collective-permute-done((f32[80,768]{1,0:T(8,128)S(1)}, f32[80,768]{1,0:T(8,128)S(1)}, u32[]{:S(2)}, u32[]{:S(2)}) %collective-permute-start.1) | collective-permute-done | bytes 245792 | tf_op jit(solution)/shard_map/ppermute | solution.py:391
  15.8 0.0 copy-start
  15.8 0.1 collective-permute-start.4
  15.9 0.0 collective-permute-done.6.rest_1_.recv_b
  15.9 2.1 %collective-permute-done.5.across = f32[40,768]{1,0:T(8,128)S(1)} collective-permute-done((f32[40,768]{1,0:T(8,128)S(1)}, f32[40,768]{1,0:T(8,128)S(1)}, u32[]{:S(2)}, u32[]{:S(2)}) %collective-permute-start.5) | collective-permute-done | bytes 122912 | tf_op jit(solution)/shard_map/ppermute | solution.py:391
  18.1 0.1 collective-permute-start.7
  18.1 0.0 collective-permute-done.4.other
  18.1 0.0 copy-done
  18.2 1.0 %shard_map.91.caps = f32[4,5,16,720]{3,2,1,0:T(8,128)S(1)} custom-call(f32[3,2,384]{2,1,0:T(2,128)S(1)} %shard_map.84.after.weights, f32[80,768]{1,0:T(8,128)S(1)} %shard_map.88.mine, f32[80,768]{1,0:T(8,128)S(1)} %collective-permute-done.4.other, f32[40,768]{1,0:T(8,128)S(1)} %shard_map.90.third, bf16[2,768,768]{2,1,0:T(8,128)(2,1)S(1)} %copy-done, ...), custom_call_target="tpu_custom_call" | custom-call | tf_op jit(solution)/shard_map/pallas_call | solution.py:450
  19.1 0.3 %collective-permute-done.7.third = f32[40,768]{1,0:T(8,128)S(1)} collective-permute-done((f32[40,768]{1,0:T(8,128)S(1)}, f32[40,768]{1,0:T(8,128)S(1)}, u32[]{:S(2)}, u32[]{:S(2)}) %collective-permute-start.7) | collective-permute-done | bytes 122912 | tf_op jit(solution)/shard_map/ppermute | solution.py:391
  19.5 1.3 %shard_map.92 = f32[4,5,16,720]{3,2,1,0:T(8,128)} custom-call(f32[3,2,384]{2,1,0:T(2,128)S(1)} %shard_map.84.after.weights, f32[4,5,16,720]{3,2,1,0:T(8,128)S(1)} %shard_map.91.caps, f32[4,5,16,720]{3,2,1,0:T(8,128)S(1)} %get-tuple-element.18.base, f32[5,16,720]{2,1,0:T(8,128)S(1)} %collective-permute-done.2.recv.recv_a, ...), custom_call_target="tpu_custom_call" | custom-call | tf_op jit(solution)/shard_map/pallas_call | solution.py:457
  (5 shorter events, 0.1 us)
Async XLA Ops:
  0.0 4.2 %copy-start.1 = (bf16[2,768,768]{2,1,0:T(8,128)(2,1)S(1)}, bf16[2,768,768]{2,1,0:T(8,128)(2,1)}, u32[]{:S(2)}) copy-start(bf16[2,768,768]{2,1,0:T(8,128)(2,1)} %constant.8.clone.fwd) | copy-start | bytes 7077892
  0.0 4.2 %copy-start.3 = (f32[4,4,768]{2,1,0:T(4,128)S(1)}, f32[4,4,768]{2,1,0:T(4,128)}, u32[]{:S(2)}) copy-start(f32[4,4,768]{2,1,0:T(4,128)} %constant.10.clone.pole) | copy-start | bytes 147460
  0.0 4.2 %copy-start.6 = (f32[4,2,384]{2,1,0:T(2,128)S(1)}, f32[4,2,384]{2,1,0:T(2,128)}, u32[]{:S(2)}) copy-start(f32[4,2,384]{2,1,0:T(2,128)} %constant.9.clone.turn) | copy-start | bytes 36868
  0.0 4.2 %copy-start.4 = (f32[4,16,720]{2,1,0:T(8,128)S(1)}, f32[4,16,720]{2,1,0:T(8,128)}, u32[]{:S(2)}) copy-start(f32[4,16,720]{2,1,0:T(8,128)} %north.1) | copy-start | bytes 552964
  0.0 4.2 %copy-start.2 = (f32[4,5,16,720]{3,2,1,0:T(8,128)S(1)}, f32[4,5,16,720]{3,2,1,0:T(8,128)}, u32[]{:S(2)}) copy-start(f32[4,5,16,720]{3,2,1,0:T(8,128)} %adj.1) | copy-start | bytes 2764804
  0.0 4.3 %copy-start.5 = (f32[4,16,720]{2,1,0:T(8,128)S(1)}, f32[4,16,720]{2,1,0:T(8,128)}, u32[]{:S(2)}) copy-start(f32[4,16,720]{2,1,0:T(8,128)} %east.1) | copy-start | bytes 552964
  1.2 4.6 %copy-start.7 = (s32[2,4]{1,0:T(2,128)S(1)}, s32[2,4]{1,0:T(2,128)}, u32[]{:S(2)}) copy-start(s32[2,4]{1,0:T(2,128)} %cutoff.1) | copy-start | bytes 100
  1.2 9.0 %collective-permute-start.2 = (f32[5,16,720]{2,1,0:T(8,128)S(1)}, f32[5,16,720]{2,1,0:T(8,128)S(1)}, u32[]{:S(2)}, u32[]{:S(2)}) collective-permute-start(f32[5,16,720]{2,1,0:T(8,128)S(1)} %shard_map.82.after), channel_id=1, source_target_pairs={{0,4},{1,5},{2,6},{3,7},{4,0},{5,1},{6,2},{7,3},{8,12},{9,13},{10,... | collective-permute-start | bytes 691208 | tf_op jit(solution)/shard_map/ppermute | solution.py:391
  5.7 1.6 %collective-permute-start = (f32[80,768]{1,0:T(8,128)S(1)}, f32[80,768]{1,0:T(8,128)S(1)}, u32[]{:S(2)}, u32[]{:S(2)}) collective-permute-start(f32[80,768]{1,0:T(8,128)S(1)} %get-tuple-element.14), channel_id=1, source_target_pairs={{0,1},{1,0},{2,3},{3,2},{4,5},{5,4},{6,7},{7,6},{8,9},{9,8},{10,11... | collective-permute-start | bytes 737288 | tf_op jit(solution)/shard_map/ppermute | solution.py:391
  7.3 8.4 %collective-permute-start.1 = (f32[80,768]{1,0:T(8,128)S(1)}, f32[80,768]{1,0:T(8,128)S(1)}, u32[]{:S(2)}, u32[]{:S(2)}) collective-permute-start(f32[80,768]{1,0:T(8,128)S(1)} %shard_map.85.after.mine), channel_id=1, source_target_pairs={{0,2},{1,3},{2,0},{3,1},{4,6},{5,7},{6,4},{7,5},{8,10},{9,11},{10,... | collective-permute-start | bytes 737288 | tf_op jit(solution)/shard_map/ppermute | solution.py:391
  8.9 7.0 %collective-permute-start.6 = (f32[5,16,720]{2,1,0:T(8,128)S(1)}, f32[5,16,720]{2,1,0:T(8,128)S(1)}, u32[]{:S(2)}, u32[]{:S(2)}) collective-permute-start(f32[5,16,720]{2,1,0:T(8,128)S(1)} %get-tuple-element.17), channel_id=1, source_target_pairs={{4,8},{5,9},{6,10},{7,11},{8,4},{9,5},{10,6},{11,7},{12,16},{13,17... | collective-permute-start | bytes 691208 | tf_op jit(solution)/shard_map/ppermute | solution.py:391
  10.7 1.4 %collective-permute-start.3 = (f32[40,768]{1,0:T(8,128)S(1)}, f32[40,768]{1,0:T(8,128)S(1)}, u32[]{:S(2)}, u32[]{:S(2)}) collective-permute-start(f32[40,768]{1,0:T(8,128)S(1)} %get-tuple-element.16.after), channel_id=1, source_target_pairs={{0,1},{1,0},{2,3},{3,2},{4,5},{5,4},{6,7},{7,6},{8,9},{9,8},{10,11... | collective-permute-start | bytes 368648 | tf_op jit(solution)/shard_map/ppermute | solution.py:391
  12.2 5.9 %collective-permute-start.5 = (f32[40,768]{1,0:T(8,128)S(1)}, f32[40,768]{1,0:T(8,128)S(1)}, u32[]{:S(2)}, u32[]{:S(2)}) collective-permute-start(f32[40,768]{1,0:T(8,128)S(1)} %shard_map.87.after.x.mine), channel_id=1, source_target_pairs={{0,2},{1,3},{2,0},{3,1},{4,6},{5,7},{6,4},{7,5},{8,10},{9,11},{10,... | collective-permute-start | bytes 368648 | tf_op jit(solution)/shard_map/ppermute | solution.py:391
  15.8 2.3 %copy-start = (bf16[2,768,768]{2,1,0:T(8,128)(2,1)S(1)}, bf16[2,768,768]{2,1,0:T(8,128)(2,1)}, u32[]{:S(2)}) copy-start(bf16[2,768,768]{2,1,0:T(8,128)(2,1)} %constant.11.clone.bwd) | copy-start | bytes 7077892
  15.8 2.3 %collective-permute-start.4 = (f32[80,768]{1,0:T(8,128)S(1)}, f32[80,768]{1,0:T(8,128)S(1)}, u32[]{:S(2)}, u32[]{:S(2)}) collective-permute-start(f32[80,768]{1,0:T(8,128)S(1)} %shard_map.88.mine), channel_id=1, source_target_pairs={{0,1},{1,0},{2,3},{3,2},{4,5},{5,4},{6,7},{7,6},{8,9},{9,8},{10,11... | collective-permute-start | bytes 737288 | tf_op jit(solution)/shard_map/ppermute | solution.py:391
  18.1 1.4 %collective-permute-start.7 = (f32[40,768]{1,0:T(8,128)S(1)}, f32[40,768]{1,0:T(8,128)S(1)}, u32[]{:S(2)}, u32[]{:S(2)}) collective-permute-start(f32[40,768]{1,0:T(8,128)S(1)} %shard_map.90.third), channel_id=1, source_target_pairs={{0,1},{1,0},{2,3},{3,2},{4,5},{5,4},{6,7},{7,6},{8,9},{9,8},{10,11... | collective-permute-start | bytes 368648 | tf_op jit(solution)/shard_map/ppermute | solution.py:391

commit v6 on v5

--- a/solution.py
+++ b/solution.py
@@ -90,10 +90,13 @@
     return jnp.concatenate([c * weights[0:1] + s * weights[1:2], s * weights[0:1] - c * weights[1:2]], axis=1)
 
 
-def weight_kernel(lat_count, circle, cutoff, after, turn, out):
-    rows = cutoff.shape[1]
+def side_kernel(lat_count, circle, cutoff, after, adj, east, north, turn, pole, out, third, flux):
+    rows, tracers, levels, cols = adj.shape
+    wide = third.shape[1]
+    half_lev = levels // 2
+    n_half = tracers * half_lev
     south, polar, _ = latitude_role(lat_count)
-    lon = lax.axis_index("lon")
+    lon, own, _ = longitude_role()
     wave = lax.broadcasted_iota(jnp.int32, (1, turn.shape[-1]), 1)
 
     @pl.when(polar)
@@ -104,6 +107,34 @@
             weight = jnp.where(wave <= kept, jnp.where(wave == 0, 1.0 / circle, 2.0 / circle), 0.0).astype(jnp.float32)
             for k in (0, 1):
                 out[slot, k : k + 1] = weight * turn[lon, k : k + 1]
+        sign = jnp.where(south, -1.0, 1.0).astype(jnp.float32)
+        top, below = jnp.where(south, rows - 1, 0), jnp.where(south, rows - 2, 1)
+        last, above = jnp.where(south, 0, rows - 1), jnp.where(south, 1, rows - 2)
+        flux[..., cols:] = jnp.zeros(flux.shape[:-1] + (wide - cols,), jnp.float32)
+        one, cos, sin = (pole[lon, k : k + 1] for k in range(3))
+        spare = (cols + 2) // LANE * LANE
+        at = cols + 2 - spare
+        lane = lax.broadcasted_iota(jnp.int32, (levels, wide - spare), 1)
+        for t in range(tracers):
+            flux[0, t, :, :cols] = east[top] * adj[top, t]
+            flux[1, t, :, :cols] = east[last] * adj[last, t]
+            flux[2, t, :, :cols] = adj[top, t] + sign * (north[below] * adj[below, t])
+            flux[3, t, :, :cols] = sign * (north[top] * adj[top, t])
+            f = flux[0, t]
+            u = pltpu.roll(f, wide - 1, 1) - pltpu.roll(f, 1, 1) + flux[2, t]
+            v = flux[3, t]
+            c0 = jnp.sum((u + v) * one, axis=1, keepdims=True)
+            c1 = jnp.sum((u - v) * cos, axis=1, keepdims=True)
+            s1 = jnp.sum((u - v) * sin, axis=1, keepdims=True)
+            f = flux[1, t]
+            move = pltpu.roll(f, wide - 1, 1) - pltpu.roll(f, 1, 1)
+            inner = adj[last, t] - sign * (north[above] * adj[above, t]) + move[:, :cols]
+            tail = jnp.where(lane == at, c0, jnp.where(lane == at + 1, c1, jnp.where(lane == at + 2, s1, move[:, spare:])))
+            for k in (0, 1):
+                spot = slice(k * n_half + t * half_lev, k * n_half + (t + 1) * half_lev)
+                first, second = slice(0, half_lev), slice(half_lev, levels)
+                third[spot, spare:] = jnp.where(own == k, tail[first], tail[second])
+                third[spot, :cols] = jnp.where(own == k, inner[first], inner[second])
 
 
 def edge_kernel(lat_count, adj_hbm, north_hbm, edge, adj, north, sems):
@@ -121,7 +152,7 @@
 
 
 def local_kernel(
-    lat_count, after, adj, east, north, fwd, turn, pole, base, edge, keep, send, third, flux, wide_x, ends
+    lat_count, after, adj, east, north, fwd, turn, base, edge, keep, send, flux, wide_x, ends
 ):
     rows, tracers, levels, cols = adj.shape
     wide = flux.shape[-1]
@@ -171,43 +202,23 @@
 
     @pl.when(polar)
     def _():
-        for r in range(rows):
-            near = jnp.where(south, rows - 1 - r, r)
-            slot = lax.rem(near + rows - 1, rows)
+        for r in range(1, rows - 1):
+            slot = jnp.where(south, rows - 2 - r, r - 1)
             for t in range(tracers):
                 move, _ = spread(r, t)
+                inner = transported(r, t) + move[:, :cols]
                 for h in (0, 1):
                     part = slice(h * half_lev, (h + 1) * half_lev)
                     where = jnp.where(own == h, 0, 1)
-                    wide_x[slot, where, t] = move[part]
-                    wide_x[slot, where, t, :, :cols] += transported(r, t)[part]
-        c, s = turned(dot3(wide_x[:2].reshape(4 * n_half, wide), fwd), turn, lon)
+                    wide_x[slot, where, t, :, :cols] = inner[part]
+                    wide_x[slot, where, t, :, cols:] = move[part, cols:]
+        c, s = turned(dot3(wide_x[...].reshape(4 * n_half, wide), fwd), turn, lon)
         for slot in range(2):
             spot = slice(slot * n_half, (slot + 1) * n_half)
             first = slice(2 * slot * n_half, (2 * slot + 1) * n_half)
             second = slice((2 * slot + 1) * n_half, (2 * slot + 2) * n_half)
             keep[spot, :half], keep[spot, half:] = c[first], s[first]
             send[spot, :half], send[spot, half:] = c[second], s[second]
-        third[...] = wide_x[2].reshape(tracers * levels, wide)
-        sign = jnp.where(south, -1.0, 1.0).astype(jnp.float32)
-        row_p = jnp.where(south, rows - 1, 0)
-        lane = lax.broadcasted_iota(jnp.int32, (half_lev, LANE), 1)
-        one, cos, sin = (pole[lon, k : k + 1] for k in range(3))
-        for t in range(tracers):
-            m = north[row_p] * adj[row_p, t] * sign
-            for k, target in ((0, keep), (1, send)):
-                u = wide_x[3, k, t]
-                flux[:half_lev, :cols] = jnp.where(own == k, m[:half_lev], m[half_lev:])
-                v = flux[:half_lev]
-                c0 = jnp.sum((u + v) * one, axis=1, keepdims=True)
-                c1 = jnp.sum((u - v) * cos, axis=1, keepdims=True)
-                s1 = jnp.sum((u - v) * sin, axis=1, keepdims=True)
-                at = KF % LANE
-                lanes = slice(half - LANE, half)
-                spot = slice(t * half_lev, (t + 1) * half_lev)
-                target[spot, lanes] = jnp.where(
-                    lane == at, c0, jnp.where(lane == at + 1, c1, jnp.where(lane == at + 2, s1, target[spot, lanes]))
-                )
 
 
 def third_kernel(lat_count, local, recv, after, fwd, turn, keep, send, block):
@@ -230,6 +241,13 @@
         c, s = turned(dot3(block[...], fwd), turn, lon)
         keep[:, :half], keep[:, half:] = c[:n_half], s[:n_half]
         send[:, :half], send[:, half:] = c[n_half:], s[n_half:]
+        at = KF % LANE
+        spare = (cols + 2) // LANE * LANE
+        lane = lax.broadcasted_iota(jnp.int32, (2 * n_half, LANE), 1)
+        sums = pltpu.roll(local[:, spare : spare + LANE], (at - (cols + 2)) % LANE, 1)
+        sums = jnp.where((lane >= at) & (lane < at + 3), sums, 0.0)
+        keep[:, half - LANE : half] += sums[:n_half]
+        send[:, half - LANE : half] += sums[n_half:]
 
 
 def token_kernel(x, *rest):
@@ -260,6 +278,13 @@
     y = y.reshape(2, -1, half_lev, y.shape[-1])
     for h in (0, 1):
         rows_ref[k, :, h * half_lev : (h + 1) * half_lev, :] = y[h][..., :cols]
+
+
+def pole_row(sums, t, half_lev, half, pole, lon, circle):
+    p = sums[t * half_lev : (t + 1) * half_lev, half - LANE : half]
+    at = KF % LANE
+    c0, c1, s1 = p[:, at : at + 1], p[:, at + 1 : at + 2], p[:, at + 2 : at + 3]
+    return (1.0 / circle) * c0 + (2.0 / circle) * (c1 * pole[lon, 1:2] + s1 * pole[lon, 2:3])
 
 
 def cap_kernel(lat_count, circle, weights, mine, other, third, bwd, pole, out):
@@ -273,15 +298,9 @@
     @pl.when(polar)
     def _():
         parts = (mine, own), (other, 1 - own)
-        cos, sin = pole[lon, 1:2], pole[lon, 2:3]
-        at = KF % LANE
-        for source, h in parts:
-            lev = pl.ds(pl.multiple_of(h * half_lev, half_lev), half_lev)
-            for t in range(tracers):
-                p = source[t * half_lev : (t + 1) * half_lev, half - LANE : half]
-                c0, c1, s1 = p[:, at : at + 1], p[:, at + 1 : at + 2], p[:, at + 2 : at + 3]
-                y = (1.0 / circle) * c0 + (2.0 / circle) * (c1 * cos + s1 * sin)
-                out[0, t, lev, :] = y[:, :cols]
+        lev = pl.ds(pl.multiple_of(own * half_lev, half_lev), half_lev)
+        for t in range(tracers):
+            out[0, t, lev, :] = pole_row(third, t, half_lev, half, pole, lon, circle)[:, :cols]
         blocks = [
             weighted(source[slot * n_half : (slot + 1) * n_half], weights[slot]) for slot in range(2) for source, _ in parts
         ]
@@ -294,23 +313,27 @@
 
 
 def finish_kernel(
-    lat_count, circle, weights, caps, base, recv_a, recv_b, from_core, from_x, third, bwd, out, rows_ref, last_ref, sems,
+    lat_count, circle, weights, caps, base, recv_a, recv_b, from_core, from_x, third, bwd, pole, out, rows_ref, last_ref, pole_ref,
+    sems,
 ):
     rows, tracers, levels, cols = base.shape
     half_lev = levels // 2
     south, polar, even = latitude_role(lat_count)
-    _, own, right_core = longitude_role()
+    lon, own, right_core = longitude_role()
 
     @pl.when(polar)
     def _():
+        here, there = (pl.ds(pl.multiple_of(h * half_lev, half_lev), half_lev) for h in (own, 1 - own))
+        top, row = jnp.where(south, rows - 1, 0), jnp.where(south, 0, rows - 1)
+        moves = [(caps.at[near], out.at[jnp.where(south, rows - 1 - near, near)]) for near in range(1, rows - 1)]
+        moves += [(caps.at[near, :, here, :], out.at[at, :, here, :]) for near, at in ((0, top), (rows - 1, row))]
         copies = []
-        for near in range(rows - 1):
-            row = jnp.where(south, rows - 1 - near, near)
-            copies.append(pltpu.make_async_copy(caps.at[near], out.at[row], sems.at[near]))
+        for k, (source, target) in enumerate(moves):
+            copies.append(pltpu.make_async_copy(source, target, sems.at[k]))
             copies[-1].start()
-        row = jnp.where(south, 0, rows - 1)
-        here, there = (pl.ds(pl.multiple_of(h * half_lev, half_lev), half_lev) for h in (own, 1 - own))
-        copies.append(pltpu.make_async_copy(caps.at[rows - 1, :, here, :], out.at[row, :, here, :], sems.at[rows - 1]))
+        for t in range(tracers):
+            pole_ref[t] = pole_row(third, t, half_lev, bwd.shape[1] // 2, pole, lon, circle)[:, :cols]
+        copies.append(pltpu.make_async_copy(pole_ref, out.at[top, :, there, :], sems.at[rows + 1]))
         copies[-1].start()
         y = dot3(weighted(third[...], weights[2]), bwd)
         last_ref[...] = y[:, :cols].reshape(tracers, half_lev, cols)
@@ -370,6 +393,7 @@
     far = pl.BlockSpec(memory_space=HBM)
     n_half = tracers * levels // 2
     pair, single = (2 * n_half, width), (n_half, width)
+    half_row = (tracers, levels // 2, cols)
 
     def put(x, space):
         return pltpu.with_memory_space_constraint(x, space)
@@ -405,19 +429,18 @@
         compiler_params=params,
     )(put(adj, HBM), put(north, HBM))
     recv_a = swap(edge, by_lat)
-    base, edge_b, keep, send, local = call(
+    base, edge_b, keep, send = call(
         local_kernel,
-        (adj.shape, adj.shape[1:], pair, pair, (2 * n_half, wide)),
+        (adj.shape, adj.shape[1:], pair, pair),
         edge,
         adj,
         east,
         north,
         fwd,
         turn,
-        pole,
-        scratch=((levels, wide), (rows, 2, tracers, levels // 2, wide), (rows, tracers, levels, LANE)),
+        scratch=((levels, wide), (rows - 2, 2, tracers, levels // 2, wide), (rows, tracers, levels, LANE)),
     )
-    got = swap(send, by_core)
+
     def token(*args):
         return pl.pallas_call(
             token_kernel,
@@ -428,14 +451,16 @@
             cost_estimate=HEAVY,
         )(*(put(x, VMEM) for x in args))
 
-    weights = pl.pallas_call(
-        functools.partial(weight_kernel, lat_count, circle),
-        out_shape=VMEM((rows - 1, 2, width // 2), f32),
-        in_specs=[smem] + [vmem] * 2,
-        out_specs=vmem,
+    got = swap(send, by_core)
+    weights, local = pl.pallas_call(
+        functools.partial(side_kernel, lat_count, circle),
+        out_shape=[VMEM((rows - 1, 2, width // 2), f32), VMEM((2 * n_half, wide), f32)],
+        in_specs=[smem] + [vmem] * 6,
+        out_specs=[vmem] * 2,
+        scratch_shapes=[VMEM((4, tracers, levels, wide), f32)],
         compiler_params=params,
         cost_estimate=HEAVY,
-    )(cutoff, put(local, VMEM), put(turn, VMEM))
+    )(cutoff, *(put(x, VMEM) for x in (keep, adj, east, north, turn, pole)))
     (part,) = call(sum_kernel, (pair,), keep, got, weights)
     across = swap(part, by_x)
     recv_b = swap(edge_b, by_next)
@@ -457,11 +482,11 @@
     return pl.pallas_call(
         functools.partial(finish_kernel, lat_count, circle),
         out_shape=jax.ShapeDtypeStruct(adj.shape, f32),
-        in_specs=[vmem] * 9,
+        in_specs=[vmem] * 10,
         out_specs=anywhere,
-        scratch_shapes=[VMEM(adj.shape, f32), VMEM((tracers, levels // 2, cols), f32), dma((rows + 1,))],
+        scratch_shapes=[VMEM(adj.shape, f32), VMEM(half_row, f32), VMEM(half_row, f32), dma((rows + 2,))],
         compiler_params=params,
-    )(*(put(x, VMEM) for x in (weights, caps, base, recv_a, recv_b, got, across, other3, bwd)))
+    )(*(put(x, VMEM) for x in (weights, caps, base, recv_a, recv_b, got, across, other3, bwd, pole)))
 
 
 full_precision = lax.Precision.HIGHEST

time: 21 us -> 20.8 us (level)
  waiting for transfers between devices: 7.11 us -> 6.6 us
  Pallas kernels: 6.14 us -> 6.52 us
    pallas_call x1, Pallas kernels: 0.58 us -> 1.32 us  [fast_body(): pl.pallas_call(functools.partial(side_kernel, lat_count, circle), out_sha...]
    ppermute x8, waiting for transfers between devices: 7.11 us -> 6.6 us  [swap(): lax.ppermute(x, ('lat', 'lon'), [(a * lon_count + i, b * lon_count + j) f...]
    pallas_call x6, Pallas kernels: 2.08 us -> 1.72 us  [call(): pl.pallas_call(functools.partial(kernel, lat_count), out_shape=[VMEM(s, f...]
  transfers between devices with their start and end apart: 8 -> 8, of which waited for: 6 -> 6; matrix products, arithmetic and copies ran while one was open for 0% -> 0% of each run, Pallas kernels for 18% -> 19%
where the time goes in v6:
time: 20.8 us; the launch traced here: 20.7 us
  starting transfers between devices  7.33 us (35%)
  waiting for transfers between devices  6.6 us (32%)
  Pallas kernels  6.52 us (31%)
    ppermute x8, starting transfers between devices, swap(): lax.ppermute(x, ('lat', 'lon'), [(a * lon_count + i, b * lon_count + j) f...  7.33 us
    ppermute x8, waiting for transfers between devices, swap(): lax.ppermute(x, ('lat', 'lon'), [(a * lon_count + i, b * lon_count + j) f...  6.6 us
    pallas_call x6, Pallas kernels, call(): pl.pallas_call(functools.partial(kernel, lat_count), out_shape=[VMEM(s, f...  1.72 us
    pallas_call x1, Pallas kernels, fast_body(): pl.pallas_call(functools.partial(finish_kernel, lat_count, circle), out_s...  1.35 us
    pallas_call x1, Pallas kernels, fast_body(): pl.pallas_call(functools.partial(side_kernel, lat_count, circle), out_sha...  1.32 us
    pallas_call x1, Pallas kernels, fast_body(): pl.pallas_call(functools.partial(edge_kernel, lat_count), out_shape=VMEM(...  1.15 us
    pallas_call x1, Pallas kernels, fast_body(): pl.pallas_call(functools.partial(cap_kernel, lat_count, circle), out_shap...  0.98 us
  transfers between devices with their start and end apart: 8, of which 6 were waited for; matrix products, arithmetic and copies ran while one was open for 0% of the time, Pallas kernels for 19%

profile of v6, /device:TPU:0, one launch (start us, length us, event | category | flops | bytes accessed | tf_op | source)
XLA Modules:
  0.0 20.7 jit_solution(5037091943769324697)
XLA Ops:
  0.0 0.0 copy-start.1
  0.0 0.0 copy-start.6
  0.0 0.0 copy-start.4
  0.0 0.0 copy-start.2
  0.0 0.0 copy-start.5
  0.0 1.1 %shard_map.82.after = f32[5,16,720]{2,1,0:T(8,128)S(1)} custom-call(f32[4,5,16,720]{3,2,1,0:T(8,128)} %adj.3, f32[4,16,720]{2,1,0:T(8,128)} %north.3), custom_call_target="tpu_custom_call" | custom-call | flops 137438953472 | tf_op jit(solution)/shard_map/pallas_call | solution.py:422
  1.2 0.0 copy-start.3
  1.2 0.0 copy-start.7
  1.2 3.0 %collective-permute-start.2 = (f32[5,16,720]{2,1,0:T(8,128)S(1)}, f32[5,16,720]{2,1,0:T(8,128)S(1)}, u32[]{:S(2)}, u32[]{:S(2)}) collective-permute-start(f32[5,16,720]{2,1,0:T(8,128)S(1)} %shard_map.82.after), channel_id=1, source_target_pairs={{0,4},{1,5},{2,6},{3,7},{4,0},{5,1},{6,2},{7,3},{8,12},{9,13},{10,... | collective-permute-start | bytes 691208 | tf_op jit(solution)/shard_map/ppermute | solution.py:415
  4.2 0.0 copy-done.1
  4.2 0.0 copy-done.6
  4.2 0.0 copy-done.4
  4.2 0.0 copy-done.2
  4.3 0.0 copy-done.5
  4.3 1.1 %shard_map.83 = (f32[4,5,16,720]{3,2,1,0:T(8,128)S(1)}, f32[5,16,720]{2,1,0:T(8,128)S(1)}, f32[80,768]{1,0:T(8,128)S(1)}, f32[80,768]{1,0:T(8,128)S(1)}) custom-call(f32[5,16,720]{2,1,0:T(8,128)S(1)} %shard_map.82.after, f32[4,5,16,720]{3,2,1,0:T(8,128)S(1)} %copy-done.2, f32[4,16,720]{2,1,0:T(8,128)S(1)} %copy-done.5, f32[4,16,720]{2,1,0:T(8,128)S(1)} %copy-done.4, ...), custom_call_target="tpu_custom_call" | custom-call | bytes 1000 | tf_op jit(solution)/shard_map/pallas_call | solution.py:402
  5.4 0.1 collective-permute-start
  5.4 0.0 copy-done.3
  5.5 0.0 copy-done.7
  5.5 1.3 %shard_map.84 = (f32[3,2,384]{2,1,0:T(2,128)S(1)}, f32[80,768]{1,0:T(8,128)S(1)}) custom-call(s32[2,4]{1,0:T(2,128)S(1)} %copy-done.7, f32[80,768]{1,0:T(8,128)S(1)} %get-tuple-element.13.after.mine, f32[4,5,16,720]{3,2,1,0:T(8,128)S(1)} %copy-done.2, f32[4,16,720]{2,1,0:T(8,128)S(1)} %copy-done.5, f32[4,16,720]{2,1,0:T(8,128)S(1)} %copy-done.4, ...), custom_call_target="tpu_custom_call" | custom-call | flops 137438953472 | tf_op jit(solution)/shard_map/pallas_call | solution.py:455
  6.8 0.2 collective-permute-done.got.from_core
  7.0 1.6 %collective-permute-start.1 = (f32[80,768]{1,0:T(8,128)S(1)}, f32[80,768]{1,0:T(8,128)S(1)}, u32[]{:S(2)}, u32[]{:S(2)}) collective-permute-start(f32[80,768]{1,0:T(8,128)S(1)} %shard_map.85.after.mine), channel_id=1, source_target_pairs={{0,2},{1,3},{2,0},{3,1},{4,6},{5,7},{6,4},{7,5},{8,10},{9,11},{10,... | collective-permute-start | bytes 737288 | tf_op jit(solution)/shard_map/ppermute | solution.py:415
  8.5 0.7 %collective-permute-start.6 = (f32[5,16,720]{2,1,0:T(8,128)S(1)}, f32[5,16,720]{2,1,0:T(8,128)S(1)}, u32[]{:S(2)}, u32[]{:S(2)}) collective-permute-start(f32[5,16,720]{2,1,0:T(8,128)S(1)} %get-tuple-element.19), channel_id=1, source_target_pairs={{4,8},{5,9},{6,10},{7,11},{8,4},{9,5},{10,6},{11,7},{12,16},{13,17... | collective-permute-start | bytes 691208 | tf_op jit(solution)/shard_map/ppermute | solution.py:415
  9.2 1.0 %collective-permute-done.2.recv.recv_a = f32[5,16,720]{2,1,0:T(8,128)S(1)} collective-permute-done((f32[5,16,720]{2,1,0:T(8,128)S(1)}, f32[5,16,720]{2,1,0:T(8,128)S(1)}, u32[]{:S(2)}, u32[]{:S(2)}) %collective-permute-start.2) | collective-permute-done | bytes 230432 | tf_op jit(solution)/shard_map/ppermute | solution.py:415
  10.2 0.5 %shard_map.86 = (f32[40,768]{1,0:T(8,128)S(1)}, f32[40,768]{1,0:T(8,128)S(1)}) custom-call(f32[80,768]{1,0:T(8,128)S(1)} %get-tuple-element.16.local, f32[5,16,720]{2,1,0:T(8,128)S(1)} %collective-permute-done.2.recv.recv_a, f32[80,768]{1,0:T(8,128)S(1)} %shard_map.85.after.mine, bf16[2,768,768]{2,1,0:T(8,128)(2,1)S(1)} %copy-done.1, f32[4,2,384]{2,1,0:T(2,128)S(1)} %copy-done.6), custom_call_target="tpu_custom_call" | custom-call | bytes 1000 | tf_op jit(solution)/shard_map/pallas_call | solution.py:402
  10.7 0.1 collective-permute-start.3
  10.8 1.3 %collective-permute-done.3.got = f32[40,768]{1,0:T(8,128)S(1)} collective-permute-done((f32[40,768]{1,0:T(8,128)S(1)}, f32[40,768]{1,0:T(8,128)S(1)}, u32[]{:S(2)}, u32[]{:S(2)}) %collective-permute-start.3) | collective-permute-done | bytes 122912 | tf_op jit(solution)/shard_map/ppermute | solution.py:415
  12.2 1.8 %collective-permute-start.5 = (f32[40,768]{1,0:T(8,128)S(1)}, f32[40,768]{1,0:T(8,128)S(1)}, u32[]{:S(2)}, u32[]{:S(2)}) collective-permute-start(f32[40,768]{1,0:T(8,128)S(1)} %shard_map.87.after.x.mine), channel_id=1, source_target_pairs={{0,2},{1,3},{2,0},{3,1},{4,6},{5,7},{6,4},{7,5},{8,10},{9,11},{10,... | collective-permute-start | bytes 368648 | tf_op jit(solution)/shard_map/ppermute | solution.py:415
  13.9 1.6 %collective-permute-done.1.across.rest_0_.from_x = f32[80,768]{1,0:T(8,128)S(1)} collective-permute-done((f32[80,768]{1,0:T(8,128)S(1)}, f32[80,768]{1,0:T(8,128)S(1)}, u32[]{:S(2)}, u32[]{:S(2)}) %collective-permute-start.1) | collective-permute-done | bytes 245792 | tf_op jit(solution)/shard_map/ppermute | solution.py:415
  15.5 0.0 copy-start
  15.5 0.1 collective-permute-start.4
  15.6 0.0 collective-permute-done.6.rest_1_.recv_b
  15.6 2.3 %collective-permute-done.5.across = f32[40,768]{1,0:T(8,128)S(1)} collective-permute-done((f32[40,768]{1,0:T(8,128)S(1)}, f32[40,768]{1,0:T(8,128)S(1)}, u32[]{:S(2)}, u32[]{:S(2)}) %collective-permute-start.5) | collective-permute-done | bytes 122912 | tf_op jit(solution)/shard_map/ppermute | solution.py:415
  17.9 0.1 collective-permute-start.7
  18.0 0.0 collective-permute-done.4.other
  18.0 0.0 copy-done
  18.0 1.0 %shard_map.91.caps = f32[4,5,16,720]{3,2,1,0:T(8,128)S(1)} custom-call(f32[3,2,384]{2,1,0:T(2,128)S(1)} %get-tuple-element.14.after.weights, f32[80,768]{1,0:T(8,128)S(1)} %shard_map.88.mine, f32[80,768]{1,0:T(8,128)S(1)} %collective-permute-done.4.other, f32[40,768]{1,0:T(8,128)S(1)} %shard_map.90.third, bf16[2,768,768]{2,1,0:T(8,128)(2,1)S(1)} %copy-done, ...), custom_call_target="tpu_custom_call" | custom-call | tf_op jit(solution)/shard_map/pallas_call | solution.py:475
  19.0 0.3 %collective-permute-done.7.third = f32[40,768]{1,0:T(8,128)S(1)} collective-permute-done((f32[40,768]{1,0:T(8,128)S(1)}, f32[40,768]{1,0:T(8,128)S(1)}, u32[]{:S(2)}, u32[]{:S(2)}) %collective-permute-start.7) | collective-permute-done | bytes 122912 | tf_op jit(solution)/shard_map/ppermute | solution.py:415
  19.3 1.4 %shard_map.92 = f32[4,5,16,720]{3,2,1,0:T(8,128)} custom-call(f32[3,2,384]{2,1,0:T(2,128)S(1)} %get-tuple-element.14.after.weights, f32[4,5,16,720]{3,2,1,0:T(8,128)S(1)} %shard_map.91.caps, f32[4,5,16,720]{3,2,1,0:T(8,128)S(1)} %get-tuple-element.20.base, f32[5,16,720]{2,1,0:T(8,128)S(1)} %collective-permute-done.2.recv.recv_a, ...), custom_call_target="tpu_custom_call" | custom-call | tf_op jit(solution)/shard_map/pallas_call | solution.py:482
  (5 shorter events, 0.1 us)
Async XLA Ops:
  0.0 4.2 %copy-start.1 = (bf16[2,768,768]{2,1,0:T(8,128)(2,1)S(1)}, bf16[2,768,768]{2,1,0:T(8,128)(2,1)}, u32[]{:S(2)}) copy-start(bf16[2,768,768]{2,1,0:T(8,128)(2,1)} %constant.8.clone.fwd) | copy-start | bytes 7077892
  0.0 4.2 %copy-start.6 = (f32[4,2,384]{2,1,0:T(2,128)S(1)}, f32[4,2,384]{2,1,0:T(2,128)}, u32[]{:S(2)}) copy-start(f32[4,2,384]{2,1,0:T(2,128)} %constant.9.clone.turn) | copy-start | bytes 36868
  0.0 4.2 %copy-start.4 = (f32[4,16,720]{2,1,0:T(8,128)S(1)}, f32[4,16,720]{2,1,0:T(8,128)}, u32[]{:S(2)}) copy-start(f32[4,16,720]{2,1,0:T(8,128)} %north.3) | copy-start | bytes 552964
  0.0 4.2 %copy-start.2 = (f32[4,5,16,720]{3,2,1,0:T(8,128)S(1)}, f32[4,5,16,720]{3,2,1,0:T(8,128)}, u32[]{:S(2)}) copy-start(f32[4,5,16,720]{3,2,1,0:T(8,128)} %adj.3) | copy-start | bytes 2764804
  0.0 4.2 %copy-start.5 = (f32[4,16,720]{2,1,0:T(8,128)S(1)}, f32[4,16,720]{2,1,0:T(8,128)}, u32[]{:S(2)}) copy-start(f32[4,16,720]{2,1,0:T(8,128)} %east.3) | copy-start | bytes 552964
  1.2 4.3 %copy-start.3 = (f32[4,4,768]{2,1,0:T(4,128)S(1)}, f32[4,4,768]{2,1,0:T(4,128)}, u32[]{:S(2)}) copy-start(f32[4,4,768]{2,1,0:T(4,128)} %constant.10.clone.pole) | copy-start | bytes 147460
  1.2 4.3 %copy-start.7 = (s32[2,4]{1,0:T(2,128)S(1)}, s32[2,4]{1,0:T(2,128)}, u32[]{:S(2)}) copy-start(s32[2,4]{1,0:T(2,128)} %cutoff.1) | copy-start | bytes 100
  1.2 9.0 %collective-permute-start.2 = (f32[5,16,720]{2,1,0:T(8,128)S(1)}, f32[5,16,720]{2,1,0:T(8,128)S(1)}, u32[]{:S(2)}, u32[]{:S(2)}) collective-permute-start(f32[5,16,720]{2,1,0:T(8,128)S(1)} %shard_map.82.after), channel_id=1, source_target_pairs={{0,4},{1,5},{2,6},{3,7},{4,0},{5,1},{6,2},{7,3},{8,12},{9,13},{10,... | collective-permute-start | bytes 691208 | tf_op jit(solution)/shard_map/ppermute | solution.py:415
  5.4 1.6 %collective-permute-start = (f32[80,768]{1,0:T(8,128)S(1)}, f32[80,768]{1,0:T(8,128)S(1)}, u32[]{:S(2)}, u32[]{:S(2)}) collective-permute-start(f32[80,768]{1,0:T(8,128)S(1)} %get-tuple-element.15), channel_id=1, source_target_pairs={{0,1},{1,0},{2,3},{3,2},{4,5},{5,4},{6,7},{7,6},{8,9},{9,8},{10,11... | collective-permute-start | bytes 737288 | tf_op jit(solution)/shard_map/ppermute | solution.py:415
  7.0 8.5 %collective-permute-start.1 = (f32[80,768]{1,0:T(8,128)S(1)}, f32[80,768]{1,0:T(8,128)S(1)}, u32[]{:S(2)}, u32[]{:S(2)}) collective-permute-start(f32[80,768]{1,0:T(8,128)S(1)} %shard_map.85.after.mine), channel_id=1, source_target_pairs={{0,2},{1,3},{2,0},{3,1},{4,6},{5,7},{6,4},{7,5},{8,10},{9,11},{10,... | collective-permute-start | bytes 737288 | tf_op jit(solution)/shard_map/ppermute | solution.py:415
  8.5 7.1 %collective-permute-start.6 = (f32[5,16,720]{2,1,0:T(8,128)S(1)}, f32[5,16,720]{2,1,0:T(8,128)S(1)}, u32[]{:S(2)}, u32[]{:S(2)}) collective-permute-start(f32[5,16,720]{2,1,0:T(8,128)S(1)} %get-tuple-element.19), channel_id=1, source_target_pairs={{4,8},{5,9},{6,10},{7,11},{8,4},{9,5},{10,6},{11,7},{12,16},{13,17... | collective-permute-start | bytes 691208 | tf_op jit(solution)/shard_map/ppermute | solution.py:415
  10.7 1.4 %collective-permute-start.3 = (f32[40,768]{1,0:T(8,128)S(1)}, f32[40,768]{1,0:T(8,128)S(1)}, u32[]{:S(2)}, u32[]{:S(2)}) collective-permute-start(f32[40,768]{1,0:T(8,128)S(1)} %get-tuple-element.18.after), channel_id=1, source_target_pairs={{0,1},{1,0},{2,3},{3,2},{4,5},{5,4},{6,7},{7,6},{8,9},{9,8},{10,11... | collective-permute-start | bytes 368648 | tf_op jit(solution)/shard_map/ppermute | solution.py:415
  12.2 5.7 %collective-permute-start.5 = (f32[40,768]{1,0:T(8,128)S(1)}, f32[40,768]{1,0:T(8,128)S(1)}, u32[]{:S(2)}, u32[]{:S(2)}) collective-permute-start(f32[40,768]{1,0:T(8,128)S(1)} %shard_map.87.after.x.mine), channel_id=1, source_target_pairs={{0,2},{1,3},{2,0},{3,1},{4,6},{5,7},{6,4},{7,5},{8,10},{9,11},{10,... | collective-permute-start | bytes 368648 | tf_op jit(solution)/shard_map/ppermute | solution.py:415
  15.5 2.5 %copy-start = (bf16[2,768,768]{2,1,0:T(8,128)(2,1)S(1)}, bf16[2,768,768]{2,1,0:T(8,128)(2,1)}, u32[]{:S(2)}) copy-start(bf16[2,768,768]{2,1,0:T(8,128)(2,1)} %constant.11.clone.bwd) | copy-start | bytes 7077892
  15.5 2.5 %collective-permute-start.4 = (f32[80,768]{1,0:T(8,128)S(1)}, f32[80,768]{1,0:T(8,128)S(1)}, u32[]{:S(2)}, u32[]{:S(2)}) collective-permute-start(f32[80,768]{1,0:T(8,128)S(1)} %shard_map.88.mine), channel_id=1, source_target_pairs={{0,1},{1,0},{2,3},{3,2},{4,5},{5,4},{6,7},{7,6},{8,9},{9,8},{10,11... | collective-permute-start | bytes 737288 | tf_op jit(solution)/shard_map/ppermute | solution.py:415
  17.9 1.4 %collective-permute-start.7 = (f32[40,768]{1,0:T(8,128)S(1)}, f32[40,768]{1,0:T(8,128)S(1)}, u32[]{:S(2)}, u32[]{:S(2)}) collective-permute-start(f32[40,768]{1,0:T(8,128)S(1)} %shard_map.90.third), channel_id=1, source_target_pairs={{0,1},{1,0},{2,3},{3,2},{4,5},{5,4},{6,7},{7,6},{8,9},{9,8},{10,11... | collective-permute-start | bytes 368648 | tf_op jit(solution)/shard_map/ppermute | solution.py:415

commit v7 on v6

--- a/solution.py
+++ b/solution.py
@@ -57,12 +57,14 @@
     return split16(forward), split16(backward), turn, pole
 
 
-def dot3(block, table_ref):
+def dot3(block, table_ref, first=0, count=None):
     rows = block.shape[0]
+    count = table_ref.shape[2] if count is None else count
+    high_table, low_table = (table_ref[k, :, first : first + count] for k in (0, 1))
     high = block.astype(jnp.bfloat16)
     low = (block - high.astype(jnp.float32)).astype(jnp.bfloat16)
-    stack = jnp.dot(jnp.concatenate([high, low]), table_ref[0], preferred_element_type=jnp.float32)
-    return stack[:rows] + stack[rows:] + jnp.dot(high, table_ref[1], preferred_element_type=jnp.float32)
+    stack = jnp.dot(jnp.concatenate([high, low]), high_table, preferred_element_type=jnp.float32)
+    return stack[:rows] + stack[rows:] + jnp.dot(high, low_table, preferred_element_type=jnp.float32)
 
 
 def latitude_role(lat_count):
@@ -335,10 +337,18 @@
             pole_ref[t] = pole_row(third, t, half_lev, bwd.shape[1] // 2, pole, lon, circle)[:, :cols]
         copies.append(pltpu.make_async_copy(pole_ref, out.at[top, :, there, :], sems.at[rows + 1]))
         copies[-1].start()
-        y = dot3(weighted(third[...], weights[2]), bwd)
-        last_ref[...] = y[:, :cols].reshape(tracers, half_lev, cols)
-        copies.append(pltpu.make_async_copy(last_ref, out.at[row, :, there, :], sems.at[rows]))
-        copies[-1].start()
+        block = weighted(third[...], weights[2])
+        middle = (cols // 2 + LANE - 1) // LANE * LANE
+        for k, (first, end) in enumerate(((0, middle), (middle, cols))):
+            y = dot3(block, bwd, first, middle)
+            last_ref[:, :, first:end] = y[:, : end - first].reshape(tracers, half_lev, end - first)
+            part = pl.ds(first, end - first)
+            copies.append(
+                pltpu.make_async_copy(
+                    last_ref.at[:, :, part], out.at[row, :, there, part], sems.at[rows if k == 0 else rows + 2]
+                )
+            )
+            copies[-1].start()
         for copy in copies:
             copy.wait()
 
@@ -484,7 +494,7 @@
         out_shape=jax.ShapeDtypeStruct(adj.shape, f32),
         in_specs=[vmem] * 10,
         out_specs=anywhere,
-        scratch_shapes=[VMEM(adj.shape, f32), VMEM(half_row, f32), VMEM(half_row, f32), dma((rows + 2,))],
+        scratch_shapes=[VMEM(adj.shape, f32), VMEM(half_row, f32), VMEM(half_row, f32), dma((rows + 3,))],
         compiler_params=params,
     )(*(put(x, VMEM) for x in (weights, caps, base, recv_a, recv_b, got, across, other3, bwd, pole)))
 

time: 20.8 us -> 20.8 us (level)
  no operation moved by 1% of the time
where the time goes in v7:
time: 20.8 us; the launch traced here: 20.7 us
  starting transfers between devices  7.33 us (35%)
  waiting for transfers between devices  6.6 us (32%)
  Pallas kernels  6.5 us (31%)
    ppermute x8, starting transfers between devices, swap(): lax.ppermute(x, ('lat', 'lon'), [(a * lon_count + i, b * lon_count + j) f...  7.33 us
    ppermute x8, waiting for transfers between devices, swap(): lax.ppermute(x, ('lat', 'lon'), [(a * lon_count + i, b * lon_count + j) f...  6.6 us
    pallas_call x6, Pallas kernels, call(): pl.pallas_call(functools.partial(kernel, lat_count), out_shape=[VMEM(s, f...  1.72 us
    pallas_call x1, Pallas kernels, fast_body(): pl.pallas_call(functools.partial(finish_kernel, lat_count, circle), out_s...  1.34 us
    pallas_call x1, Pallas kernels, fast_body(): pl.pallas_call(functools.partial(side_kernel, lat_count, circle), out_sha...  1.32 us
    pallas_call x1, Pallas kernels, fast_body(): pl.pallas_call(functools.partial(edge_kernel, lat_count), out_shape=VMEM(...  1.15 us
    pallas_call x1, Pallas kernels, fast_body(): pl.pallas_call(functools.partial(cap_kernel, lat_count, circle), out_shap...  0.98 us
  transfers between devices with their start and end apart: 8, of which 6 were waited for; matrix products, arithmetic and copies ran while one was open for 0% of the time, Pallas kernels for 19%

profile of v7, /device:TPU:0, one launch (start us, length us, event | category | flops | bytes accessed | tf_op | source)
XLA Modules:
  0.0 20.7 jit_solution(2450601275622637273)
XLA Ops:
  0.0 0.0 copy-start.1
  0.0 0.0 copy-start.6
  0.0 0.0 copy-start.4
  0.0 0.0 copy-start.2
  0.0 0.0 copy-start.5
  0.0 1.1 %shard_map.82.after = f32[5,16,720]{2,1,0:T(8,128)S(1)} custom-call(f32[4,5,16,720]{3,2,1,0:T(8,128)} %adj.3, f32[4,16,720]{2,1,0:T(8,128)} %north.3), custom_call_target="tpu_custom_call" | custom-call | flops 137438953472 | tf_op jit(solution)/shard_map/pallas_call | solution.py:432
  1.2 0.0 copy-start.3
  1.2 0.0 copy-start.7
  1.2 3.0 %collective-permute-start.2 = (f32[5,16,720]{2,1,0:T(8,128)S(1)}, f32[5,16,720]{2,1,0:T(8,128)S(1)}, u32[]{:S(2)}, u32[]{:S(2)}) collective-permute-start(f32[5,16,720]{2,1,0:T(8,128)S(1)} %shard_map.82.after), channel_id=1, source_target_pairs={{0,4},{1,5},{2,6},{3,7},{4,0},{5,1},{6,2},{7,3},{8,12},{9,13},{10,... | collective-permute-start | bytes 691208 | tf_op jit(solution)/shard_map/ppermute | solution.py:425
  4.2 0.0 copy-done.1
  4.2 0.0 copy-done.6
  4.2 0.0 copy-done.4
  4.2 0.0 copy-done.2
  4.3 0.0 copy-done.5
  4.3 1.1 %shard_map.83 = (f32[4,5,16,720]{3,2,1,0:T(8,128)S(1)}, f32[5,16,720]{2,1,0:T(8,128)S(1)}, f32[80,768]{1,0:T(8,128)S(1)}, f32[80,768]{1,0:T(8,128)S(1)}) custom-call(f32[5,16,720]{2,1,0:T(8,128)S(1)} %shard_map.82.after, f32[4,5,16,720]{3,2,1,0:T(8,128)S(1)} %copy-done.2, f32[4,16,720]{2,1,0:T(8,128)S(1)} %copy-done.5, f32[4,16,720]{2,1,0:T(8,128)S(1)} %copy-done.4, ...), custom_call_target="tpu_custom_call" | custom-call | bytes 1000 | tf_op jit(solution)/shard_map/pallas_call | solution.py:412
  5.4 0.1 collective-permute-start
  5.4 0.0 copy-done.3
  5.5 0.0 copy-done.7
  5.5 1.3 %shard_map.84 = (f32[3,2,384]{2,1,0:T(2,128)S(1)}, f32[80,768]{1,0:T(8,128)S(1)}) custom-call(s32[2,4]{1,0:T(2,128)S(1)} %copy-done.7, f32[80,768]{1,0:T(8,128)S(1)} %get-tuple-element.13.after.mine, f32[4,5,16,720]{3,2,1,0:T(8,128)S(1)} %copy-done.2, f32[4,16,720]{2,1,0:T(8,128)S(1)} %copy-done.5, f32[4,16,720]{2,1,0:T(8,128)S(1)} %copy-done.4, ...), custom_call_target="tpu_custom_call" | custom-call | flops 137438953472 | tf_op jit(solution)/shard_map/pallas_call | solution.py:465
  6.8 0.2 collective-permute-done.got.from_core
  7.0 1.6 %collective-permute-start.1 = (f32[80,768]{1,0:T(8,128)S(1)}, f32[80,768]{1,0:T(8,128)S(1)}, u32[]{:S(2)}, u32[]{:S(2)}) collective-permute-start(f32[80,768]{1,0:T(8,128)S(1)} %shard_map.85.after.mine), channel_id=1, source_target_pairs={{0,2},{1,3},{2,0},{3,1},{4,6},{5,7},{6,4},{7,5},{8,10},{9,11},{10,... | collective-permute-start | bytes 737288 | tf_op jit(solution)/shard_map/ppermute | solution.py:425
  8.5 0.7 %collective-permute-start.6 = (f32[5,16,720]{2,1,0:T(8,128)S(1)}, f32[5,16,720]{2,1,0:T(8,128)S(1)}, u32[]{:S(2)}, u32[]{:S(2)}) collective-permute-start(f32[5,16,720]{2,1,0:T(8,128)S(1)} %get-tuple-element.19), channel_id=1, source_target_pairs={{4,8},{5,9},{6,10},{7,11},{8,4},{9,5},{10,6},{11,7},{12,16},{13,17... | collective-permute-start | bytes 691208 | tf_op jit(solution)/shard_map/ppermute | solution.py:425
  9.2 1.0 %collective-permute-done.2.recv.recv_a = f32[5,16,720]{2,1,0:T(8,128)S(1)} collective-permute-done((f32[5,16,720]{2,1,0:T(8,128)S(1)}, f32[5,16,720]{2,1,0:T(8,128)S(1)}, u32[]{:S(2)}, u32[]{:S(2)}) %collective-permute-start.2) | collective-permute-done | bytes 230432 | tf_op jit(solution)/shard_map/ppermute | solution.py:425
  10.2 0.5 %shard_map.86 = (f32[40,768]{1,0:T(8,128)S(1)}, f32[40,768]{1,0:T(8,128)S(1)}) custom-call(f32[80,768]{1,0:T(8,128)S(1)} %get-tuple-element.16.local, f32[5,16,720]{2,1,0:T(8,128)S(1)} %collective-permute-done.2.recv.recv_a, f32[80,768]{1,0:T(8,128)S(1)} %shard_map.85.after.mine, bf16[2,768,768]{2,1,0:T(8,128)(2,1)S(1)} %copy-done.1, f32[4,2,384]{2,1,0:T(2,128)S(1)} %copy-done.6), custom_call_target="tpu_custom_call" | custom-call | bytes 1000 | tf_op jit(solution)/shard_map/pallas_call | solution.py:412
  10.7 0.1 collective-permute-start.3
  10.8 1.3 %collective-permute-done.3.got = f32[40,768]{1,0:T(8,128)S(1)} collective-permute-done((f32[40,768]{1,0:T(8,128)S(1)}, f32[40,768]{1,0:T(8,128)S(1)}, u32[]{:S(2)}, u32[]{:S(2)}) %collective-permute-start.3) | collective-permute-done | bytes 122912 | tf_op jit(solution)/shard_map/ppermute | solution.py:425
  12.2 1.8 %collective-permute-start.5 = (f32[40,768]{1,0:T(8,128)S(1)}, f32[40,768]{1,0:T(8,128)S(1)}, u32[]{:S(2)}, u32[]{:S(2)}) collective-permute-start(f32[40,768]{1,0:T(8,128)S(1)} %shard_map.87.after.x.mine), channel_id=1, source_target_pairs={{0,2},{1,3},{2,0},{3,1},{4,6},{5,7},{6,4},{7,5},{8,10},{9,11},{10,... | collective-permute-start | bytes 368648 | tf_op jit(solution)/shard_map/ppermute | solution.py:425
  13.9 1.6 %collective-permute-done.1.across.rest_0_.from_x = f32[80,768]{1,0:T(8,128)S(1)} collective-permute-done((f32[80,768]{1,0:T(8,128)S(1)}, f32[80,768]{1,0:T(8,128)S(1)}, u32[]{:S(2)}, u32[]{:S(2)}) %collective-permute-start.1) | collective-permute-done | bytes 245792 | tf_op jit(solution)/shard_map/ppermute | solution.py:425
  15.5 0.0 copy-start
  15.5 0.1 collective-permute-start.4
  15.6 0.0 collective-permute-done.6.rest_1_.recv_b
  15.6 2.3 %collective-permute-done.5.across = f32[40,768]{1,0:T(8,128)S(1)} collective-permute-done((f32[40,768]{1,0:T(8,128)S(1)}, f32[40,768]{1,0:T(8,128)S(1)}, u32[]{:S(2)}, u32[]{:S(2)}) %collective-permute-start.5) | collective-permute-done | bytes 122912 | tf_op jit(solution)/shard_map/ppermute | solution.py:425
  17.9 0.1 collective-permute-start.7
  18.0 0.0 collective-permute-done.4.other
  18.0 0.0 copy-done
  18.0 1.0 %shard_map.91.caps = f32[4,5,16,720]{3,2,1,0:T(8,128)S(1)} custom-call(f32[3,2,384]{2,1,0:T(2,128)S(1)} %get-tuple-element.14.after.weights, f32[80,768]{1,0:T(8,128)S(1)} %shard_map.88.mine, f32[80,768]{1,0:T(8,128)S(1)} %collective-permute-done.4.other, f32[40,768]{1,0:T(8,128)S(1)} %shard_map.90.third, bf16[2,768,768]{2,1,0:T(8,128)(2,1)S(1)} %copy-done, ...), custom_call_target="tpu_custom_call" | custom-call | tf_op jit(solution)/shard_map/pallas_call | solution.py:485
  19.0 0.3 %collective-permute-done.7.third = f32[40,768]{1,0:T(8,128)S(1)} collective-permute-done((f32[40,768]{1,0:T(8,128)S(1)}, f32[40,768]{1,0:T(8,128)S(1)}, u32[]{:S(2)}, u32[]{:S(2)}) %collective-permute-start.7) | collective-permute-done | bytes 122912 | tf_op jit(solution)/shard_map/ppermute | solution.py:425
  19.3 1.3 %shard_map.92 = f32[4,5,16,720]{3,2,1,0:T(8,128)} custom-call(f32[3,2,384]{2,1,0:T(2,128)S(1)} %get-tuple-element.14.after.weights, f32[4,5,16,720]{3,2,1,0:T(8,128)S(1)} %shard_map.91.caps, f32[4,5,16,720]{3,2,1,0:T(8,128)S(1)} %get-tuple-element.20.base, f32[5,16,720]{2,1,0:T(8,128)S(1)} %collective-permute-done.2.recv.recv_a, ...), custom_call_target="tpu_custom_call" | custom-call | tf_op jit(solution)/shard_map/pallas_call | solution.py:492
  (5 shorter events, 0.1 us)
Async XLA Ops:
  0.0 4.2 %copy-start.1 = (bf16[2,768,768]{2,1,0:T(8,128)(2,1)S(1)}, bf16[2,768,768]{2,1,0:T(8,128)(2,1)}, u32[]{:S(2)}) copy-start(bf16[2,768,768]{2,1,0:T(8,128)(2,1)} %constant.8.clone.fwd) | copy-start | bytes 7077892
  0.0 4.2 %copy-start.6 = (f32[4,2,384]{2,1,0:T(2,128)S(1)}, f32[4,2,384]{2,1,0:T(2,128)}, u32[]{:S(2)}) copy-start(f32[4,2,384]{2,1,0:T(2,128)} %constant.9.clone.turn) | copy-start | bytes 36868
  0.0 4.2 %copy-start.4 = (f32[4,16,720]{2,1,0:T(8,128)S(1)}, f32[4,16,720]{2,1,0:T(8,128)}, u32[]{:S(2)}) copy-start(f32[4,16,720]{2,1,0:T(8,128)} %north.3) | copy-start | bytes 552964
  0.0 4.2 %copy-start.2 = (f32[4,5,16,720]{3,2,1,0:T(8,128)S(1)}, f32[4,5,16,720]{3,2,1,0:T(8,128)}, u32[]{:S(2)}) copy-start(f32[4,5,16,720]{3,2,1,0:T(8,128)} %adj.3) | copy-start | bytes 2764804
  0.0 4.2 %copy-start.5 = (f32[4,16,720]{2,1,0:T(8,128)S(1)}, f32[4,16,720]{2,1,0:T(8,128)}, u32[]{:S(2)}) copy-start(f32[4,16,720]{2,1,0:T(8,128)} %east.3) | copy-start | bytes 552964
  1.2 4.3 %copy-start.3 = (f32[4,4,768]{2,1,0:T(4,128)S(1)}, f32[4,4,768]{2,1,0:T(4,128)}, u32[]{:S(2)}) copy-start(f32[4,4,768]{2,1,0:T(4,128)} %constant.10.clone.pole) | copy-start | bytes 147460
  1.2 4.3 %copy-start.7 = (s32[2,4]{1,0:T(2,128)S(1)}, s32[2,4]{1,0:T(2,128)}, u32[]{:S(2)}) copy-start(s32[2,4]{1,0:T(2,128)} %cutoff.1) | copy-start | bytes 100
  1.2 9.0 %collective-permute-start.2 = (f32[5,16,720]{2,1,0:T(8,128)S(1)}, f32[5,16,720]{2,1,0:T(8,128)S(1)}, u32[]{:S(2)}, u32[]{:S(2)}) collective-permute-start(f32[5,16,720]{2,1,0:T(8,128)S(1)} %shard_map.82.after), channel_id=1, source_target_pairs={{0,4},{1,5},{2,6},{3,7},{4,0},{5,1},{6,2},{7,3},{8,12},{9,13},{10,... | collective-permute-start | bytes 691208 | tf_op jit(solution)/shard_map/ppermute | solution.py:425
  5.4 1.6 %collective-permute-start = (f32[80,768]{1,0:T(8,128)S(1)}, f32[80,768]{1,0:T(8,128)S(1)}, u32[]{:S(2)}, u32[]{:S(2)}) collective-permute-start(f32[80,768]{1,0:T(8,128)S(1)} %get-tuple-element.15), channel_id=1, source_target_pairs={{0,1},{1,0},{2,3},{3,2},{4,5},{5,4},{6,7},{7,6},{8,9},{9,8},{10,11... | collective-permute-start | bytes 737288 | tf_op jit(solution)/shard_map/ppermute | solution.py:425
  7.0 8.5 %collective-permute-start.1 = (f32[80,768]{1,0:T(8,128)S(1)}, f32[80,768]{1,0:T(8,128)S(1)}, u32[]{:S(2)}, u32[]{:S(2)}) collective-permute-start(f32[80,768]{1,0:T(8,128)S(1)} %shard_map.85.after.mine), channel_id=1, source_target_pairs={{0,2},{1,3},{2,0},{3,1},{4,6},{5,7},{6,4},{7,5},{8,10},{9,11},{10,... | collective-permute-start | bytes 737288 | tf_op jit(solution)/shard_map/ppermute | solution.py:425
  8.5 7.1 %collective-permute-start.6 = (f32[5,16,720]{2,1,0:T(8,128)S(1)}, f32[5,16,720]{2,1,0:T(8,128)S(1)}, u32[]{:S(2)}, u32[]{:S(2)}) collective-permute-start(f32[5,16,720]{2,1,0:T(8,128)S(1)} %get-tuple-element.19), channel_id=1, source_target_pairs={{4,8},{5,9},{6,10},{7,11},{8,4},{9,5},{10,6},{11,7},{12,16},{13,17... | collective-permute-start | bytes 691208 | tf_op jit(solution)/shard_map/ppermute | solution.py:425
  10.7 1.4 %collective-permute-start.3 = (f32[40,768]{1,0:T(8,128)S(1)}, f32[40,768]{1,0:T(8,128)S(1)}, u32[]{:S(2)}, u32[]{:S(2)}) collective-permute-start(f32[40,768]{1,0:T(8,128)S(1)} %get-tuple-element.18.after), channel_id=1, source_target_pairs={{0,1},{1,0},{2,3},{3,2},{4,5},{5,4},{6,7},{7,6},{8,9},{9,8},{10,11... | collective-permute-start | bytes 368648 | tf_op jit(solution)/shard_map/ppermute | solution.py:425
  12.2 5.7 %collective-permute-start.5 = (f32[40,768]{1,0:T(8,128)S(1)}, f32[40,768]{1,0:T(8,128)S(1)}, u32[]{:S(2)}, u32[]{:S(2)}) collective-permute-start(f32[40,768]{1,0:T(8,128)S(1)} %shard_map.87.after.x.mine), channel_id=1, source_target_pairs={{0,2},{1,3},{2,0},{3,1},{4,6},{5,7},{6,4},{7,5},{8,10},{9,11},{10,... | collective-permute-start | bytes 368648 | tf_op jit(solution)/shard_map/ppermute | solution.py:425
  15.5 2.5 %copy-start = (bf16[2,768,768]{2,1,0:T(8,128)(2,1)S(1)}, bf16[2,768,768]{2,1,0:T(8,128)(2,1)}, u32[]{:S(2)}) copy-start(bf16[2,768,768]{2,1,0:T(8,128)(2,1)} %constant.11.clone.bwd) | copy-start | bytes 7077892
  15.5 2.5 %collective-permute-start.4 = (f32[80,768]{1,0:T(8,128)S(1)}, f32[80,768]{1,0:T(8,128)S(1)}, u32[]{:S(2)}, u32[]{:S(2)}) collective-permute-start(f32[80,768]{1,0:T(8,128)S(1)} %shard_map.88.mine), channel_id=1, source_target_pairs={{0,1},{1,0},{2,3},{3,2},{4,5},{5,4},{6,7},{7,6},{8,9},{9,8},{10,11... | collective-permute-start | bytes 737288 | tf_op jit(solution)/shard_map/ppermute | solution.py:425
  17.9 1.4 %collective-permute-start.7 = (f32[40,768]{1,0:T(8,128)S(1)}, f32[40,768]{1,0:T(8,128)S(1)}, u32[]{:S(2)}, u32[]{:S(2)}) collective-permute-start(f32[40,768]{1,0:T(8,128)S(1)} %shard_map.90.third), channel_id=1, source_target_pairs={{0,1},{1,0},{2,3},{3,2},{4,5},{5,4},{6,7},{7,6},{8,9},{9,8},{10,11... | collective-permute-start | bytes 368648 | tf_op jit(solution)/shard_map/ppermute | solution.py:425
